TPU v7x, 32 devices: a whole 2x2x4 slice. The times are simulated.
32 devices in a mesh: pipe: 4 (over y, x), expert: 8 (over z, core).
Axes of the slice: x: 2, y: 2, z: 4, core: 2. Of those that a mesh axis runs over, the one named last changes fastest.
Arguments:
- x_fwd: bfloat16 [4096, 1536], P(('pipe', 'expert')), may hold values from -6 to 6
- gate_fwd: float32 [4096, 6], P(('pipe', 'expert')), may hold values from 0.05 to 0.4
- route_fwd: int32 [4096, 6], P(('pipe', 'expert')), may hold values from 0 to 15, all different within a row; in each aligned block of 128 rows (0 to 127, 128 to 255, ...) at most 64 rows name the same one
- x_bwd: bfloat16 [4096, 1536], P(('pipe', 'expert')), may hold values from -6 to 6
- gate_bwd: float32 [4096, 6], P(('pipe', 'expert')), may hold values from 0.05 to 0.4
- route_bwd: int32 [4096, 6], P(('pipe', 'expert')), may hold values from 0 to 15, all different within a row; in each aligned block of 128 rows (0 to 127, 128 to 255, ...) at most 64 rows name the same one
- cotangent: bfloat16 [4096, 1536], P(('pipe', 'expert')), may hold values from -6 to 6
- norm_gain: float32 [1536], replicated, may hold values from 0.5 to 1.5
- w_gate_up: bfloat16 [4, 16, 1536, 1536], P('pipe', 'expert'), as said below
- w_down: bfloat16 [4, 16, 768, 1536], P('pipe', 'expert'), as said below
Outputs:
- y_fwd: bfloat16 [4096, 1536], P(('pipe', 'expert'))
- dx_bwd: bfloat16 [4096, 1536], P(('pipe', 'expert'))
- grad_gate_up: bfloat16 [4, 8, 1536, 1536], P('pipe', 'expert')
- grad_down: bfloat16 [4, 8, 768, 1536], P('pipe', 'expert')
Inputs may be any that keep to these rules, and one draw needn't show every extreme that they name: `route_fwd`: each row names 6 different experts; in the 128 rows of one group no expert is named more than 64 times. `route_bwd`: each row names 6 different experts; in the 128 rows of one group no expert is named more than 64 times. w_gate_up[p] equals w_gate_up[3 - p]. w_down[p] equals w_down[3 - p].
All inputs are finite; a program needn't handle non-finite values.
Results may differ from a plain program's by a relative error of at most 0.0078.
Values may be sent and summed in bfloat16 or wider, within the bound.
No kernel may reach another device: no remote copies, remote signals or barrier semaphores. Data moves between devices by JAX's collectives and lax.ppermute only.
A program may use at most 192 MiB of HBM per device.

v0:
```python
import jax
import jax.numpy as jnp
from jax import lax
from jax.sharding import PartitionSpec as P

norm_eps = 1e-06


def from_partner(value, axis, bit):
    return lax.ppermute(value, axis, [(i, i ^ 1 << bit) for i in range(lax.axis_size(axis))])


def normalize(inputs):
    values = inputs.astype(jnp.float32)
    scale = lax.rsqrt(jnp.mean(values * values, axis=-1, keepdims=True) + norm_eps)
    return (values * scale, scale)


def destinations(routes, expert_count, capacity):
    flat_routes = routes.reshape(-1)
    onehot = (flat_routes[:, None] == jnp.arange(expert_count, dtype=jnp.int32)[None, :]).astype(
        jnp.int32
    )
    before = jnp.cumsum(onehot, axis=0) - onehot
    slot = jnp.sum(before * onehot, axis=1)
    return (flat_routes * capacity + slot).reshape(routes.shape)


def place_rows(values, dest, slot_total):
    flat_values = values.reshape(-1, values.shape[-1])
    return (
        jnp.zeros((slot_total, values.shape[-1]), values.dtype)
        .at[dest.reshape(-1)]
        .set(flat_values)
    )


def expert_forward(inputs, weight_gu, weight_dn):
    hidden_units = weight_dn.shape[1]
    both_parts = jnp.einsum("secd,edf->secf", inputs, weight_gu, preferred_element_type=jnp.float32)
    gate_pre = both_parts[..., :hidden_units]
    up_pre = both_parts[..., hidden_units:]
    hidden = (jax.nn.silu(gate_pre) * up_pre).astype(jnp.bfloat16)
    return jnp.einsum(
        "secf,efd->secd", hidden, weight_dn, preferred_element_type=jnp.float32
    ).astype(jnp.bfloat16)


def expert_backward(inputs, cot_rows, weight_gu, weight_dn):
    hidden_units = weight_dn.shape[1]
    both_parts = jnp.einsum("secd,edf->secf", inputs, weight_gu, preferred_element_type=jnp.float32)
    gate_pre = both_parts[..., :hidden_units]
    up_pre = both_parts[..., hidden_units:]
    squash = jax.nn.sigmoid(gate_pre)
    activated = gate_pre * squash
    hidden = (activated * up_pre).astype(jnp.bfloat16)
    back_hidden = jnp.einsum(
        "secd,efd->secf", cot_rows, weight_dn, preferred_element_type=jnp.float32
    )
    d_gate = back_hidden * up_pre * squash * (1.0 + gate_pre * (1.0 - squash))
    d_up = back_hidden * activated
    d_both = jnp.concatenate([d_gate, d_up], axis=-1).astype(jnp.bfloat16)
    d_inputs = jnp.einsum(
        "secf,edf->secd", d_both, weight_gu, preferred_element_type=jnp.float32
    ).astype(jnp.bfloat16)
    grad_dn = jnp.einsum(
        "secf,secd->efd", hidden, cot_rows, preferred_element_type=jnp.float32
    ).astype(jnp.bfloat16)
    grad_gu = jnp.einsum(
        "secd,secf->edf", inputs, d_both, preferred_element_type=jnp.float32
    ).astype(jnp.bfloat16)
    return (d_inputs, grad_gu, grad_dn)


def per_device(
    x_fwd, gate_fwd, route_fwd, x_bwd, gate_bwd, route_bwd, cotangent, norm_gain, w_gate_up, w_down
):
    group_count = lax.axis_size("expert")
    local_count = w_gate_up.shape[1]
    expert_count = local_count * group_count
    token_count = x_fwd.shape[0]
    model_width = x_fwd.shape[1]
    pick_count = route_fwd.shape[1]
    capacity = token_count * pick_count * 4 // (3 * expert_count)
    slot_total = expert_count * capacity
    buffer_shape = (group_count, local_count, capacity, model_width)
    row_shape = (token_count, pick_count, model_width)
    weight_gu = w_gate_up[0]
    weight_dn = w_down[0]
    fwd_normed = (normalize(x_fwd)[0] * norm_gain).astype(jnp.bfloat16)
    dest_fwd = destinations(route_fwd, expert_count, capacity)
    send_fwd = place_rows(
        jnp.broadcast_to(fwd_normed[:, None, :], row_shape), dest_fwd, slot_total
    ).reshape(buffer_shape)
    bwd_hat, bwd_scale = normalize(x_bwd)
    bwd_normed = (bwd_hat * norm_gain).astype(jnp.bfloat16)
    scaled_cot = (gate_bwd[:, :, None] * cotangent.astype(jnp.float32)[:, None, :]).astype(
        jnp.bfloat16
    )
    dest_bwd = destinations(route_bwd, expert_count, capacity)
    send_inputs = place_rows(
        jnp.broadcast_to(bwd_normed[:, None, :], row_shape), dest_bwd, slot_total
    ).reshape(buffer_shape)
    send_cot = place_rows(scaled_cot, dest_bwd, slot_total).reshape(buffer_shape)
    recv_fwd = lax.all_to_all(send_fwd, "expert", split_axis=0, concat_axis=0, tiled=True)
    recv_inputs, recv_cot = (
        lax.all_to_all(send_inputs, "expert", split_axis=0, concat_axis=0, tiled=True),
        lax.all_to_all(send_cot, "expert", split_axis=0, concat_axis=0, tiled=True),
    )
    out_fwd = expert_forward(recv_fwd, weight_gu, weight_dn)
    back_fwd = lax.all_to_all(out_fwd, "expert", split_axis=0, concat_axis=0, tiled=True)
    d_inputs, grad_gu, grad_dn = expert_backward(recv_inputs, recv_cot, weight_gu, weight_dn)
    back_dh = lax.all_to_all(d_inputs, "expert", split_axis=0, concat_axis=0, tiled=True)
    picked = back_fwd.reshape(slot_total, model_width)[dest_fwd]
    y_fwd = jnp.sum(picked.astype(jnp.float32) * gate_fwd[:, :, None], axis=1).astype(jnp.bfloat16)
    dh_sum = jnp.sum(back_dh.reshape(slot_total, model_width)[dest_bwd].astype(jnp.float32), axis=1)
    scaled_dh = norm_gain * dh_sum
    dx_bwd = (
        bwd_scale * (scaled_dh - bwd_hat * jnp.mean(bwd_hat * scaled_dh, axis=-1, keepdims=True))
    ).astype(jnp.bfloat16)
    section_index = lax.axis_index("pipe")
    section_count = lax.axis_size("pipe")
    upper_half = (section_index >= section_count // 2).astype(jnp.int32)
    half_local = local_count // 2
    keep_gu = lax.dynamic_slice_in_dim(grad_gu, upper_half * half_local, half_local, 0)
    give_gu = lax.dynamic_slice_in_dim(grad_gu, (1 - upper_half) * half_local, half_local, 0)
    keep_dn = lax.dynamic_slice_in_dim(grad_dn, upper_half * half_local, half_local, 0)
    give_dn = lax.dynamic_slice_in_dim(grad_dn, (1 - upper_half) * half_local, half_local, 0)
    bit_count = section_count.bit_length() - 1
    for bit_number in range(bit_count):
        give_gu = from_partner(give_gu, "pipe", bit_number)
    down_bits = list(range(bit_count))
    for bit_number in down_bits:
        give_dn = from_partner(give_dn, "pipe", bit_number)
    out_gu = (keep_gu.astype(jnp.float32) + give_gu.astype(jnp.float32)).astype(jnp.bfloat16)
    out_dn = (keep_dn.astype(jnp.float32) + give_dn.astype(jnp.float32)).astype(jnp.bfloat16)
    return (y_fwd, dx_bwd, out_gu[None], out_dn[None])


def solution(mesh):
    return jax.shard_map(
        per_device,
        mesh=mesh,
        in_specs=(
            P(("pipe", "expert"), None),
            P(("pipe", "expert"), None),
            P(("pipe", "expert"), None),
            P(("pipe", "expert"), None),
            P(("pipe", "expert"), None),
            P(("pipe", "expert"), None),
            P(("pipe", "expert"), None),
            P(),
            P("pipe", "expert", None, None),
            P("pipe", "expert", None, None),
        ),
        out_specs=(
            P(("pipe", "expert"), None),
            P(("pipe", "expert"), None),
            P("pipe", "expert", None, None),
            P("pipe", "expert", None, None),
        ),
        check_vma=False,
    )
```

profile of v0, /device:TPU:9, one launch (start us, length us, event | category | flops | bytes accessed | tf_op | source)
XLA Modules:
  0.0 593.8 jit_solution(7035733871110516777)
XLA Ops:
  0.6 0.8 copy.37
  1.4 0.1 eq.62
  1.6 0.1 eq.58
  1.7 1.2 fusion.53
  2.9 1.2 fusion.61
  4.0 1.7 reduce-window.16
  5.7 0.3 slice_reduce_fusion
  6.3 0.6 compare_select_fusion
  6.9 0.1 mul.162
  7.1 1.2 fusion.56
  8.3 0.4 broadcast_in_dim.14
  8.6 2.2 reshape.200
  10.9 8.9 %scatter_custom_fusion.2 = bf16[1024,1536]{1,0:T(8,128)(2,1)} fusion(s32[768]{0:T(1024)S(1)} %fusion.72, bf16[768,1536]{1,0:T(8,128)(2,1)} %reshape.200, bf16[]{:T(256)} %constant.12.clone.1), kind=kCustom, calls=%fused_computation.49 | custom fusion | bytes 3146240 | tf_op jit(solution)/shard_map/scatter | solution.py:34
  19.7 6.0 %all-to-all-start.3 = ((bf16[8,2,64,1536]{3,2,1,0:T(8,128)(2,1)}), bf16[8,2,64,1536]{3,2,1,0:T(8,128)(2,1)S(1)}, u32[]{:S(2)}, u32[]{:S(2)}) async-start(bf16[8,2,64,1536]{3,2,1,0:T(8,128)(2,1)} %bitcast.15), calls=%async_computation.3 | async-start | bytes 6291456 | tf_op jit(solution)/shard_map/all_to_all | solution.py:107
  25.7 0.7 copy.41
  26.5 1.0 mul.164
  27.5 3.5 mul.166
  30.9 6.5 %mul.167 = f32[768,1536]{1,0:T(8,128)} reshape(f32[128,6,1536]{2,1,0:T(8,128)} %mul.166) | data formatting | bytes 9437184 | tf_op jit(solution)/shard_map/mul | solution.py:97
  37.4 13.3 %scatter_custom_fusion.1 = bf16[1024,1536]{1,0:T(8,128)(2,1)} fusion(s32[768]{0:T(1024)S(1)} %fusion.72, f32[768,1536]{1,0:T(8,128)} %mul.167, f32[768]{0:T(1024)S(1)} %mul.164, bf16[]{:T(256)} %constant.12.clone.1), kind=kCustom, calls=%fused_computation.45 | custom fusion | flops 2359296 | bytes 7868418 | tf_op jit(solution)/shard_map/scatter | solution.py:34
  50.7 43.0 %all-to-all-done.3 = bf16[8,2,64,1536]{3,2,1,0:T(8,128)(2,1)S(1)} async-done(((bf16[8,2,64,1536]{3,2,1,0:T(8,128)(2,1)}), bf16[8,2,64,1536]{3,2,1,0:T(8,128)(2,1)S(1)}, u32[]{:S(2)}, u32[]{:S(2)}) %all-to-all-start.3) | async-done | bytes 3145760 | tf_op jit(solution)/shard_map/all_to_all | solution.py:107
  93.7 8.1 %all-to-all-start.2 = ((bf16[8,2,64,1536]{3,2,1,0:T(8,128)(2,1)}), bf16[8,2,64,1536]{3,2,1,0:T(8,128)(2,1)}, u32[]{:S(2)}, u32[]{:S(2)}) async-start(bf16[8,2,64,1536]{3,2,1,0:T(8,128)(2,1)} %bitcast.12), calls=%async_computation.2 | async-start | bytes 6291456 | tf_op jit(solution)/shard_map/all_to_all | solution.py:108
  101.8 10.6 %fusion.14 = f32[8,2,64,1536]{3,2,0,1:T(8,128)} fusion(bf16[1,2,1536,1536]{3,2,1,0:T(8,128)(2,1)} %param.18, bf16[8,2,64,1536]{3,2,1,0:T(8,128)(2,1)S(1)} %all-to-all-done.3), kind=kOutput, calls=%fused_computation.23 | convolution fusion | flops 4831838208 | bytes 18874368 | tf_op jit(solution)/shard_map/secd,edf->secf/dot_general | solution.py:51
  112.4 57.3 %all-to-all-done.2 = bf16[8,2,64,1536]{3,2,1,0:T(8,128)(2,1)} async-done(((bf16[8,2,64,1536]{3,2,1,0:T(8,128)(2,1)}), bf16[8,2,64,1536]{3,2,1,0:T(8,128)(2,1)}, u32[]{:S(2)}, u32[]{:S(2)}) %all-to-all-start.2) | async-done | bytes 3145760 | tf_op jit(solution)/shard_map/all_to_all | solution.py:108
  169.7 8.5 %fusion.32 = (bf16[8,2,64,768]{3,2,0,1:T(8,128)(2,1)S(1)}, bf16[8,2,64,768]{3,2,0,1:T(8,128)(2,1)S(1)}) fusion(f32[8,2,64,1536]{3,2,0,1:T(8,128)} %fusion.14, bf16[1,2,768,1536]{3,2,1,0:T(8,128)(2,1)} %param.19, bf16[8,2,64,1536]{3,2,1,0:T(8,128)(2,1)} %all-to-all-done.2), kind=kOutput, calls=%fused_computation.35 | convolution fusion | flops 2426142720 | bytes 17301504 | tf_op jit(solution)/shard_map/secd,efd->secf/dot_general | solution.py:57
  178.3 10.1 %fusion.23 = bf16[8,2,64,1536]{3,2,0,1:T(8,128)(2,1)S(1)} fusion(bf16[1,2,1536,1536]{3,2,1,0:T(8,128)(2,1)} %param.18, bf16[8,2,64,768]{3,2,0,1:T(8,128)(2,1)S(1)} %get-tuple-element.5, bf16[8,2,64,768]{3,2,0,1:T(8,128)(2,1)S(1)} %get-tuple-element.4), kind=kOutput, calls=%fused_computation.26 | convolution fusion | flops 4839702528 | bytes 15728640 | tf_op jit(solution)/shard_map/secf,edf->secd/dot_general | solution.py:63
  188.4 2.0 copy.44
  190.3 7.7 %all-to-all-start.4 = ((bf16[8,2,64,1536]{3,2,1,0:T(8,128)(2,1)}), bf16[8,2,64,1536]{3,2,1,0:T(8,128)(2,1)S(1)}, u32[]{:S(2)}, u32[]{:S(2)}) async-start(bf16[8,2,64,1536]{3,2,1,0:T(8,128)(2,1)} %copy.44), calls=%async_computation.4 | async-start | bytes 6291456 | tf_op jit(solution)/shard_map/all_to_all | solution.py:113
  198.2 0.1 eq.54
  198.4 1.7 reduce-window.14
  200.2 0.3 slice_reduce_fusion.1
  200.4 0.1 reshape.174
  200.8 0.1 mul.148
  201.0 64.9 %all-to-all-done.4 = bf16[8,2,64,1536]{3,2,1,0:T(8,128)(2,1)S(1)} async-done(((bf16[8,2,64,1536]{3,2,1,0:T(8,128)(2,1)}), bf16[8,2,64,1536]{3,2,1,0:T(8,128)(2,1)S(1)}, u32[]{:S(2)}, u32[]{:S(2)}) %all-to-all-start.4) | async-done | bytes 3145760 | tf_op jit(solution)/shard_map/all_to_all | solution.py:113
  266.0 3.8 gather_fusion.1
  269.7 5.0 reshape.209
  274.7 4.7 reduce_sum.80
  279.5 0.3 fusion.57
  279.8 1.0 fusion.60
  280.8 0.4 broadcast_in_dim.12
  281.1 2.2 reshape.184
  283.4 8.8 %scatter_custom_fusion = bf16[1024,1536]{1,0:T(8,128)(2,1)} fusion(s32[768]{0:T(1024)S(1)} %fusion.71, bf16[768,1536]{1,0:T(8,128)(2,1)} %reshape.184, bf16[]{:T(256)} %constant.12.clone.1), kind=kCustom, calls=%fused_computation.52 | custom fusion | bytes 3146240 | tf_op jit(solution)/shard_map/scatter | solution.py:34
  292.2 8.7 %all-to-all-start = ((bf16[8,2,64,1536]{3,2,1,0:T(8,128)(2,1)}), bf16[8,2,64,1536]{3,2,1,0:T(8,128)(2,1)}, u32[]{:S(2)}, u32[]{:S(2)}) async-start(bf16[8,2,64,1536]{3,2,1,0:T(8,128)(2,1)} %bitcast.1), calls=%async_computation | async-start | bytes 6291456 | tf_op jit(solution)/shard_map/all_to_all | solution.py:105
  300.9 7.3 %bitcast_convert_fusion = bf16[2,1536,1536]{2,1,0:T(8,128)(2,1)S(1)} fusion(bf16[8,2,64,1536]{3,2,1,0:T(8,128)(2,1)S(1)} %copy-done.4, bf16[8,2,64,768]{3,2,0,1:T(8,128)(2,1)} %copy-done.13, bf16[8,2,64,768]{3,2,0,1:T(8,128)(2,1)} %copy-done.12), kind=kOutput, calls=%fused_computation.5 | convolution fusion | flops 4842848256 | bytes 15728640 | tf_op jit(solution)/shard_map/secd,secf->edf/dot_general | solution.py:69
  308.2 0.3 constant_dynamic-slice_fusion.1
  308.6 3.3 copy-done
  311.8 1.2 collective-permute-start
  313.1 6.5 %bitcast_convert_fusion.1 = bf16[2,768,1536]{2,1,0:T(8,128)(2,1)S(1)} fusion(bf16[8,2,64,1536]{3,2,1,0:T(8,128)(2,1)} %all-to-all-done.2, f32[8,2,64,1536]{3,2,0,1:T(8,128)} %fusion.14), kind=kOutput, calls=%fused_computation.6 | convolution fusion | flops 2422996992 | bytes 14155776 | tf_op jit(solution)/shard_map/secf,secd->efd/dot_general | solution.py:66
  319.6 2.2 copy-done.2
  321.7 1.6 constant_dynamic-slice_fusion
  323.3 0.3 collective-permute-start.2
  323.6 91.4 %collective-permute-done = bf16[1,1536,1536]{2,1,0:T(8,128)(2,1)} collective-permute-done((bf16[1,1536,1536]{2,1,0:T(8,128)(2,1)S(1)}, bf16[1,1536,1536]{2,1,0:T(8,128)(2,1)}, u32[]{:S(2)}, u32[]{:S(2)}) %collective-permute-start) | collective-permute-done | bytes 4718624 | tf_op jit(solution)/shard_map/ppermute | solution.py:10
  415.0 1.2 collective-permute-start.1
  416.2 8.5 %fusion.11 = f32[8,2,64,1536]{3,2,0,1:T(8,128)S(1)} fusion(bf16[1,2,1536,1536]{3,2,1,0:T(8,128)(2,1)} %param.18, bf16[8,2,64,1536]{3,2,1,0:T(8,128)(2,1)} %all-to-all-done), kind=kOutput, calls=%fused_computation.22 | convolution fusion | flops 4831838208 | bytes 18874368 | tf_op jit(solution)/shard_map/secd,edf->secf/dot_general | solution.py:40
  424.8 5.2 fusion.26
  430.0 2.0 copy.35
  432.0 7.3 %all-to-all-start.1 = ((bf16[8,2,64,1536]{3,2,1,0:T(8,128)(2,1)}), bf16[8,2,64,1536]{3,2,1,0:T(8,128)(2,1)S(1)}, u32[]{:S(2)}, u32[]{:S(2)}) async-start(bf16[8,2,64,1536]{3,2,1,0:T(8,128)(2,1)} %copy.35), calls=%async_computation.1 | async-start | bytes 6291456 | tf_op jit(solution)/shard_map/all_to_all | solution.py:111
  439.3 26.2 %collective-permute-done.2 = bf16[1,768,1536]{2,1,0:T(8,128)(2,1)} collective-permute-done((bf16[1,768,1536]{2,1,0:T(8,128)(2,1)}, bf16[1,768,1536]{2,1,0:T(8,128)(2,1)}, u32[]{:S(2)}, u32[]{:S(2)}) %collective-permute-start.2) | collective-permute-done | bytes 2359328 | tf_op jit(solution)/shard_map/ppermute | solution.py:10
  465.5 1.2 collective-permute-start.3
  467.1 100.1 %collective-permute-done.3 = bf16[1,768,1536]{2,1,0:T(8,128)(2,1)} collective-permute-done((bf16[1,768,1536]{2,1,0:T(8,128)(2,1)}, bf16[1,768,1536]{2,1,0:T(8,128)(2,1)}, u32[]{:S(2)}, u32[]{:S(2)}) %collective-permute-start.3) | collective-permute-done | bytes 2359328 | tf_op jit(solution)/shard_map/ppermute | solution.py:10
  567.2 4.4 fusion.41
  571.6 7.3 %fusion.6 = bf16[1,1,1536,1536]{3,2,1,0:T(8,128)(2,1)} fusion(bf16[1,1536,1536]{2,1,0:T(8,128)(2,1)} %collective-permute-done.1, bf16[2,1536,1536]{2,1,0:T(8,128)(2,1)} %copy-done, s32[]{:T(128)S(6)} %select_n.39), kind=kLoop, calls=%fused_computation.15 | loop fusion | flops 9437184 | bytes 14155780 | tf_op jit(solution)/shard_map/broadcast_in_dim | solution.py:137
  578.8 3.9 gather_fusion
  582.7 5.0 reshape.208
  587.7 5.9 multiply_reduce_fusion
  (48 shorter events, 1.1 us)
Async XLA Ops:
  19.7 6.0 %copy-start.9 = (f32[128,6]{0,1:T(8,128)S(1)}, f32[128,6]{0,1:T(8,128)}, u32[]{:S(2)}) copy-start(f32[128,6]{0,1:T(8,128)} %param.14) | copy-start | bytes 9220
  19.7 7.7 %copy-start.6 = (bf16[128,1536]{1,0:T(8,128)(2,1)S(1)}, bf16[128,1536]{1,0:T(8,128)(2,1)}, u32[]{:S(2)}) copy-start(bf16[128,1536]{1,0:T(8,128)(2,1)} %param.16) | copy-start | bytes 1179652
  19.7 73.9 %all-to-all-start.3 = ((bf16[8,2,64,1536]{3,2,1,0:T(8,128)(2,1)}), bf16[8,2,64,1536]{3,2,1,0:T(8,128)(2,1)S(1)}, u32[]{:S(2)}, u32[]{:S(2)}) async-start(bf16[8,2,64,1536]{3,2,1,0:T(8,128)(2,1)} %bitcast.15), calls=%async_computation.3 | async-start | bytes 6291456 | tf_op jit(solution)/shard_map/all_to_all | solution.py:107
  93.7 8.2 %copy-start.3 = (bf16[8,2,64,1536]{3,2,1,0:T(8,128)(2,1)}, bf16[8,2,64,1536]{3,2,1,0:T(8,128)(2,1)S(1)}, u32[]{:S(2)}) copy-start(bf16[8,2,64,1536]{3,2,1,0:T(8,128)(2,1)S(1)} %all-to-all-done.3) | copy-start | bytes 9437188
  93.7 76.1 %all-to-all-start.2 = ((bf16[8,2,64,1536]{3,2,1,0:T(8,128)(2,1)}), bf16[8,2,64,1536]{3,2,1,0:T(8,128)(2,1)}, u32[]{:S(2)}, u32[]{:S(2)}) async-start(bf16[8,2,64,1536]{3,2,1,0:T(8,128)(2,1)} %bitcast.12), calls=%async_computation.2 | async-start | bytes 6291456 | tf_op jit(solution)/shard_map/all_to_all | solution.py:108
  178.2 10.1 %copy-start.12 = (bf16[8,2,64,768]{3,2,0,1:T(8,128)(2,1)}, bf16[8,2,64,768]{3,2,0,1:T(8,128)(2,1)S(1)}, u32[]{:S(2)}) copy-start(bf16[8,2,64,768]{3,2,0,1:T(8,128)(2,1)S(1)} %get-tuple-element.4) | copy-start | bytes 4718596
  178.2 10.1 %copy-start.13 = (bf16[8,2,64,768]{3,2,0,1:T(8,128)(2,1)}, bf16[8,2,64,768]{3,2,0,1:T(8,128)(2,1)S(1)}, u32[]{:S(2)}) copy-start(bf16[8,2,64,768]{3,2,0,1:T(8,128)(2,1)S(1)} %get-tuple-element.5) | copy-start | bytes 4718596
  190.3 7.7 %copy-start.10 = (s32[128,6]{0,1:T(8,128)S(1)}, s32[128,6]{0,1:T(8,128)}, u32[]{:S(2)}) copy-start(s32[128,6]{0,1:T(8,128)} %param.12) | copy-start | bytes 9220
  190.3 10.1 %copy-start.7 = (s32[128,6]{1,0:T(8,128)S(1)}, s32[128,6]{1,0:T(8,128)}, u32[]{:S(2)}) copy-start(s32[128,6]{1,0:T(8,128)} %get-tuple-element.6) | copy-start | bytes 9220
  190.3 75.6 %all-to-all-start.4 = ((bf16[8,2,64,1536]{3,2,1,0:T(8,128)(2,1)}), bf16[8,2,64,1536]{3,2,1,0:T(8,128)(2,1)S(1)}, u32[]{:S(2)}, u32[]{:S(2)}) async-start(bf16[8,2,64,1536]{3,2,1,0:T(8,128)(2,1)} %copy.44), calls=%async_computation.4 | async-start | bytes 6291456 | tf_op jit(solution)/shard_map/all_to_all | solution.py:113
  274.7 4.7 copy-start.1
  274.7 4.8 copy-start.8
  274.7 5.0 copy-start.5
  292.2 8.7 %copy-start.4 = (bf16[8,2,64,1536]{3,2,1,0:T(8,128)(2,1)S(1)}, bf16[8,2,64,1536]{3,2,1,0:T(8,128)(2,1)}, u32[]{:S(2)}) copy-start(bf16[8,2,64,1536]{3,2,1,0:T(8,128)(2,1)} %copy-done.3) | copy-start | bytes 9437188
  292.2 124.0 %all-to-all-start = ((bf16[8,2,64,1536]{3,2,1,0:T(8,128)(2,1)}), bf16[8,2,64,1536]{3,2,1,0:T(8,128)(2,1)}, u32[]{:S(2)}, u32[]{:S(2)}) async-start(bf16[8,2,64,1536]{3,2,1,0:T(8,128)(2,1)} %bitcast.1), calls=%async_computation | async-start | bytes 6291456 | tf_op jit(solution)/shard_map/all_to_all | solution.py:105
  308.2 3.6 copy-start
  311.8 103.1 %collective-permute-start = (bf16[1,1536,1536]{2,1,0:T(8,128)(2,1)S(1)}, bf16[1,1536,1536]{2,1,0:T(8,128)(2,1)}, u32[]{:S(2)}, u32[]{:S(2)}) collective-permute-start(bf16[1,1536,1536]{2,1,0:T(8,128)(2,1)S(1)} %constant_dynamic-slice_fusion.1), channel_id=1, source_target_pairs={{0,8},{8,0},{16,24},{24,16},{1,9},{9,1},{17,25},{25,17},{2,10},{10... | collective-permute-start | bytes 14155784 | tf_op jit(solution)/shard_map/ppermute | solution.py:10
  319.5 2.2 copy-start.2
  323.3 142.3 %collective-permute-start.2 = (bf16[1,768,1536]{2,1,0:T(8,128)(2,1)}, bf16[1,768,1536]{2,1,0:T(8,128)(2,1)}, u32[]{:S(2)}, u32[]{:S(2)}) collective-permute-start(bf16[1,768,1536]{2,1,0:T(8,128)(2,1)} %constant_dynamic-slice_fusion), channel_id=1, source_target_pairs={{0,8},{8,0},{16,24},{24,16},{1,9},{9,1},{17,25},{25,17},{2,10},{10... | collective-permute-start | bytes 7077896 | tf_op jit(solution)/shard_map/ppermute | solution.py:10
  415.0 156.6 %collective-permute-start.1 = (bf16[1,1536,1536]{2,1,0:T(8,128)(2,1)}, bf16[1,1536,1536]{2,1,0:T(8,128)(2,1)}, u32[]{:S(2)}, u32[]{:S(2)}) collective-permute-start(bf16[1,1536,1536]{2,1,0:T(8,128)(2,1)} %collective-permute-done), channel_id=1, source_target_pairs={{0,16},{8,24},{16,0},{24,8},{1,17},{9,25},{17,1},{25,9},{2,18},{10... | collective-permute-start | bytes 14155784 | tf_op jit(solution)/shard_map/ppermute | solution.py:10
  432.0 35.0 %copy-start.11 = (f32[128,6]{0,1:T(8,128)S(1)}, f32[128,6]{0,1:T(8,128)}, u32[]{:S(2)}) copy-start(f32[128,6]{0,1:T(8,128)} %param.11) | copy-start | bytes 9220
  432.0 146.9 %all-to-all-start.1 = ((bf16[8,2,64,1536]{3,2,1,0:T(8,128)(2,1)}), bf16[8,2,64,1536]{3,2,1,0:T(8,128)(2,1)S(1)}, u32[]{:S(2)}, u32[]{:S(2)}) async-start(bf16[8,2,64,1536]{3,2,1,0:T(8,128)(2,1)} %copy.35), calls=%async_computation.1 | async-start | bytes 6291456 | tf_op jit(solution)/shard_map/all_to_all | solution.py:111
  465.5 101.6 %collective-permute-start.3 = (bf16[1,768,1536]{2,1,0:T(8,128)(2,1)}, bf16[1,768,1536]{2,1,0:T(8,128)(2,1)}, u32[]{:S(2)}, u32[]{:S(2)}) collective-permute-start(bf16[1,768,1536]{2,1,0:T(8,128)(2,1)} %collective-permute-done.2), channel_id=1, source_target_pairs={{0,16},{8,24},{16,0},{24,8},{1,17},{9,25},{17,1},{25,9},{2,18},{10... | collective-permute-start | bytes 7077896 | tf_op jit(solution)/shard_map/ppermute | solution.py:10
where the time goes:
time: 604 us; the launch traced here: 594 us
  waiting for transfers between devices  383 us (63%)
  local copies, waits for them, and re-layouts  66.4 us (11%)
  matrix products  56.7 us (9%)
  other arithmetic  44.7 us (7%)
  starting transfers between devices  41.8 us (7%)
    ppermute x4, waiting for transfers between devices, from_partner(): lax.ppermute(value, axis, [(i, i ^ 1 << bit) for i in range(lax.axis_size...  218 us
    all_to_all x1, waiting for transfers between devices, per_device(): lax.all_to_all(d_inputs, 'expert', split_axis=0, concat_axis=0, tiled=True)  64.9 us
    all_to_all x1, waiting for transfers between devices, per_device(): lax.all_to_all(send_cot, 'expert', split_axis=0, concat_axis=0, tiled=True)  57.3 us
    all_to_all x1, waiting for transfers between devices, per_device(): lax.all_to_all(send_inputs, 'expert', split_axis=0, concat_axis=0, tiled=...  43 us
    scatter x2, local copies, waits for them, and re-layouts, place_rows(): return jnp.zeros((slot_total, values.shape[-1]), values.dtype).at[dest.re...  17.7 us
    scatter x1, other arithmetic, place_rows(): return jnp.zeros((slot_total, values.shape[-1]), values.dtype).at[dest.re...  13.3 us
  transfers between devices with their start and end apart: 9, of which 6 were waited for; matrix products, arithmetic and copies ran while one was open for 14% of the time, Pallas kernels for 0%

commit v1 on v0

v1 whole, which is shorter than its diff:
```python
import jax
import jax.numpy as jnp
from jax import lax
from jax.sharding import PartitionSpec as P

norm_eps = 1e-06


def normalize(inputs):
    values = inputs.astype(jnp.float32)
    scale = lax.rsqrt(jnp.mean(values * values, axis=-1, keepdims=True) + norm_eps)
    return (values * scale, scale)


def expert_gates(gates, routes, expert_count):
    chosen = routes[None, :, :] == jnp.arange(expert_count, dtype=jnp.int32)[:, None, None]
    return jnp.sum(jnp.where(chosen, gates[None], 0.0), axis=-1)


def placement(gates, capacity):
    named = gates > 0.0
    slot = jnp.cumsum(named.astype(jnp.int32), axis=-1) - 1
    wanted = jnp.arange(capacity, dtype=jnp.int32)[:, None]
    onehot = (slot[..., None, :] == wanted) & named[..., None, :]
    slot_gates = jnp.sum(jnp.where(onehot, gates[..., None, :], 0.0), axis=-1)
    return (onehot.astype(jnp.bfloat16), slot_gates)


def hidden_parts(inputs, weight_gu, hidden_units):
    both_parts = jnp.einsum("erd,edf->erf", inputs, weight_gu, preferred_element_type=jnp.float32)
    return (both_parts[..., :hidden_units], both_parts[..., hidden_units:])


def backward_parts(inputs, cot_rows, weight_gu, weight_dn):
    gate_pre, up_pre = hidden_parts(inputs, weight_gu, weight_dn.shape[1])
    squash = jax.nn.sigmoid(gate_pre)
    activated = gate_pre * squash
    hidden = (activated * up_pre).astype(jnp.bfloat16)
    back_hidden = jnp.einsum(
        "erd,efd->erf", cot_rows, weight_dn, preferred_element_type=jnp.float32
    )
    d_gate = back_hidden * up_pre * squash * (1.0 + gate_pre * (1.0 - squash))
    d_up = back_hidden * activated
    return (hidden, jnp.concatenate([d_gate, d_up], axis=-1).astype(jnp.bfloat16))


def per_device(
    x_fwd, gate_fwd, route_fwd, x_bwd, gate_bwd, route_bwd, cotangent, norm_gain, w_gate_up, w_down
):
    group_count = lax.axis_size("expert")
    section_count = lax.axis_size("pipe")
    local_count = w_gate_up.shape[1]
    expert_count = local_count * group_count
    token_count, model_width = x_fwd.shape
    pick_count = route_fwd.shape[1]
    capacity = token_count * pick_count * 4 // (3 * expert_count)
    row_count = group_count * capacity
    weight_gu = w_gate_up[0]
    weight_dn = w_down[0]
    hidden_units = weight_dn.shape[1]

    bwd_hat, bwd_scale = normalize(x_bwd)
    bwd_normed = (bwd_hat * norm_gain).astype(jnp.bfloat16)
    fwd_normed = (normalize(x_fwd)[0] * norm_gain).astype(jnp.bfloat16)

    send_gates = jnp.stack(
        [
            expert_gates(gate_fwd, route_fwd, expert_count),
            expert_gates(gate_bwd, route_bwd, expert_count),
        ]
    ).reshape(2, group_count, local_count, token_count)
    recv_gates = lax.all_to_all(
        send_gates.transpose(1, 0, 2, 3), "expert", split_axis=0, concat_axis=0, tiled=True
    ).transpose(1, 2, 0, 3)

    gathered_bwd = lax.all_gather(
        jnp.concatenate([bwd_normed, cotangent], axis=0)[None], "expert", axis=0, tiled=True
    )
    gathered_fwd = lax.all_gather(fwd_normed[None], "expert", axis=0, tiled=True)

    place_bwd, slot_gates_bwd = placement(recv_gates[1], capacity)
    rows_h = jnp.einsum(
        "egst,gtd->egsd", place_bwd, gathered_bwd[:, :token_count], preferred_element_type=jnp.float32
    ).astype(jnp.bfloat16)
    rows_c = jnp.einsum(
        "egst,gtd->egsd", place_bwd, gathered_bwd[:, token_count:], preferred_element_type=jnp.float32
    )
    rows_c = (rows_c * slot_gates_bwd[..., None]).astype(jnp.bfloat16)
    rows_h = rows_h.reshape(local_count, row_count, model_width)
    rows_c = rows_c.reshape(local_count, row_count, model_width)

    section_index = lax.axis_index("pipe")
    upper_half = (section_index >= section_count // 2).astype(jnp.int32)
    half_local = local_count // 2

    def kept(value):
        return lax.dynamic_slice_in_dim(value, upper_half * half_local, half_local, 0)

    def given(value):
        return lax.dynamic_slice_in_dim(value, (1 - upper_half) * half_local, half_local, 0)

    mirror = [(i, section_count - 1 - i) for i in range(section_count)]
    mirror_h = lax.ppermute(given(rows_h), "pipe", mirror)
    mirror_c = lax.ppermute(given(rows_c), "pipe", mirror)

    hidden, d_both = backward_parts(rows_h, rows_c, weight_gu, weight_dn)
    d_inputs = jnp.einsum(
        "erf,edf->erd", d_both, weight_gu, preferred_element_type=jnp.float32
    ).astype(jnp.bfloat16)
    partial_dh = jnp.einsum(
        "egst,egsd->gtd",
        place_bwd,
        d_inputs.reshape(local_count, group_count, capacity, model_width),
        preferred_element_type=jnp.float32,
    ).astype(jnp.bfloat16)
    dh_sum = lax.psum_scatter(
        partial_dh.reshape(group_count * token_count, model_width),
        "expert",
        scatter_dimension=0,
        tiled=True,
    ).astype(jnp.float32)

    place_fwd, slot_gates_fwd = placement(recv_gates[0], capacity)
    rows_f = (
        jnp.einsum(
            "egst,gtd->egsd", place_fwd, gathered_fwd, preferred_element_type=jnp.float32
        )
        .astype(jnp.bfloat16)
        .reshape(local_count, row_count, model_width)
    )
    gate_pre, up_pre = hidden_parts(rows_f, weight_gu, hidden_units)
    hidden_fwd = (jax.nn.silu(gate_pre) * up_pre).astype(jnp.bfloat16)
    out_rows = jnp.einsum(
        "erf,efd->erd", hidden_fwd, weight_dn, preferred_element_type=jnp.float32
    )
    out_rows = (out_rows * slot_gates_fwd.reshape(local_count, row_count, 1)).astype(jnp.bfloat16)
    partial_y = jnp.einsum(
        "egst,egsd->gtd",
        place_fwd,
        out_rows.reshape(local_count, group_count, capacity, model_width),
        preferred_element_type=jnp.float32,
    ).astype(jnp.bfloat16)
    y_fwd = lax.psum_scatter(
        partial_y.reshape(group_count * token_count, model_width),
        "expert",
        scatter_dimension=0,
        tiled=True,
    )

    mirror_hidden, mirror_d = backward_parts(mirror_h, mirror_c, kept(weight_gu), kept(weight_dn))
    all_h = jnp.concatenate([kept(rows_h), mirror_h], axis=1)
    all_c = jnp.concatenate([kept(rows_c), mirror_c], axis=1)
    all_hidden = jnp.concatenate([kept(hidden), mirror_hidden], axis=1)
    all_d = jnp.concatenate([kept(d_both), mirror_d], axis=1)
    out_dn = jnp.einsum(
        "erf,erd->efd", all_hidden, all_c, preferred_element_type=jnp.float32
    ).astype(jnp.bfloat16)
    out_gu = jnp.einsum("erd,erf->edf", all_h, all_d, preferred_element_type=jnp.float32).astype(
        jnp.bfloat16
    )

    scaled_dh = norm_gain * dh_sum
    dx_bwd = (
        bwd_scale * (scaled_dh - bwd_hat * jnp.mean(bwd_hat * scaled_dh, axis=-1, keepdims=True))
    ).astype(jnp.bfloat16)
    return (y_fwd, dx_bwd, out_gu[None], out_dn[None])


def solution(mesh):
    rows = P(("pipe", "expert"), None)
    experts = P("pipe", "expert", None, None)
    return jax.shard_map(
        per_device,
        mesh=mesh,
        in_specs=(rows,) * 7 + (P(), experts, experts),
        out_specs=(rows, rows, experts, experts),
        check_vma=False,
    )
```

time: 604 us -> 304 us (0.50); the launches traced: 594 us -> 301 us
  waiting for transfers between devices: 383 us -> 187 us
  local copies, waits for them, and re-layouts: 66.4 us -> 7.33 us
  starting transfers between devices: 41.8 us -> 4.15 us
  other arithmetic: 44.7 us -> 12.8 us
  between operations: 1.22 us -> 14.1 us
  blocking collectives: 0 us -> 9.32 us
  matrix products: 56.7 us -> 65.7 us
    all_to_all x5 -> x0, waiting for transfers between devices: 165 us -> none  [the longest x1 64.9 us: per_device(): lax.all_to_all(d_inputs, 'expert', split_axis=0, concat_axis=0, tiled=True)]
    ppermute x4 -> x2, waiting for transfers between devices: 218 us -> 61.2 us  [the longest x1 32 us: per_device(): mirror_h = lax.ppermute(given(rows_h), 'pipe', mirror)]
    all_gather x0 -> x2, waiting for transfers between devices: none -> 89.4 us  [the longest x1 52.8 us: per_device(): lax.all_gather(jnp.concatenate([bwd_normed, cotangent], axis=0)[None], 'e...]
    all_to_all x5 -> x0, starting transfers between devices: 37.8 us -> none  [the longest x1 8.69 us: per_device(): lax.all_to_all(send_fwd, 'expert', split_axis=0, concat_axis=0, tiled=True)]
    reduce_scatter x0 -> x2, waiting for transfers between devices: none -> 36.8 us  [the longest x1 36.8 us: per_device(): lax.psum_scatter(partial_dh.reshape(group_count * token_count, model_widt...]
    scatter x2 -> x0, local copies, waits for them, and re-layouts: 17.7 us -> none  [place_rows(): return jnp.zeros((slot_total, values.shape[-1]), values.dtype).at[dest.re...]
    scatter x1 -> x0, other arithmetic: 13.3 us -> none  [place_rows(): return jnp.zeros((slot_total, values.shape[-1]), values.dtype).at[dest.re...]
    broadcast_in_dim x2 -> x0, other arithmetic: 11.6 us -> none  [per_device(): return (y_fwd, dx_bwd, out_gu[None], out_dn[None])]
  transfers between devices with their start and end apart: 9 -> 6, of which waited for: 6 -> 5; matrix products, arithmetic and copies ran while one was open for 14% -> 9% of each run, Pallas kernels for 0% -> 0%
where the time goes in v1:
time: 304 us; the launch traced here: 301 us
  waiting for transfers between devices  187 us (62%)
  matrix products  65.7 us (22%)
  between operations  14.1 us (5%)
  other arithmetic  12.8 us (4%)
  blocking collectives  9.32 us (3%)
  local copies, waits for them, and re-layouts  7.33 us (2%)
  starting transfers between devices  4.15 us (1%)
    all_gather x1, waiting for transfers between devices, per_device(): lax.all_gather(jnp.concatenate([bwd_normed, cotangent], axis=0)[None], 'e...  52.8 us
    reduce_scatter x1, waiting for transfers between devices, per_device(): lax.psum_scatter(partial_dh.reshape(group_count * token_count, model_widt...  36.8 us
    all_gather x1, waiting for transfers between devices, per_device(): lax.all_gather(fwd_normed[None], 'expert', axis=0, tiled=True)  36.6 us
    ppermute x1, waiting for transfers between devices, per_device(): mirror_h = lax.ppermute(given(rows_h), 'pipe', mirror)  32 us
    ppermute x1, waiting for transfers between devices, per_device(): mirror_c = lax.ppermute(given(rows_c), 'pipe', mirror)  29.2 us
    dot_general x3, matrix products, hidden_parts(): jnp.einsum('erd,edf->erf', inputs, weight_gu, preferred_element_type=jnp....  17.3 us
    dot_general x2, matrix products, backward_parts(): jnp.einsum('erd,efd->erf', cot_rows, weight_dn, preferred_element_type=jn...  12.2 us
    dot_general x1, matrix products, per_device(): jnp.einsum('erd,erf->edf', all_h, all_d, preferred_element_type=jnp.float32)  9.84 us
  transfers between devices with their start and end apart: 6, of which 5 were waited for; matrix products, arithmetic and copies ran while one was open for 9% of the time, Pallas kernels for 0%

profile of v1, /device:TPU:9, one launch (start us, length us, event | category | flops | bytes accessed | tf_op | source)
XLA Modules:
  0.0 300.8 jit_solution(11996782616701386571)
XLA Ops:
  7.2 0.0 all-gather.7.cloned.1.call-start
  7.3 1.2 fusion.65
  8.4 1.2 fusion.60
  9.6 1.9 pad_maximum_fusion.2
  11.5 0.0 all-gather.7.cloned.1.call-update
  11.5 0.0 reduce-scatter.5.cloned.1.call-start
  11.7 9.3 %all_to_all.5 = f32[8,2,2,128]{3,2,1,0:T(2,128)S(1)} all-to-all(f32[8,2,2,128]{3,2,1,0:T(2,128)S(1)} %copy.70), channel_id=1, replica_groups=mesh['pipe'=4,'expert'=8] {'expert'}, dimensions={0} | all-to-all | bytes 32768 | tf_op jit(solution)/shard_map/all_to_all | solution.py:72
  21.0 0.6 fusion.89
  21.6 0.6 reduce_window_sum.18
  22.2 0.6 slice_bitcast_fusion.4
  22.8 0.2 select_reduce_fusion
  23.1 52.8 %all-gather.7.cloned.1.call-done = bf16[2048,1536]{1,0:T(8,128)(2,1)} async-done(((bf16[256,1536]{1,0:T(8,128)(2,1)}), bf16[2048,1536]{1,0:T(8,128)(2,1)}) %all-gather.7.cloned.1.call-update) | async-done | bytes 6291472 | tf_op jit(solution)/shard_map/all_gather | solution.py:76
  75.8 3.0 fusion.21
  78.8 0.7 copy-done.4
  79.6 1.0 fusion.7
  80.5 0.0 slice-start.2
  80.5 1.9 copy.79
  82.5 0.3 copy.80
  82.8 1.4 slice-done.1
  84.2 0.4 slice-done.2
  84.6 5.0 %fusion.2 = f32[2,512,1536]{2,1,0:T(8,128)S(1)} fusion(bf16[2,512,1536]{2,1,0:T(8,128)(2,1)S(1)} %bitcast.125, bf16[1,2,1536,1536]{3,2,1,0:T(8,128)(2,1)S(1)} %bitcast.128), kind=kOutput, calls=%fused_computation.2 | convolution fusion | flops 4831838208 | bytes 18874368 | tf_op jit(solution)/shard_map/erd,edf->erf/dot_general | solution.py:30
  89.6 10.4 %multiply_convert_fusion.2 = (bf16[2,512,768]{2,1,0:T(8,128)(2,1)}, bf16[2,512,768]{2,1,0:T(8,128)(2,1)}, f32[2,512,768]{2,1,0:T(8,128)}, f32[2,512,768]{2,1,0:T(8,128)}) fusion(f32[2,512,1536]{2,1,0:T(8,128)S(1)} %fusion.2, bf16[2,512,1536]{2,1,0:T(8,128)(2,1)} %bitcast.130, bf16[1,2,768,1536]{3,2,1,0:T(8,128)(2,1)} %param.19), kind=kOutput, calls=%fused_computation.48 | convolution fusion | flops 2426142720 | bytes 23592960 | tf_op jit(solution)/shard_map/erd,efd->erf/dot_general | solution.py:39
  100.0 7.2 %fusion.17 = bf16[2,512,1536]{2,1,0:T(8,128)(2,1)S(1)} fusion(bf16[1,2,1536,1536]{3,2,1,0:T(8,128)(2,1)S(1)} %bitcast.128, bf16[2,512,768]{2,1,0:T(8,128)(2,1)} %get-tuple-element.9, bf16[2,512,768]{2,1,0:T(8,128)(2,1)} %get-tuple-element.8), kind=kOutput, calls=%fused_computation.20 | convolution fusion | flops 4839702528 | bytes 15728640 | tf_op jit(solution)/shard_map/erf,edf->erd/dot_general | solution.py:107
  107.2 2.7 bitcast_convert_fusion
  110.0 0.0 reduce-scatter.5.cloned.1.call-update
  110.0 0.2 all-gather.5.cloned.1.call-start
  110.2 1.2 fusion.57
  111.4 0.6 add_rsqrt_fusion.1
  112.0 36.8 %reduce-scatter.5.cloned.1.call-done = bf16[128,1536]{1,0:T(8,128)(2,1)} async-done(((bf16[1024,1536]{1,0:T(8,128)(2,1)}), bf16[128,1536]{1,0:T(8,128)(2,1)}) %reduce-scatter.5.cloned.1.call-update) | async-done | bytes 393232 | tf_op jit(solution)/shard_map/reduce_scatter | solution.py:116
  148.8 0.0 copy-done.1
  148.8 1.3 fusion.61
  150.1 2.3 fusion.64
  152.4 0.0 all-gather.5.cloned.1.call-update
  152.4 0.0 reduce-scatter.3.cloned.1.call-start
  152.4 0.7 copy.72
  153.1 0.6 reduce_window_sum.17
  153.7 0.9 select_reduce_fusion.1
  154.6 0.1 mul.133
  154.7 36.6 %all-gather.5.cloned.1.call-done = bf16[1024,1536]{1,0:T(8,128)(2,1)} async-done(((bf16[128,1536]{1,0:T(8,128)(2,1)}), bf16[1024,1536]{1,0:T(8,128)(2,1)}) %all-gather.5.cloned.1.call-update) | async-done | bytes 3145744 | tf_op jit(solution)/shard_map/all_gather | solution.py:79
  191.3 2.9 fusion.20
  194.2 0.0 slice-start.3
  194.2 0.3 copy.74
  194.5 0.0 slice-start.4
  194.5 7.8 %fusion.4 = f32[2,512,1536]{2,1,0:T(8,128)S(1)} fusion(bf16[2,512,1536]{2,1,0:T(8,128)(2,1)S(1)} %bitcast.129, bf16[1,2,1536,1536]{3,2,1,0:T(8,128)(2,1)} %param.18), kind=kOutput, calls=%fused_computation.4 | convolution fusion | flops 4831838208 | bytes 18874368 | tf_op jit(solution)/shard_map/erd,edf->erf/dot_general | solution.py:30
  202.3 2.9 multiply_convert_fusion
  205.2 2.7 bitcast_convert_fusion.1
  208.0 0.0 reduce-scatter.3.cloned.1.call-update
  208.0 0.0 copy-start
  208.0 0.2 constant_dynamic-slice_fusion.3
  208.2 2.2 collective-permute-start
  210.4 0.2 constant_dynamic-slice_fusion
  210.6 0.0 copy-start.2
  210.6 1.6 collective-permute-start.1
  212.3 0.0 copy-done.6
  212.3 0.1 fusion.43
  212.4 0.4 copy-done.3
  212.8 0.1 fusion.42
  212.9 0.0 slice-start.6
  213.0 32.0 %collective-permute-done = bf16[1,512,1536]{2,1,0:T(8,128)(2,1)S(1)} collective-permute-done((bf16[1,512,1536]{2,1,0:T(8,128)(2,1)S(1)}, bf16[1,512,1536]{2,1,0:T(8,128)(2,1)S(1)}, u32[]{:S(2)}, u32[]{:S(2)}) %collective-permute-start) | collective-permute-done | bytes 1572896 | tf_op jit(solution)/shard_map/ppermute | solution.py:103
  244.9 4.5 %fusion.22 = f32[1,512,1536]{2,1,0:T(8,128)S(1)} fusion(bf16[1,2,1536,1536]{3,2,1,0:T(8,128)(2,1)} %param.18, s32[]{:T(128)S(6)} %select_n.30, bf16[1,512,1536]{2,1,0:T(8,128)(2,1)S(1)} %collective-permute-done), kind=kOutput, calls=%fused_computation.29 | convolution fusion | flops 2415919104 | bytes 9437188 | tf_op jit(solution)/shard_map/erd,edf->erf/dot_general | solution.py:30
  249.5 29.2 %collective-permute-done.1 = bf16[1,512,1536]{2,1,0:T(8,128)(2,1)S(1)} collective-permute-done((bf16[1,512,1536]{2,1,0:T(8,128)(2,1)S(1)}, bf16[1,512,1536]{2,1,0:T(8,128)(2,1)S(1)}, u32[]{:S(2)}, u32[]{:S(2)}) %collective-permute-start.1) | collective-permute-done | bytes 1572896 | tf_op jit(solution)/shard_map/ppermute | solution.py:104
  278.7 1.8 fusion.49
  280.5 3.9 %fusion.37 = bf16[1,1,768,1536]{3,2,1,0:T(8,128)(2,1)} fusion(bf16[1,512,1536]{2,1,0:T(8,128)(2,1)S(1)} %collective-permute-done.1, bf16[1,512,1536]{2,1,0:T(8,128)(2,1)S(1)} %get-tuple-element.15, bf16[1,512,768]{2,1,0:T(8,128)(2,1)S(1)} %get-tuple-element.14, bf16[1,512,768]{2,1,0:T(8,128)(2,1)S(1)} %fusion.43), kind=kOutput, calls=%fused_computation.51 | convolution fusion | flops 2426535936 | bytes 7077888 | tf_op jit(solution)/shard_map/erf,erd->efd/dot_general | solution.py:155
  284.4 9.8 %fusion.6 = bf16[1,1,1536,1536]{3,2,1,0:T(8,128)(2,1)} fusion(bf16[1,512,1536]{2,1,0:T(8,128)(2,1)S(1)} %collective-permute-done, bf16[1,512,1536]{2,1,0:T(8,128)(2,1)S(1)} %get-tuple-element.17, bf16[1,512,768]{2,1,0:T(8,128)(2,1)S(1)} %get-tuple-element.13, bf16[1,512,768]{2,1,0:T(8,128)(2,1)S(1)} %get-tuple-element.12, bf16[1,512,1536]{2,1,0:T(8,128)(2,1)S(1)} %fusion.42), kind=kOutput, calls=%fused_computation.7 | convolution fusion | flops 4849926144 | bytes 11010048 | tf_op jit(solution)/shard_map/erd,erf->edf/dot_general | solution.py:158
  (42 shorter events, 0.1 us)
Async XLA Ops:
  7.2 4.4 %copy-start.8 = (f32[128,6]{0,1:T(8,128)S(1)}, f32[128,6]{0,1:T(8,128)}, u32[]{:S(2)}) copy-start(f32[128,6]{0,1:T(8,128)} %param.11) | copy-start | bytes 9220
  7.2 4.4 %copy-start.9 = (s32[128,6]{0,1:T(8,128)S(1)}, s32[128,6]{0,1:T(8,128)}, u32[]{:S(2)}) copy-start(s32[128,6]{0,1:T(8,128)} %param.12) | copy-start | bytes 9220
  7.2 4.4 %copy-start.10 = (f32[128,6]{0,1:T(8,128)S(1)}, f32[128,6]{0,1:T(8,128)}, u32[]{:S(2)}) copy-start(f32[128,6]{0,1:T(8,128)} %param.14) | copy-start | bytes 9220
  7.2 4.4 %copy-start.11 = (s32[128,6]{0,1:T(8,128)S(1)}, s32[128,6]{0,1:T(8,128)}, u32[]{:S(2)}) copy-start(s32[128,6]{0,1:T(8,128)} %param.15) | copy-start | bytes 9220
  7.2 68.6 %all-gather.7.cloned.1.call-start = ((), (), s32[]{:S(2)}) async-start(), calls=%async_computation.6 | async-start | bytes 7077888 | tf_op jit(solution)/shard_map/all_gather | solution.py:76
  11.5 137.3 %reduce-scatter.5.cloned.1.call-start = ((), (), s32[]{:S(2)}) async-start(), calls=%async_computation.4 | async-start | bytes 3538944 | tf_op jit(solution)/shard_map/reduce_scatter | solution.py:116
  75.8 3.7 %copy-start.4 = (bf16[2048,1536]{1,0:T(8,128)(2,1)S(1)}, bf16[2048,1536]{1,0:T(8,128)(2,1)}, u32[]{:S(2)}) copy-start(bf16[2048,1536]{1,0:T(8,128)(2,1)} %all-gather.7.cloned.1.call-done) | copy-start | bytes 18874372
  79.5 3.2 %slice-start = ((s8[9437184]{0:T(1024)(128)(4,1)}), s8[4194304]{0:T(1024)(128)(4,1)S(1)}, s32[]{:S(2)}) async-start(s8[9437184]{0:T(1024)(128)(4,1)} %bitcast.127), calls=%async_computation.7 | async-start | bytes 8388608
  79.6 4.6 %slice-start.1 = ((s8[9437184]{0:T(1024)(128)(4,1)}), s8[4194304]{0:T(1024)(128)(4,1)S(1)}, s32[]{:S(2)}) async-start(s8[9437184]{0:T(1024)(128)(4,1)} %bitcast.127), calls=%async_computation.8 | async-start | bytes 8388608
  80.5 4.1 %slice-start.2 = ((s8[9437184]{0:T(1024)(128)(4,1)}), s8[1048576]{0:T(1024)(128)(4,1)S(1)}, s32[]{:S(2)}) async-start(s8[9437184]{0:T(1024)(128)(4,1)} %bitcast.127), calls=%async_computation.9 | async-start | bytes 2097152
  109.9 38.9 %copy-start.1 = (bf16[128,1536]{1,0:T(8,128)(2,1)S(1)}, bf16[128,1536]{1,0:T(8,128)(2,1)}, u32[]{:S(2)}) copy-start(bf16[128,1536]{1,0:T(8,128)(2,1)} %param.13) | copy-start | bytes 1179652
  109.9 38.9 %copy-start.7 = (f32[1536]{0:T(1024)S(1)}, f32[1536]{0:T(1024)}, u32[]{:S(2)}) copy-start(f32[1536]{0:T(1024)} %param.17) | copy-start | bytes 18436
  110.0 81.4 %all-gather.5.cloned.1.call-start = ((), (), s32[]{:S(2)}) async-start(), calls=%async_computation.5 | async-start | bytes 3538944 | tf_op jit(solution)/shard_map/all_gather | solution.py:79
  152.4 141.9 %reduce-scatter.3.cloned.1.call-start = ((), (), s32[]{:S(2)}) async-start(), calls=%async_computation.3 | async-start | bytes 3538944 | tf_op jit(solution)/shard_map/reduce_scatter | solution.py:143
  194.2 8.1 %slice-start.3 = ((s8[4718592]{0:T(1024)(128)(4,1)}), s8[4194304]{0:T(1024)(128)(4,1)S(1)}, s32[]{:S(2)}) async-start(s8[4718592]{0:T(1024)(128)(4,1)} %bitcast.143), calls=%async_computation.10 | async-start | bytes 8388608
  194.5 7.8 %slice-start.4 = ((s8[4718592]{0:T(1024)(128)(4,1)}), s8[524288]{0:T(1024)(128)(4,1)S(1)}, s32[]{:S(2)}) async-start(s8[4718592]{0:T(1024)(128)(4,1)} %bitcast.143), calls=%async_computation.11 | async-start | bytes 1048576
  208.0 2.4 copy-start
  208.2 4.1 %copy-start.5 = (f32[2,512,768]{2,1,0:T(8,128)S(1)}, f32[2,512,768]{2,1,0:T(8,128)}, u32[]{:S(2)}) copy-start(f32[2,512,768]{2,1,0:T(8,128)} %get-tuple-element.10) | copy-start | bytes 9437188
  208.2 4.0 %copy-start.6 = (f32[2,512,768]{2,1,0:T(8,128)S(1)}, f32[2,512,768]{2,1,0:T(8,128)}, u32[]{:S(2)}) copy-start(f32[2,512,768]{2,1,0:T(8,128)} %get-tuple-element.11) | copy-start | bytes 9437188
  208.2 36.7 %collective-permute-start = (bf16[1,512,1536]{2,1,0:T(8,128)(2,1)S(1)}, bf16[1,512,1536]{2,1,0:T(8,128)(2,1)S(1)}, u32[]{:S(2)}, u32[]{:S(2)}) collective-permute-start(bf16[1,512,1536]{2,1,0:T(8,128)(2,1)S(1)} %get-tuple-element.18), channel_id=1, source_target_pairs={{0,24},{8,16},{16,8},{24,0},{1,25},{9,17},{17,9},{25,1},{2,26},{10... | collective-permute-start | bytes 4718600 | tf_op jit(solution)/shard_map/ppermute | solution.py:103
  210.6 1.8 copy-start.2
  210.6 2.2 copy-start.3
  210.6 68.0 %collective-permute-start.1 = (bf16[1,512,1536]{2,1,0:T(8,128)(2,1)S(1)}, bf16[1,512,1536]{2,1,0:T(8,128)(2,1)S(1)}, u32[]{:S(2)}, u32[]{:S(2)}) collective-permute-start(bf16[1,512,1536]{2,1,0:T(8,128)(2,1)S(1)} %get-tuple-element.16), channel_id=1, source_target_pairs={{0,24},{8,16},{16,8},{24,0},{1,25},{9,17},{17,9},{25,1},{2,26},{10... | collective-permute-start | bytes 4718600 | tf_op jit(solution)/shard_map/ppermute | solution.py:104
  212.8 65.8 %slice-start.5 = ((s8[4718592]{0:T(1024)(128)(4,1)}), s8[4194304]{0:T(1024)(128)(4,1)S(1)}, s32[]{:S(2)}) async-start(s8[4718592]{0:T(1024)(128)(4,1)} %bitcast.145), calls=%async_computation.12 | async-start | bytes 8388608
  212.9 65.7 %slice-start.6 = ((s8[4718592]{0:T(1024)(128)(4,1)}), s8[524288]{0:T(1024)(128)(4,1)S(1)}, s32[]{:S(2)}) async-start(s8[4718592]{0:T(1024)(128)(4,1)} %bitcast.145), calls=%async_computation.13 | async-start | bytes 1048576
Sparse Core Ops, SparseCore 0:
  11.7 64.1 all-gather.6
  110.1 38.6 reduce-scatter.4
  152.5 38.7 all-gather.4
  208.1 37.8 reduce-scatter.2

commit v2 on v1

v2 whole, which is shorter than its diff:
```python
import functools

import jax
import jax.numpy as jnp
from jax import lax
from jax.experimental import pallas as pl
from jax.experimental.pallas import tpu as pltpu
from jax.sharding import PartitionSpec as P

norm_eps = 1e-06
tile = 256
vmem_bytes = 56 * 1024 * 1024


def params():
    return pltpu.CompilerParams(
        dimension_semantics=("arbitrary",), vmem_limit_bytes=vmem_bytes
    )


def light():
    return pl.CostEstimate(flops=1000, bytes_accessed=1000, transcendentals=0)


def dot(a, b, contract=((1,), (0,))):
    return lax.dot_general(a, b, (contract, ((), ())), preferred_element_type=jnp.float32)


def normalize(inputs):
    values = inputs.astype(jnp.float32)
    scale = lax.rsqrt(jnp.mean(values * values, axis=-1, keepdims=True) + norm_eps)
    return (values * scale, scale)


def expert_gates(gates, routes, expert_count):
    chosen = routes[None, :, :] == jnp.arange(expert_count, dtype=jnp.int32)[:, None, None]
    return jnp.sum(jnp.where(chosen, gates[None], 0.0), axis=-1)


def ranks(gates):
    named = gates > 0.0
    token_count = gates.shape[1]
    upto = lax.broadcasted_iota(jnp.int32, (token_count, token_count), 0) <= (
        lax.broadcasted_iota(jnp.int32, (token_count, token_count), 1)
    )
    count = dot(
        jnp.where(named, 1.0, 0.0).astype(jnp.bfloat16), jnp.where(upto, 1.0, 0.0).astype(jnp.bfloat16)
    )
    return jnp.where(named, count - 1.0, -1.0)


def onehot_rows(rank, group, local_count, capacity):
    token_count = rank.shape[1]
    slots = lax.broadcasted_iota(jnp.int32, (capacity, token_count), 0).astype(jnp.float32)
    parts = []
    for local in range(local_count):
        row = group * local_count + local
        parts.append(jnp.where(rank[row : row + 1, :] == slots, 1.0, 0.0))
    return jnp.concatenate(parts, axis=0)


def slot_gates(onehot, gates, group, local_count, capacity):
    parts = []
    for local in range(local_count):
        row = group * local_count + local
        own = onehot[local * capacity : (local + 1) * capacity]
        parts.append(jnp.sum(own * gates[row : row + 1, :], axis=1, keepdims=True))
    return jnp.concatenate(parts, axis=0)


def cuts(row_count):
    ends = [0, row_count * 5 // 8, row_count * 21 // 16, row_count * 2]
    return [(start, end) for start, end in zip(ends[:-1], ends[1:])]


def overlaps(row_count, start, end):
    for send, (low, high) in enumerate(cuts(row_count)):
        first, last = max(start, low), min(end, high)
        if first < last:
            yield send, slice(first - low, last - low), slice(first - start, last - start)


def place_kernel(
    capacity, sides_ref, c_ref, h_ref, gates_ref, rows_c_ref, rows_h_ref, *give_refs
):
    half = h_ref.shape[0]
    local_count = rows_h_ref.shape[0]
    row_count = 2 * half * capacity

    def place(side):
        gates = gates_ref[0]
        rank = ranks(gates)
        for group in range(half):
            onehot = onehot_rows(rank, group, local_count, capacity)
            scale = slot_gates(onehot, gates, group, local_count, capacity)
            onehot = onehot.astype(jnp.bfloat16)
            rows_c = (dot(onehot, c_ref[group, 0, 0]) * scale).astype(jnp.bfloat16)
            rows_h = dot(onehot, h_ref[group, 0, 0]).astype(jnp.bfloat16)
            for local in range(local_count):
                own = slice(local * capacity, (local + 1) * capacity)
                here = slice(group * capacity, (group + 1) * capacity)
                rows_c_ref[local, here] = rows_c[own]
                rows_h_ref[local, here] = rows_h[own]
            first = (side * half + group) * capacity
            for base, rows in ((first, rows_c), (row_count + first, rows_h)):
                for send, there, part in overlaps(row_count, base, base + capacity):
                    give_refs[send][there] = rows[part]

    for side in range(2):
        pl.when(pl.program_id(0) == side)(functools.partial(place, side))


def place_rows(tokens, gates, sides, capacity):
    group_count, _, token_count, width = tokens.shape
    local_count = gates.shape[1]
    half = group_count // 2
    row_count = group_count * capacity
    rows_spec = pl.BlockSpec((local_count, row_count // 2, width), lambda i, sides: (0, i, 0))
    give_shapes = [(end - start, width) for start, end in cuts(row_count)]
    block = (half, 1, 1, token_count, width)
    tokens = tokens.reshape(half, 2, 2, token_count, width)
    return pl.pallas_call(
        functools.partial(place_kernel, capacity),
        grid_spec=pltpu.PrefetchScalarGridSpec(
            num_scalar_prefetch=1,
            grid=(2,),
            in_specs=[
                pl.BlockSpec(block, lambda i, sides: (0, sides[i], 0, 0, 0)),
                pl.BlockSpec(block, lambda i, sides: (0, sides[i], 1, 0, 0)),
                pl.BlockSpec((1, half * local_count, token_count), lambda i, sides: (i, 0, 0)),
            ],
            out_specs=[rows_spec, rows_spec]
            + [pl.BlockSpec(shape, lambda i, sides: (0, 0)) for shape in give_shapes],
        ),
        out_shape=[jax.ShapeDtypeStruct((local_count, row_count, width), jnp.bfloat16)] * 2
        + [jax.ShapeDtypeStruct(shape, jnp.bfloat16) for shape in give_shapes],
        compiler_params=params(),
        cost_estimate=light(),
        name="place_rows",
    )(sides, tokens, tokens, gates.reshape(2, half * local_count, token_count))


def combine(gates, rows_ref, capacity, local_count, store):
    rank = ranks(gates)
    for group in range(rows_ref.shape[0]):
        onehot = onehot_rows(rank, group, local_count, capacity).T.astype(jnp.bfloat16)
        store(group, dot(onehot, rows_ref[group]).astype(jnp.bfloat16))


def hidden_gradients(h, c, gu_ref, dn_ref, hidden_ref, d_ref):
    hidden_units = dn_ref.shape[1]
    for start in range(0, hidden_units, tile):
        cols = slice(start, start + tile)
        up_cols = slice(hidden_units + start, hidden_units + start + tile)
        gate_pre = dot(h, gu_ref[0, :, cols])
        up_pre = dot(h, gu_ref[0, :, up_cols])
        back = dot(c, dn_ref[0, cols, :], ((1,), (1,)))
        squash = 1.0 / (1.0 + jnp.exp(-gate_pre))
        activated = gate_pre * squash
        hidden_ref[:, cols] = (activated * up_pre).astype(jnp.bfloat16)
        d_ref[:, cols] = (back * up_pre * squash * (1.0 + gate_pre * (1.0 - squash))).astype(
            jnp.bfloat16
        )
        d_ref[:, up_cols] = (back * activated).astype(jnp.bfloat16)


def backward_kernel(
    capacity, which_ref, h_ref, c_ref, gu_ref, dn_ref, gates_ref,
    own_ref, other_ref, hidden_ref, d_ref, dh_ref,
):
    step = pl.program_id(0)
    hidden_units = dn_ref.shape[1]
    width = dn_ref.shape[2]
    group_count = dh_ref.shape[0]
    local_count = dh_ref.shape[1] // capacity
    token_count = gates_ref.shape[1]
    hidden_gradients(h_ref[0], c_ref[0], gu_ref, dn_ref, hidden_ref, d_ref)
    d = d_ref[...]
    for start in range(0, width, tile):
        cols = slice(start, start + tile)
        dh = dot(d, gu_ref[0, cols, :], ((1,), (1,))).astype(jnp.bfloat16)
        dh = dh.reshape(group_count, capacity, tile)
        dh_ref[:, pl.ds(pl.multiple_of(step * capacity, capacity), capacity), cols] = dh

    @pl.when(step == local_count - 1)
    def _():
        half = group_count // 2

        def store(group, value):
            target = own_ref if group < half else other_ref
            target[group % half] = value

        combine(gates_ref[...], dh_ref, capacity, local_count, store)


def backward_rows(rows_h, rows_c, weight_gu, weight_dn, gates, which, capacity):
    local_count, row_count, width = rows_h.shape
    hidden_units = weight_dn.shape[1]
    group_count = row_count // capacity
    token_count = gates.shape[-1]
    half = (group_count // 2, token_count, width)
    whole = lambda shape: pl.BlockSpec(shape, lambda e, which: (0,) * len(shape))
    rows_spec = pl.BlockSpec((1, row_count, width), lambda e, which: (e, 0, 0))
    return pl.pallas_call(
        functools.partial(backward_kernel, capacity),
        grid_spec=pltpu.PrefetchScalarGridSpec(
            num_scalar_prefetch=1,
            grid=(local_count,),
            in_specs=[
                rows_spec,
                rows_spec,
                pl.BlockSpec((1, width, 2 * hidden_units), lambda e, which: (which[e], 0, 0)),
                pl.BlockSpec((1, hidden_units, width), lambda e, which: (which[e], 0, 0)),
                whole((group_count * local_count, token_count)),
            ],
            out_specs=[
                whole(half),
                whole(half),
                whole((row_count, hidden_units)),
                whole((row_count, 2 * hidden_units)),
            ],
            scratch_shapes=[
                pltpu.VMEM((group_count, local_count * capacity, width), jnp.bfloat16)
            ],
        ),
        out_shape=[
            jax.ShapeDtypeStruct(half, jnp.bfloat16),
            jax.ShapeDtypeStruct(half, jnp.bfloat16),
            jax.ShapeDtypeStruct((row_count, hidden_units), jnp.bfloat16),
            jax.ShapeDtypeStruct((row_count, 2 * hidden_units), jnp.bfloat16),
        ],
        compiler_params=params(),
        cost_estimate=light(),
        name="backward_rows",
    )(which, rows_h, rows_c, weight_gu, weight_dn, gates.reshape(-1, token_count))


def forward_kernel(
    capacity, tokens_ref, gates_ref, gu_ref, dn_ref, out_ref, rows_ref, scale_ref, hidden_ref, o_ref
):
    step = pl.program_id(0)
    hidden_units = dn_ref.shape[1]
    width = dn_ref.shape[2]
    group_count = rows_ref.shape[0]
    local_count = rows_ref.shape[1] // capacity
    row_count = group_count * capacity
    own = pl.ds(pl.multiple_of(step * capacity, capacity), capacity)

    @pl.when(step == 0)
    def _():
        gates = gates_ref[...]
        rank = ranks(gates)
        for group in range(group_count):
            onehot = onehot_rows(rank, group, local_count, capacity)
            rows_ref[group] = dot(onehot.astype(jnp.bfloat16), tokens_ref[group]).astype(
                jnp.bfloat16
            )
            scale_ref[group] = jnp.broadcast_to(
                slot_gates(onehot, gates, group, local_count, capacity), scale_ref.shape[1:]
            )

    h = rows_ref[:, own, :].reshape(row_count, width)
    scale = scale_ref[:, own, :].reshape(row_count, scale_ref.shape[2])[:, :1]
    for start in range(0, hidden_units, tile):
        cols = slice(start, start + tile)
        up_cols = slice(hidden_units + start, hidden_units + start + tile)
        gate_pre = dot(h, gu_ref[0, :, cols])
        up_pre = dot(h, gu_ref[0, :, up_cols])
        hidden_ref[:, cols] = (gate_pre / (1.0 + jnp.exp(-gate_pre)) * up_pre).astype(jnp.bfloat16)
    hidden = hidden_ref[...]
    for start in range(0, width, tile):
        cols = slice(start, start + tile)
        o = (dot(hidden, dn_ref[0, :, cols]) * scale).astype(jnp.bfloat16)
        o_ref[:, own, cols] = o.reshape(group_count, capacity, tile)

    @pl.when(step == local_count - 1)
    def _():
        def store(group, value):
            out_ref[group] = value

        combine(gates_ref[...], o_ref, capacity, local_count, store)


def forward_rows(tokens, gates, weight_gu, weight_dn, capacity):
    group_count, token_count, width = tokens.shape
    local_count, hidden_units = weight_dn.shape[:2]
    whole = lambda shape: pl.BlockSpec(shape, lambda e: (0,) * len(shape))
    placed = (group_count, local_count * capacity, width)
    return pl.pallas_call(
        functools.partial(forward_kernel, capacity),
        grid=(local_count,),
        in_specs=[
            whole((group_count, token_count, width)),
            whole((group_count * local_count, token_count)),
            pl.BlockSpec((1, width, 2 * hidden_units), lambda e: (e, 0, 0)),
            pl.BlockSpec((1, hidden_units, width), lambda e: (e, 0, 0)),
        ],
        out_specs=whole((group_count, token_count, width)),
        out_shape=jax.ShapeDtypeStruct((group_count, token_count, width), jnp.bfloat16),
        scratch_shapes=[
            pltpu.VMEM(placed, jnp.bfloat16),
            pltpu.VMEM(placed[:2] + (128,), jnp.float32),
            pltpu.VMEM((group_count * capacity, hidden_units), jnp.bfloat16),
            pltpu.VMEM(placed, jnp.bfloat16),
        ],
        compiler_params=params(),
        cost_estimate=light(),
        name="forward_rows",
    )(tokens, gates.reshape(-1, token_count), weight_gu, weight_dn)


def gradient_kernel(
    which_ref, h_ref, c_ref, hidden_ref, d_ref, far_1_ref, far_2_ref, far_3_ref, gu_ref, dn_ref,
    out_gu_ref, out_dn_ref, far_c_ref, far_h_ref, far_hidden_ref, far_d_ref,
):
    step = pl.program_id(0)
    row_count = far_c_ref.shape[0]

    @pl.when(step == 0)
    def _():
        for target, base in ((far_c_ref, 0), (far_h_ref, row_count)):
            for send, there, part in overlaps(row_count, base, base + row_count):
                target[part] = (far_1_ref, far_2_ref, far_3_ref)[send][there]
        hidden_gradients(
            far_h_ref[...], far_c_ref[...], gu_ref, dn_ref, far_hidden_ref, far_d_ref
        )

    def columns(size):
        return pl.ds(pl.multiple_of(step * size, size), size)

    first = ((0,), (0,))
    cols = columns(out_gu_ref.shape[0])
    out_gu_ref[...] = (
        dot(h_ref[0, :, cols], d_ref[...], first)
        + dot(far_h_ref[:, cols], far_d_ref[...], first)
    ).astype(jnp.bfloat16)
    cols = columns(out_dn_ref.shape[0])
    out_dn_ref[...] = (
        dot(hidden_ref[:, cols], c_ref[0], first)
        + dot(far_hidden_ref[:, cols], far_c_ref[...], first)
    ).astype(jnp.bfloat16)


def weight_gradients(which, rows_h, rows_c, hidden, d, far, weight_gu, weight_dn):
    _, row_count, width = rows_h.shape
    hidden_units = weight_dn.shape[1]
    steps = width // tile
    whole = lambda shape: pl.BlockSpec(shape, lambda i, which: (0,) * len(shape))
    kept = lambda shape: pl.BlockSpec((1,) + shape, lambda i, which: (which[1], 0, 0))
    rows_spec = pl.BlockSpec((1, row_count, width), lambda i, which: (1, 0, 0))
    return pl.pallas_call(
        gradient_kernel,
        grid_spec=pltpu.PrefetchScalarGridSpec(
            num_scalar_prefetch=1,
            grid=(steps,),
            in_specs=[
                rows_spec,
                rows_spec,
                whole((row_count, hidden_units)),
                whole((row_count, 2 * hidden_units)),
                *[whole(part.shape) for part in far],
                kept((width, 2 * hidden_units)),
                kept((hidden_units, width)),
            ],
            out_specs=[
                pl.BlockSpec((width // steps, 2 * hidden_units), lambda i, which: (i, 0)),
                pl.BlockSpec((hidden_units // steps, width), lambda i, which: (i, 0)),
            ],
            scratch_shapes=[
                pltpu.VMEM((row_count, width), jnp.bfloat16),
                pltpu.VMEM((row_count, width), jnp.bfloat16),
                pltpu.VMEM((row_count, hidden_units), jnp.bfloat16),
                pltpu.VMEM((row_count, 2 * hidden_units), jnp.bfloat16),
            ],
        ),
        out_shape=[
            jax.ShapeDtypeStruct((width, 2 * hidden_units), jnp.bfloat16),
            jax.ShapeDtypeStruct((hidden_units, width), jnp.bfloat16),
        ],
        compiler_params=params(),
        cost_estimate=light(),
        name="weight_gradients",
    )(which, rows_h, rows_c, hidden, d, *far, weight_gu, weight_dn)


def swap_cores(value):
    return lax.ppermute(value, "expert", [(i, i ^ 1) for i in range(lax.axis_size("expert"))])


def exchange_sums(chip):
    group_count = lax.axis_size("expert")
    lines = [list(range(c, group_count, 2)) for c in range(2)]
    return lax.all_to_all(
        chip, "expert", split_axis=0, concat_axis=0, tiled=True, axis_index_groups=lines
    )


def per_device(
    x_fwd, gate_fwd, route_fwd, x_bwd, gate_bwd, route_bwd, cotangent, norm_gain, w_gate_up, w_down
):
    group_count = lax.axis_size("expert")
    section_count = lax.axis_size("pipe")
    local_count = w_gate_up.shape[1]
    expert_count = local_count * group_count
    token_count, model_width = x_fwd.shape
    pick_count = route_fwd.shape[1]
    capacity = token_count * pick_count * 4 // (3 * expert_count)
    weight_gu = w_gate_up[0]
    weight_dn = w_down[0]

    upper_half = (lax.axis_index("pipe") >= section_count // 2).astype(jnp.int32)
    which = jnp.stack([1 - upper_half, upper_half])
    core = lax.axis_index("expert") % 2
    chips = 2 * jnp.arange(group_count // 2, dtype=jnp.int32)
    order = jnp.concatenate([chips + core, chips + 1 - core])
    sides = jnp.stack([core, 1 - core])

    bwd_hat, bwd_scale = normalize(x_bwd)
    bwd_normed = (bwd_hat * norm_gain).astype(jnp.bfloat16)
    fwd_normed = (normalize(x_fwd)[0] * norm_gain).astype(jnp.bfloat16)
    send_gates = jnp.stack(
        [
            expert_gates(gate_fwd, route_fwd, expert_count),
            expert_gates(gate_bwd, route_bwd, expert_count),
        ]
    ).reshape(2, group_count, local_count, token_count)
    recv_gates = lax.all_to_all(
        send_gates.transpose(1, 0, 2, 3), "expert", split_axis=0, concat_axis=0, tiled=True
    )
    gates_f = recv_gates[:, 0]
    gates_b = recv_gates[:, 1][order][:, which]
    gathered_bwd = lax.all_gather(
        jnp.stack([cotangent, bwd_normed])[None], "expert", axis=0, tiled=True
    )
    gathered_fwd = lax.all_gather(fwd_normed[None], "expert", axis=0, tiled=True)

    mirror = [(i, section_count - 1 - i) for i in range(section_count)]
    rows_c, rows_h, *give = place_rows(gathered_bwd, gates_b, sides, capacity)
    far = [lax.ppermute(part, "pipe", mirror) for part in give]

    own_dh, other_dh, keep_hidden, keep_d = backward_rows(
        rows_h, rows_c, weight_gu, weight_dn, gates_b, which, capacity
    )
    other_dh, far[0] = lax.optimization_barrier((other_dh, far[0]))
    other_dh = swap_cores(other_dh)
    middle = token_count // 2
    chip_dh = [
        (own_dh[:, part].astype(jnp.float32) + other_dh[:, part].astype(jnp.float32)).astype(
            jnp.bfloat16
        )
        for part in (slice(0, middle), slice(middle, token_count))
    ]
    chip_dh, gathered_fwd = lax.optimization_barrier((chip_dh, gathered_fwd))
    parts_dh = [exchange_sums(chip) for chip in chip_dh]

    partial_y = forward_rows(gathered_fwd, gates_f, weight_gu, weight_dn, capacity)
    partial_y, parts_dh[0], far[1] = lax.optimization_barrier((partial_y, parts_dh[0], far[1]))
    y_fwd = lax.psum_scatter(
        partial_y.reshape(group_count * token_count, model_width),
        "expert",
        scatter_dimension=0,
        tiled=True,
    )

    out_gu, out_dn = weight_gradients(
        which, rows_h, rows_c, keep_hidden, keep_d, far, weight_gu, weight_dn
    )

    dh_sum = jnp.concatenate([jnp.sum(part.astype(jnp.float32), axis=0) for part in parts_dh])
    scaled_dh = norm_gain * dh_sum
    dx_bwd = (
        bwd_scale * (scaled_dh - bwd_hat * jnp.mean(bwd_hat * scaled_dh, axis=-1, keepdims=True))
    ).astype(jnp.bfloat16)
    return (y_fwd, dx_bwd, out_gu[None, None], out_dn[None, None])


def solution(mesh):
    rows = P(("pipe", "expert"), None)
    experts = P("pipe", "expert", None, None)
    return jax.shard_map(
        per_device,
        mesh=mesh,
        in_specs=(rows,) * 7 + (P(), experts, experts),
        out_specs=(rows, rows, experts, experts),
        check_vma=False,
    )
```

time: 304 us -> 214 us (0.70)
  waiting for transfers between devices: 187 us -> 95.5 us
  matrix products: 65.7 us -> 0 us
  Pallas kernels: 0 us -> 64.6 us
  starting transfers between devices: 4.15 us -> 22.2 us
  blocking collectives: 9.32 us -> 0 us
    dot_general x14 -> x0, matrix products: 65.7 us -> none  [the longest x3 17.3 us: hidden_parts(): jnp.einsum('erd,edf->erf', inputs, weight_gu, preferred_element_type=jnp....]
    pallas_call x0 -> x4, Pallas kernels: none -> 64.6 us  [the longest x1 21.8 us: backward_rows(): pl.pallas_call(functools.partial(backward_kernel, capacity), grid_spec=pl...]
    reduce_scatter x1 -> x0, waiting for transfers between devices: 36.8 us -> none  [per_device(): lax.psum_scatter(partial_dh.reshape(group_count * token_count, model_widt...]
    all_gather x1, waiting for transfers between devices: 36.6 us -> 1.29 us  [per_device(): lax.all_gather(fwd_normed[None], 'expert', axis=0, tiled=True)]
    ppermute x2 -> x4, waiting for transfers between devices: 61.2 us -> 29.5 us  [the longest x3 26.3 us: per_device(): far = [lax.ppermute(part, 'pipe', mirror) for part in give]]
    all_to_all x0 -> x3, starting transfers between devices: none -> 15 us  [the longest x2 9.35 us: exchange_sums(): lax.all_to_all(chip, 'expert', split_axis=0, concat_axis=0, tiled=True, a...]
    reduce_scatter x1, waiting for transfers between devices: 0.01 us -> 9.96 us  [per_device(): lax.psum_scatter(partial_y.reshape(group_count * token_count, model_width...]
    all_to_all x1 -> x0, blocking collectives: 9.32 us -> none  [per_device(): lax.all_to_all(send_gates.transpose(1, 0, 2, 3), 'expert', split_axis=0,...]
  transfers between devices with their start and end apart: 6 -> 10, of which waited for: 5 -> 7; matrix products, arithmetic and copies ran while one was open for 9% -> 4% of each run, Pallas kernels for 0% -> 30%
where the time goes in v2:
time: 214 us; the launch traced here: 213 us
  waiting for transfers between devices  95.5 us (45%)
  Pallas kernels  64.6 us (30%)
  starting transfers between devices  22.2 us (10%)
  between operations  13.9 us (6%)
  other arithmetic  12.1 us (6%)
  local copies, waits for them, and re-layouts  5.06 us (2%)
    all_gather x1, waiting for transfers between devices, per_device(): lax.all_gather(jnp.stack([cotangent, bwd_normed])[None], 'expert', axis=0...  51 us
    ppermute x3, waiting for transfers between devices, per_device(): far = [lax.ppermute(part, 'pipe', mirror) for part in give]  26.3 us
    pallas_call x1, Pallas kernels, backward_rows(): pl.pallas_call(functools.partial(backward_kernel, capacity), grid_spec=pl...  21.8 us
    pallas_call x1, Pallas kernels, weight_gradients(): pl.pallas_call(gradient_kernel, grid_spec=pltpu.PrefetchScalarGridSpec(nu...  19.7 us
    pallas_call x1, Pallas kernels, forward_rows(): pl.pallas_call(functools.partial(forward_kernel, capacity), grid=(local_c...  15.7 us
    reduce_scatter x1, waiting for transfers between devices, per_device(): lax.psum_scatter(partial_y.reshape(group_count * token_count, model_width...  9.96 us
    all_to_all x2, starting transfers between devices, exchange_sums(): lax.all_to_all(chip, 'expert', split_axis=0, concat_axis=0, tiled=True, a...  9.35 us
    pallas_call x1, Pallas kernels, place_rows(): pl.pallas_call(functools.partial(place_kernel, capacity), grid_spec=pltpu...  7.46 us
  transfers between devices with their start and end apart: 10, of which 7 were waited for; matrix products, arithmetic and copies ran while one was open for 4% of the time, Pallas kernels for 30%

profile of v2, /device:TPU:9, one launch (start us, length us, event | category | flops | bytes accessed | tf_op | source)
XLA Modules:
  0.0 213.2 jit_solution(14560768616113512909)
XLA Ops:
  7.2 0.0 copy-start.4
  7.2 0.0 all-gather.5.cloned.1.call-start
  7.2 1.2 fusion.9
  8.4 1.2 fusion.8
  9.6 2.0 fusion.11
  11.6 0.0 copy-start.6
  11.6 0.0 copy-start.7
  11.6 0.0 copy-start.8
  11.6 0.0 copy-start.9
  11.6 0.0 copy-done.4
  11.7 0.9 pad_maximum_fusion
  12.6 0.0 all-gather.5.cloned.1.call-update
  12.6 0.0 all-gather.7.cloned.1.call-start
  12.7 0.7 all-gather.7.cloned.1.call-update
  13.4 0.0 copy-done.6
  13.4 0.0 copy-done.7
  13.4 0.0 copy-done.8
  13.4 0.0 copy-done.9
  13.5 0.6 maximum_bitcast_fusion
  14.1 5.6 %all-to-all-start = ((f32[8,2,2,128]{3,2,1,0:T(2,128)}), f32[8,2,2,128]{3,2,1,0:T(2,128)S(1)}, u32[]{:S(2)}, u32[]{:S(2)}) async-start(f32[8,2,2,128]{3,2,1,0:T(2,128)} %maximum_bitcast_fusion), calls=%async_computation | async-start | bytes 32768 | tf_op jit(solution)/shard_map/all_to_all | solution.py:427
  19.7 0.1 fusion.13
  19.8 0.1 fusion.14
  19.9 0.7 pad_add_fusion.1.sides_ref
  20.5 3.1 %all-to-all-done = f32[8,2,2,128]{3,2,1,0:T(2,128)S(1)} async-done(((f32[8,2,2,128]{3,2,1,0:T(2,128)}), f32[8,2,2,128]{3,2,1,0:T(2,128)S(1)}, u32[]{:S(2)}, u32[]{:S(2)}) %all-to-all-start) | async-done | bytes 16416 | tf_op jit(solution)/shard_map/all_to_all | solution.py:427
  23.6 0.6 fusion.15
  24.2 0.6 gather_fusion
  24.8 0.5 gather_fusion.1
  25.3 0.6 copy.43
  25.9 51.0 %all-gather.5.cloned.1.call-done = bf16[16,128,1536]{2,1,0:T(8,128)(2,1)} async-done(((bf16[2,128,1536]{2,1,0:T(8,128)(2,1)}), bf16[16,128,1536]{2,1,0:T(8,128)(2,1)}) %all-gather.5.cloned.1.call-update) | async-done | bytes 6291472 | tf_op jit(solution)/shard_map/all_gather | solution.py:432
  76.9 7.5 %place_rows.1 = (bf16[2,512,1536]{2,1,0:T(8,128)(2,1)}, bf16[2,512,1536]{2,1,0:T(8,128)(2,1)}, bf16[320,1536]{1,0:T(8,128)(2,1)}, bf16[352,1536]{1,0:T(8,128)(2,1)}, bf16[352,1536]{1,0:T(8,128)(2,1)}) custom-call(s32[2]{0:T(128)} %pad_add_fusion.1.sides_ref, bf16[4,2,2,128,1536]{4,3,2,1,0:T(8,128)(2,1)} %bitcast.46, bf16[4,2,2,128,1536]{4,3,2,1,0:T(8,128)(2,1)} %bitcast.47, ...), custom_call_target="tpu_custom_call" | custom-call | flops 1000 | bytes 1000 | tf_op jit(solution)/shard_map/place_rows/pallas_call | solution.py:122
  84.4 2.2 %collective-permute-start = (bf16[320,1536]{1,0:T(8,128)(2,1)}, bf16[320,1536]{1,0:T(8,128)(2,1)S(1)}, u32[]{:S(2)}, u32[]{:S(2)}) collective-permute-start(bf16[320,1536]{1,0:T(8,128)(2,1)} %get-tuple-element.27), channel_id=1, source_target_pairs={{0,24},{8,16},{16,8},{24,0},{1,25},{9,17},{17,9},{25,1},{2,26},{10... | collective-permute-start | bytes 2949128 | tf_op jit(solution)/shard_map/ppermute | solution.py:439
  86.6 0.7 pad_add_fusion.which_ref
  87.2 21.8 %backward_rows.1 = (bf16[4,128,1536]{2,1,0:T(8,128)(2,1)}, bf16[4,128,1536]{2,1,0:T(8,128)(2,1)}, bf16[512,768]{1,0:T(8,128)(2,1)}, bf16[512,1536]{1,0:T(8,128)(2,1)}) custom-call(s32[2]{0:T(128)} %pad_add_fusion.which_ref, bf16[2,512,1536]{2,1,0:T(8,128)(2,1)} %get-tuple-element.23.h_ref, bf16[2,512,1536]{2,1,0:T(8,128)(2,1)} %get-tuple-element.24.c_ref, ...), custom_call_target="tpu_custom_call" | custom-call | flops 1000 | bytes 1000 | tf_op jit(solution)/shard_map/backward_rows/pallas_call | solution.py:204
  109.0 0.0 collective-permute-done.far_1_ref
  109.0 0.0 copy-start.3
  109.0 0.7 collective-permute-start.1
  109.7 3.2 %collective-permute-done.1 = bf16[4,128,1536]{2,1,0:T(8,128)(2,1)S(1)} collective-permute-done((bf16[4,128,1536]{2,1,0:T(8,128)(2,1)}, bf16[4,128,1536]{2,1,0:T(8,128)(2,1)S(1)}, u32[]{:S(2)}, u32[]{:S(2)}) %collective-permute-start.1) | collective-permute-done | bytes 1572896 | tf_op jit(solution)/shard_map/ppermute | solution.py:387
  113.0 0.0 copy-done.3
  113.0 3.1 %add_convert_fusion = (bf16[4,64,1536]{2,1,0:T(8,128)(2,1)}, bf16[4,64,1536]{2,1,0:T(8,128)(2,1)}) fusion(bf16[4,128,1536]{2,1,0:T(8,128)(2,1)S(1)} %collective-permute-done.1, bf16[4,128,1536]{2,1,0:T(8,128)(2,1)} %get-tuple-element.25), kind=kLoop, calls=%fused_computation.4 | loop fusion | flops 3145728 | bytes 4718592 | tf_op jit(solution)/shard_map/convert_element_type | solution.py:448
  116.0 0.0 copy-start.10
  116.0 1.3 all-gather.7.cloned.1.call-done
  117.3 4.8 %all-to-all-start.1 = ((bf16[4,64,1536]{2,1,0:T(8,128)(2,1)}), bf16[4,64,1536]{2,1,0:T(8,128)(2,1)S(1)}, u32[]{:S(2)}, u32[]{:S(2)}) async-start(bf16[4,64,1536]{2,1,0:T(8,128)(2,1)} %get-tuple-element.30), calls=%async_computation.1 | async-start | bytes 1572864 | tf_op jit(solution)/shard_map/all_to_all | solution.py:393
  122.1 0.0 reduce-scatter.2.cloned.1.call-start
  122.1 0.0 copy-done.10
  122.1 2.1 collective-permute-start.2
  124.2 15.7 %forward_rows.1 = bf16[8,128,1536]{2,1,0:T(8,128)(2,1)} custom-call(bf16[8,128,1536]{2,1,0:T(8,128)(2,1)} %bitcast.49, f32[16,128]{1,0:T(8,128)} %bitcast.53, bf16[2,1536,1536]{2,1,0:T(8,128)(2,1)} %bitcast.41, bf16[2,768,1536]{2,1,0:T(8,128)(2,1)} %bitcast.44), custom_call_target="tpu_custom_call" | custom-call | flops 1000 | bytes 1000 | tf_op jit(solution)/shard_map/forward_rows/pallas_call | solution.py:289
  139.9 7.9 %collective-permute-done.2.far_2_ref = bf16[352,1536]{1,0:T(8,128)(2,1)S(1)} collective-permute-done((bf16[352,1536]{1,0:T(8,128)(2,1)S(1)}, bf16[352,1536]{1,0:T(8,128)(2,1)S(1)}, u32[]{:S(2)}, u32[]{:S(2)}) %collective-permute-start.2) | collective-permute-done | bytes 1081376 | tf_op jit(solution)/shard_map/ppermute | solution.py:439
  147.8 0.0 copy-start.1
  147.8 0.0 all-to-all-done.1
  147.8 0.0 reduce-scatter.2.cloned.1.call-update
  147.9 1.0 copy-done.1
  148.8 2.1 collective-permute-start.3
  150.9 4.5 %all-to-all-start.2 = ((bf16[4,64,1536]{2,1,0:T(8,128)(2,1)}), bf16[4,64,1536]{2,1,0:T(8,128)(2,1)S(1)}, u32[]{:S(2)}, u32[]{:S(2)}) async-start(bf16[4,64,1536]{2,1,0:T(8,128)(2,1)} %get-tuple-element.34), calls=%async_computation.3 | async-start | bytes 1572864 | tf_op jit(solution)/shard_map/all_to_all | solution.py:393
  155.5 18.3 %collective-permute-done.3.far_3_ref = bf16[352,1536]{1,0:T(8,128)(2,1)S(1)} collective-permute-done((bf16[352,1536]{1,0:T(8,128)(2,1)}, bf16[352,1536]{1,0:T(8,128)(2,1)S(1)}, u32[]{:S(2)}, u32[]{:S(2)}) %collective-permute-start.3) | collective-permute-done | bytes 1081376 | tf_op jit(solution)/shard_map/ppermute | solution.py:439
  173.8 1.0 copy-done.2
  174.8 19.7 %weight_gradients.1 = (bf16[1536,1536]{1,0:T(8,128)(2,1)}, bf16[768,1536]{1,0:T(8,128)(2,1)}) custom-call(s32[2]{0:T(128)} %pad_add_fusion.which_ref, bf16[2,512,1536]{2,1,0:T(8,128)(2,1)} %get-tuple-element.23.h_ref, bf16[2,512,1536]{2,1,0:T(8,128)(2,1)} %get-tuple-element.24.c_ref, bf16[512,768]{1,0:T(8,128)(2,1)} %get-tuple-element.35.hidden_ref, ...), custom_call_target="tpu_custom_call" | custom-call | flops 1000 | bytes 1000 | tf_op jit(solution)/shard_map/weight_gradients/pallas_call | solution.py:351
  194.5 0.1 convert_reduce_fusion.1
  194.6 0.0 all-to-all-done.2
  194.6 0.1 convert_reduce_fusion
  194.7 0.7 copy-done
  195.5 0.0 copy-done.5
  195.5 0.3 fusion.4
  195.7 1.0 fusion.7
  196.8 10.0 %reduce-scatter.2.cloned.1.call-done = bf16[128,1536]{1,0:T(8,128)(2,1)} async-done(((bf16[1024,1536]{1,0:T(8,128)(2,1)}), bf16[128,1536]{1,0:T(8,128)(2,1)}) %reduce-scatter.2.cloned.1.call-update) | async-done | bytes 393232 | tf_op jit(solution)/shard_map/reduce_scatter | solution.py:458
  (11 shorter events, 0.1 us)
Async XLA Ops:
  7.2 4.5 %copy-start.4 = (bf16[128,1536]{1,0:T(8,128)(2,1)S(1)}, bf16[128,1536]{1,0:T(8,128)(2,1)}, u32[]{:S(2)}) copy-start(bf16[128,1536]{1,0:T(8,128)(2,1)} %param.16) | copy-start | bytes 1179652
  7.2 69.7 %all-gather.5.cloned.1.call-start = ((), (), s32[]{:S(2)}) async-start(), calls=%async_computation.5 | async-start | bytes 7077888 | tf_op jit(solution)/shard_map/all_gather | solution.py:432
  11.6 1.8 copy-start.6
  11.6 1.8 copy-start.7
  11.6 1.8 copy-start.8
  11.6 1.8 copy-start.9
  12.6 104.7 %all-gather.7.cloned.1.call-start = ((), (), s32[]{:S(2)}) async-start(), calls=%async_computation.6 | async-start | bytes 3538944 | tf_op jit(solution)/shard_map/all_gather | solution.py:435
  14.1 9.5 %all-to-all-start = ((f32[8,2,2,128]{3,2,1,0:T(2,128)}), f32[8,2,2,128]{3,2,1,0:T(2,128)S(1)}, u32[]{:S(2)}, u32[]{:S(2)}) async-start(f32[8,2,2,128]{3,2,1,0:T(2,128)} %maximum_bitcast_fusion), calls=%async_computation | async-start | bytes 32768 | tf_op jit(solution)/shard_map/all_to_all | solution.py:427
  84.4 24.7 %collective-permute-start = (bf16[320,1536]{1,0:T(8,128)(2,1)}, bf16[320,1536]{1,0:T(8,128)(2,1)S(1)}, u32[]{:S(2)}, u32[]{:S(2)}) collective-permute-start(bf16[320,1536]{1,0:T(8,128)(2,1)} %get-tuple-element.27), channel_id=1, source_target_pairs={{0,24},{8,16},{16,8},{24,0},{1,25},{9,17},{17,9},{25,1},{2,26},{10... | collective-permute-start | bytes 2949128 | tf_op jit(solution)/shard_map/ppermute | solution.py:439
  109.0 3.9 %copy-start.3 = (bf16[320,1536]{1,0:T(8,128)(2,1)}, bf16[320,1536]{1,0:T(8,128)(2,1)S(1)}, u32[]{:S(2)}) copy-start(bf16[320,1536]{1,0:T(8,128)(2,1)S(1)} %collective-permute-done.far_1_ref) | copy-start | bytes 2949124
  109.0 3.9 %collective-permute-start.1 = (bf16[4,128,1536]{2,1,0:T(8,128)(2,1)}, bf16[4,128,1536]{2,1,0:T(8,128)(2,1)S(1)}, u32[]{:S(2)}, u32[]{:S(2)}) collective-permute-start(bf16[4,128,1536]{2,1,0:T(8,128)(2,1)} %get-tuple-element.28), channel_id=1, source_target_pairs={{0,1},{1,0},{2,3},{3,2},{4,5},{5,4},{6,7},{7,6},{8,9},{9,8},{10,11... | collective-permute-start | bytes 4718600 | tf_op jit(solution)/shard_map/ppermute | solution.py:387
  116.0 6.1 %copy-start.10 = (bf16[352,1536]{1,0:T(8,128)(2,1)S(1)}, bf16[352,1536]{1,0:T(8,128)(2,1)}, u32[]{:S(2)}) copy-start(bf16[352,1536]{1,0:T(8,128)(2,1)} %get-tuple-element.31) | copy-start | bytes 3244036
  117.3 30.5 %all-to-all-start.1 = ((bf16[4,64,1536]{2,1,0:T(8,128)(2,1)}), bf16[4,64,1536]{2,1,0:T(8,128)(2,1)S(1)}, u32[]{:S(2)}, u32[]{:S(2)}) async-start(bf16[4,64,1536]{2,1,0:T(8,128)(2,1)} %get-tuple-element.30), calls=%async_computation.1 | async-start | bytes 1572864 | tf_op jit(solution)/shard_map/all_to_all | solution.py:393
  122.1 84.6 %reduce-scatter.2.cloned.1.call-start = ((), (), s32[]{:S(2)}) async-start(), calls=%async_computation.4 | async-start | bytes 3538944 | tf_op jit(solution)/shard_map/reduce_scatter | solution.py:458
  122.1 25.7 %collective-permute-start.2 = (bf16[352,1536]{1,0:T(8,128)(2,1)S(1)}, bf16[352,1536]{1,0:T(8,128)(2,1)S(1)}, u32[]{:S(2)}, u32[]{:S(2)}) collective-permute-start(bf16[352,1536]{1,0:T(8,128)(2,1)S(1)} %copy-done.10), channel_id=1, source_target_pairs={{0,24},{8,16},{16,8},{24,0},{1,25},{9,17},{17,9},{25,1},{2,26},{10... | collective-permute-start | bytes 3244040 | tf_op jit(solution)/shard_map/ppermute | solution.py:439
  147.8 1.0 copy-start.1
  148.8 25.0 %collective-permute-start.3 = (bf16[352,1536]{1,0:T(8,128)(2,1)}, bf16[352,1536]{1,0:T(8,128)(2,1)S(1)}, u32[]{:S(2)}, u32[]{:S(2)}) collective-permute-start(bf16[352,1536]{1,0:T(8,128)(2,1)} %get-tuple-element.39), channel_id=1, source_target_pairs={{0,24},{8,16},{16,8},{24,0},{1,25},{9,17},{17,9},{25,1},{2,26},{10... | collective-permute-start | bytes 3244040 | tf_op jit(solution)/shard_map/ppermute | solution.py:439
  150.9 43.7 %all-to-all-start.2 = ((bf16[4,64,1536]{2,1,0:T(8,128)(2,1)}), bf16[4,64,1536]{2,1,0:T(8,128)(2,1)S(1)}, u32[]{:S(2)}, u32[]{:S(2)}) async-start(bf16[4,64,1536]{2,1,0:T(8,128)(2,1)} %get-tuple-element.34), calls=%async_computation.3 | async-start | bytes 1572864 | tf_op jit(solution)/shard_map/all_to_all | solution.py:393
  173.8 1.0 copy-start.2
  194.5 1.0 copy-start
  194.5 1.0 copy-start.5
Sparse Core Ops, SparseCore 0:
  12.7 64.1 all-gather.4
  79.1 38.1 all-gather.6
  148.0 58.6 reduce-scatter.1

commit v3 on v2

v3 whole, which is shorter than its diff:
```python
import functools

import jax
import jax.numpy as jnp
from jax import lax
from jax.experimental import pallas as pl
from jax.experimental.pallas import tpu as pltpu
from jax.sharding import PartitionSpec as P

norm_eps = 1e-06
tile = 256
vmem_bytes = 56 * 1024 * 1024


def params():
    return pltpu.CompilerParams(
        dimension_semantics=("arbitrary",), vmem_limit_bytes=vmem_bytes
    )


def light():
    return pl.CostEstimate(flops=1000, bytes_accessed=1000, transcendentals=0)


def dot(a, b, contract=((1,), (0,))):
    return lax.dot_general(a, b, (contract, ((), ())), preferred_element_type=jnp.float32)


def normalize(inputs):
    values = inputs.astype(jnp.float32)
    scale = lax.rsqrt(jnp.mean(values * values, axis=-1, keepdims=True) + norm_eps)
    return (values * scale, scale)


def norm_kernel(x_ref, gain_ref, *refs):
    out_ref = refs[-1]
    values = x_ref[...].astype(jnp.float32)
    scale = lax.rsqrt(jnp.mean(values * values, axis=-1, keepdims=True) + norm_eps)
    out_ref[len(refs) - 1] = (values * scale * gain_ref[...][None, :]).astype(jnp.bfloat16)
    for index, other_ref in enumerate(refs[:-1]):
        out_ref[index] = other_ref[...]


def normed(x, gain, *others):
    return pl.pallas_call(
        norm_kernel,
        out_shape=jax.ShapeDtypeStruct((1 + len(others),) + x.shape, jnp.bfloat16),
        cost_estimate=light(),
        name="normed",
    )(x, gain, *others)


def expert_gates(gates, routes, expert_count):
    chosen = routes[None, :, :] == jnp.arange(expert_count, dtype=jnp.int32)[:, None, None]
    return jnp.sum(jnp.where(chosen, gates[None], 0.0), axis=-1)


def ranks(gates):
    named = gates > 0.0
    token_count = gates.shape[1]
    upto = lax.broadcasted_iota(jnp.int32, (token_count, token_count), 0) <= (
        lax.broadcasted_iota(jnp.int32, (token_count, token_count), 1)
    )
    count = dot(
        jnp.where(named, 1.0, 0.0).astype(jnp.bfloat16), jnp.where(upto, 1.0, 0.0).astype(jnp.bfloat16)
    )
    return jnp.where(named, count - 1.0, -1.0)


def onehot_rows(rank, group, local_count, capacity):
    token_count = rank.shape[1]
    slots = lax.broadcasted_iota(jnp.int32, (capacity, token_count), 0).astype(jnp.float32)
    parts = []
    for local in range(local_count):
        row = group * local_count + local
        parts.append(jnp.where(rank[row : row + 1, :] == slots, 1.0, 0.0))
    return jnp.concatenate(parts, axis=0)


def slot_gates(onehot, gates, group, local_count, capacity):
    parts = []
    for local in range(local_count):
        row = group * local_count + local
        own = onehot[local * capacity : (local + 1) * capacity]
        parts.append(jnp.sum(own * gates[row : row + 1, :], axis=1, keepdims=True))
    return jnp.concatenate(parts, axis=0)


def cuts(row_count):
    ends = [0, row_count * 5 // 8, row_count * 35 // 32, row_count * 2]
    return [(start, end) for start, end in zip(ends[:-1], ends[1:])]


def overlaps(row_count, start, end):
    for send, (low, high) in enumerate(cuts(row_count)):
        first, last = max(start, low), min(end, high)
        if first < last:
            yield send, slice(first - low, last - low), slice(first - start, last - start)


def place_kernel(
    capacity, sides_ref, c_ref, h_ref, gates_ref, keep_c_ref, keep_h_ref, *give_refs
):
    half = h_ref.shape[0]
    row_count = 2 * half * capacity

    def place(side):
        gates = gates_ref[0]
        rank = ranks(gates)
        for group in range(half):
            onehot = onehot_rows(rank, group, 2, capacity)
            scale = slot_gates(onehot, gates, group, 2, capacity)
            onehot = onehot.astype(jnp.bfloat16)
            rows_c = (dot(onehot, c_ref[group, 0, 0]) * scale).astype(jnp.bfloat16)
            rows_h = dot(onehot, h_ref[group, 0, 0]).astype(jnp.bfloat16)
            here = slice(group * capacity, (group + 1) * capacity)
            keep_c_ref[here] = rows_c[:capacity]
            keep_h_ref[here] = rows_h[:capacity]
            first = (side * half + group) * capacity
            for base, rows in ((first, rows_c), (row_count + first, rows_h)):
                for send, there, part in overlaps(row_count, base, base + capacity):
                    give_refs[send][there] = rows[capacity:][part]

    for side in range(2):
        pl.when(pl.program_id(0) == side)(functools.partial(place, side))


def place_rows(tokens, gates, sides, capacity):
    group_count, _, token_count, width = tokens.shape
    half = group_count // 2
    row_count = group_count * capacity
    rows_spec = pl.BlockSpec((row_count // 2, width), lambda i, sides: (i, 0))
    give_shapes = [(end - start, width) for start, end in cuts(row_count)]
    block = (half, 1, 1, token_count, width)
    tokens = tokens.reshape(half, 2, 2, token_count, width)
    return pl.pallas_call(
        functools.partial(place_kernel, capacity),
        grid_spec=pltpu.PrefetchScalarGridSpec(
            num_scalar_prefetch=1,
            grid=(2,),
            in_specs=[
                pl.BlockSpec(block, lambda i, sides: (0, sides[i], 0, 0, 0)),
                pl.BlockSpec(block, lambda i, sides: (0, sides[i], 1, 0, 0)),
                pl.BlockSpec((1, half * 2, token_count), lambda i, sides: (i, 0, 0)),
            ],
            out_specs=[rows_spec, rows_spec]
            + [pl.BlockSpec(shape, lambda i, sides: (0, 0)) for shape in give_shapes],
        ),
        out_shape=[jax.ShapeDtypeStruct((row_count, width), jnp.bfloat16)] * 2
        + [jax.ShapeDtypeStruct(shape, jnp.bfloat16) for shape in give_shapes],
        compiler_params=params(),
        cost_estimate=light(),
        name="place_rows",
    )(sides, tokens, tokens, gates.reshape(2, half * 2, token_count))


class Copies:
    def __init__(self, sems):
        self.sems = sems
        self.count = 0
        self.waiting = {}

    def start(self, name, source, target):
        copy = pltpu.make_async_copy(source, target, self.sems.at[self.count])
        self.count += 1
        copy.start()
        self.waiting.setdefault(name, []).append(copy)

    def wait(self, name):
        for copy in self.waiting.pop(name, []):
            copy.wait()

    def wait_all(self):
        for name in list(self.waiting):
            self.wait(name)


def weight_copies(copies, expert, source, gu_ref, dn_ref, gu, dn):
    hidden_units = dn.shape[1]
    for start in range(0, hidden_units, tile):
        for base in (0, hidden_units):
            cols = slice(base + start, base + start + tile)
            copies.start(("gu", expert, start), gu_ref.at[source, :, cols], gu.at[expert, :, cols])
        rows = slice(start, start + tile)
        copies.start(("dn", expert, start), dn_ref.at[source, rows], dn.at[expert, rows])


def hidden_gradients(copies, expert, h, c, gu, dn, hidden_ref, d_ref):
    hidden_units = dn.shape[1]
    for start in range(0, hidden_units, tile):
        cols = slice(start, start + tile)
        up_cols = slice(hidden_units + start, hidden_units + start + tile)
        copies.wait(("gu", expert, start))
        gate_pre = dot(h(), gu[expert, :, cols])
        up_pre = dot(h(), gu[expert, :, up_cols])
        copies.wait(("dn", expert, start))
        back = dot(c(), dn[expert, cols, :], ((1,), (1,)))
        squash = 1.0 / (1.0 + jnp.exp(-gate_pre))
        activated = gate_pre * squash
        if hidden_ref is not None:
            hidden_ref[:, cols] = (activated * up_pre).astype(jnp.bfloat16)
        d_ref[:, cols] = (back * up_pre * squash * (1.0 + gate_pre * (1.0 - squash))).astype(
            jnp.bfloat16
        )
        d_ref[:, up_cols] = (back * activated).astype(jnp.bfloat16)


anywhere = pl.BlockSpec(memory_space=pl.ANY)
vector = pl.BlockSpec(memory_space=pltpu.VMEM)
scalar = pl.BlockSpec(memory_space=pltpu.SMEM)


def kernel_params():
    return pltpu.CompilerParams(vmem_limit_bytes=vmem_bytes)


def combine(gates, rows_ref, capacity, store):
    rank = ranks(gates)
    for group in range(rows_ref.shape[0]):
        onehot = onehot_rows(rank, group, 2, capacity).T.astype(jnp.bfloat16)
        store(group, dot(onehot, rows_ref[group]).astype(jnp.bfloat16))


def backward_kernel(
    capacity, which_ref, gates_ref, keep_c_ref, keep_h_ref, give_1_ref, give_2_ref, give_3_ref,
    gu_ref, dn_ref, own_ref, other_ref, hidden_out, d_out,
    c, h, gu, dn, hidden, d, dh, sums, sems,
):
    row_count, width = keep_c_ref.shape
    group_count = row_count // capacity
    half = group_count // 2
    copies = Copies(sems)
    copies.start("h0", keep_h_ref, h.at[0])
    copies.start("c0", keep_c_ref, c.at[0])
    weight_copies(copies, 0, which_ref[0], gu_ref, dn_ref, gu, dn)
    for name, target, base in (("c1", c, 0), ("h1", h, row_count)):
        for send, there, part in overlaps(row_count, base, base + row_count):
            copies.start(
                name, (give_1_ref, give_2_ref, give_3_ref)[send].at[there], target.at[1, part]
            )
    weight_copies(copies, 1, which_ref[1], gu_ref, dn_ref, gu, dn)
    for expert in range(2):
        copies.wait("h%d" % expert)
        copies.wait("c%d" % expert)
        hidden_gradients(
            copies,
            expert,
            lambda: h[expert],
            lambda: c[expert],
            gu,
            dn,
            hidden if expert == 0 else None,
            d.at[expert],
        )
        if expert == 0:
            copies.start("out", hidden, hidden_out)
            copies.start("out", d.at[0], d_out)
        for start in range(0, width, tile):
            cols = slice(start, start + tile)
            part = dot(d[expert], gu[expert, cols, :], ((1,), (1,))).astype(jnp.bfloat16)
            dh[:, expert * capacity : (expert + 1) * capacity, cols] = part.reshape(
                group_count, capacity, tile
            )

    def store(group, value):
        sums[group] = value
        target = own_ref if group < half else other_ref
        copies.start("out", sums.at[group], target.at[group % half])

    combine(gates_ref[...], dh, capacity, store)
    copies.wait_all()


def backward_rows(keep_c, keep_h, give, weight_gu, weight_dn, gates, which, capacity):
    row_count, width = keep_c.shape
    hidden_units = weight_dn.shape[1]
    group_count = row_count // capacity
    token_count = gates.shape[-1]
    half = (group_count // 2, token_count, width)
    tiles = hidden_units // tile
    bf16 = jnp.bfloat16
    return pl.pallas_call(
        functools.partial(backward_kernel, capacity),
        in_specs=[scalar, vector] + [anywhere] * 7,
        out_specs=[anywhere] * 4,
        out_shape=[
            jax.ShapeDtypeStruct(half, bf16),
            jax.ShapeDtypeStruct(half, bf16),
            jax.ShapeDtypeStruct((row_count, hidden_units), bf16),
            jax.ShapeDtypeStruct((row_count, 2 * hidden_units), bf16),
        ],
        scratch_shapes=[
            pltpu.VMEM((2, row_count, width), bf16),
            pltpu.VMEM((2, row_count, width), bf16),
            pltpu.VMEM(weight_gu.shape, bf16),
            pltpu.VMEM(weight_dn.shape, bf16),
            pltpu.VMEM((row_count, hidden_units), bf16),
            pltpu.VMEM((2, row_count, 2 * hidden_units), bf16),
            pltpu.VMEM((group_count, 2 * capacity, width), bf16),
            pltpu.VMEM((group_count, token_count, width), bf16),
            pltpu.SemaphoreType.DMA((8 + 6 * tiles + group_count,)),
        ],
        compiler_params=kernel_params(),
        cost_estimate=light(),
        name="backward_rows",
    )(which, gates.reshape(-1, token_count), keep_c, keep_h, *give, weight_gu, weight_dn)


def forward_kernel(
    capacity, gates_ref, tokens_ref, gu_ref, dn_ref, out_ref,
    tokens, gu, dn, rows, scales, hidden, o, sums, sems,
):
    group_count, _, width = tokens.shape
    hidden_units = dn.shape[1]
    row_count = group_count * capacity
    copies = Copies(sems)
    for group in range(group_count):
        copies.start(("tokens", group), tokens_ref.at[group], tokens.at[group])
    for expert in range(2):
        weight_copies(copies, expert, expert, gu_ref, dn_ref, gu, dn)
    gates = gates_ref[...]
    rank = ranks(gates)
    for group in range(group_count):
        onehot = onehot_rows(rank, group, 2, capacity)
        scale = slot_gates(onehot, gates, group, 2, capacity)
        copies.wait(("tokens", group))
        placed = dot(onehot.astype(jnp.bfloat16), tokens[group]).astype(jnp.bfloat16)
        here = slice(group * capacity, (group + 1) * capacity)
        for expert in range(2):
            own = slice(expert * capacity, (expert + 1) * capacity)
            rows[expert, here] = placed[own]
            scales[expert, here] = jnp.broadcast_to(scale[own], (capacity, 128))
    for expert in range(2):
        for start in range(0, hidden_units, tile):
            cols = slice(start, start + tile)
            up_cols = slice(hidden_units + start, hidden_units + start + tile)
            copies.wait(("gu", expert, start))
            gate_pre = dot(rows[expert], gu[expert, :, cols])
            up_pre = dot(rows[expert], gu[expert, :, up_cols])
            hidden[:, cols] = (gate_pre / (1.0 + jnp.exp(-gate_pre)) * up_pre).astype(jnp.bfloat16)
        for start in range(0, hidden_units, tile):
            copies.wait(("dn", expert, start))
        scale = scales[expert][:, :1]
        for start in range(0, width, tile):
            cols = slice(start, start + tile)
            part = (dot(hidden[...], dn[expert, :, cols]) * scale).astype(jnp.bfloat16)
            o[:, expert * capacity : (expert + 1) * capacity, cols] = part.reshape(
                group_count, capacity, tile
            )

    def store(group, value):
        sums[group] = value
        copies.start("out", sums.at[group], out_ref.at[group])

    combine(gates, o, capacity, store)
    copies.wait_all()


def forward_rows(tokens, gates, weight_gu, weight_dn, capacity):
    group_count, token_count, width = tokens.shape
    hidden_units = weight_dn.shape[1]
    row_count = group_count * capacity
    tiles = hidden_units // tile
    bf16 = jnp.bfloat16
    return pl.pallas_call(
        functools.partial(forward_kernel, capacity),
        in_specs=[vector] + [anywhere] * 3,
        out_specs=anywhere,
        out_shape=jax.ShapeDtypeStruct((group_count, token_count, width), bf16),
        scratch_shapes=[
            pltpu.VMEM((group_count, token_count, width), bf16),
            pltpu.VMEM(weight_gu.shape, bf16),
            pltpu.VMEM(weight_dn.shape, bf16),
            pltpu.VMEM((2, row_count, width), bf16),
            pltpu.VMEM((2, row_count, 128), jnp.float32),
            pltpu.VMEM((row_count, hidden_units), bf16),
            pltpu.VMEM((group_count, 2 * capacity, width), bf16),
            pltpu.VMEM((group_count, token_count, width), bf16),
            pltpu.SemaphoreType.DMA((6 * tiles + 2 * group_count,)),
        ],
        compiler_params=kernel_params(),
        cost_estimate=light(),
        name="forward_rows",
    )(gates.reshape(-1, token_count), tokens, weight_gu, weight_dn)


def gradient_kernel(
    which_ref, keep_c_ref, keep_h_ref, hidden_ref, d_ref, far_1_ref, far_2_ref, far_3_ref,
    gu_ref, dn_ref, gu_out, dn_out, c, h, hidden, d, gu, dn, gu_sums, dn_sums, sems,
):
    row_count, width = keep_c_ref.shape
    hidden_units = dn.shape[1]
    far = slice(row_count, 2 * row_count)
    near = slice(0, row_count)
    copies = Copies(sems)
    for name, target, base in (("far", h, row_count), ("far", c, 0)):
        for send, there, part in overlaps(row_count, base, base + row_count):
            place = slice(row_count + part.start, row_count + part.stop)
            copies.start(
                name, (far_1_ref, far_2_ref, far_3_ref)[send].at[there], target.at[place]
            )
    weight_copies(copies, 0, which_ref[0], gu_ref, dn_ref, gu, dn)
    copies.start("hidden", hidden_ref, hidden.at[near])
    copies.start("c", keep_c_ref, c.at[near])
    copies.start("d", d_ref, d.at[near])
    copies.start("h", keep_h_ref, h.at[near])
    copies.wait("far")
    hidden_gradients(
        copies, 0, lambda: h[far], lambda: c[far], gu, dn, hidden.at[far], d.at[far]
    )
    first = ((0,), (0,))
    copies.wait("hidden")
    copies.wait("c")
    for start in range(0, hidden_units, tile):
        cols = slice(start, start + tile)
        dn_sums[cols] = dot(hidden[:, cols], c[...], first).astype(jnp.bfloat16)
        copies.start("out", dn_sums.at[cols], dn_out.at[cols])
    copies.wait("d")
    copies.wait("h")
    for start in range(0, width, tile):
        cols = slice(start, start + tile)
        gu_sums[cols] = dot(h[:, cols], d[...], first).astype(jnp.bfloat16)
        copies.start("out", gu_sums.at[cols], gu_out.at[cols])
    copies.wait_all()


def weight_gradients(which, keep_c, keep_h, hidden, d, far, weight_gu, weight_dn):
    row_count, width = keep_c.shape
    hidden_units = weight_dn.shape[1]
    bf16 = jnp.bfloat16
    gu_shape = (width, 2 * hidden_units)
    dn_shape = (hidden_units, width)
    count = 4 + 4 + 4 * (hidden_units // tile) + width // tile
    return pl.pallas_call(
        gradient_kernel,
        in_specs=[scalar] + [anywhere] * 9,
        out_specs=[anywhere] * 2,
        out_shape=[jax.ShapeDtypeStruct(gu_shape, bf16), jax.ShapeDtypeStruct(dn_shape, bf16)],
        scratch_shapes=[
            pltpu.VMEM((2 * row_count, width), bf16),
            pltpu.VMEM((2 * row_count, width), bf16),
            pltpu.VMEM((2 * row_count, hidden_units), bf16),
            pltpu.VMEM((2 * row_count, 2 * hidden_units), bf16),
            pltpu.VMEM((1,) + gu_shape, bf16),
            pltpu.VMEM((1,) + dn_shape, bf16),
            pltpu.VMEM(gu_shape, bf16),
            pltpu.VMEM(dn_shape, bf16),
            pltpu.SemaphoreType.DMA((count,)),
        ],
        compiler_params=kernel_params(),
        cost_estimate=light(),
        name="weight_gradients",
    )(which, keep_c, keep_h, hidden, d, *far, weight_gu, weight_dn)


def swap_cores(value):
    return lax.ppermute(value, "expert", [(i, i ^ 1) for i in range(lax.axis_size("expert"))])


def exchange_sums(chip):
    group_count = lax.axis_size("expert")
    lines = [list(range(c, group_count, 2)) for c in range(2)]
    return lax.all_to_all(
        chip, "expert", split_axis=0, concat_axis=0, tiled=True, axis_index_groups=lines
    )


def per_device(
    x_fwd, gate_fwd, route_fwd, x_bwd, gate_bwd, route_bwd, cotangent, norm_gain, w_gate_up, w_down
):
    group_count = lax.axis_size("expert")
    section_count = lax.axis_size("pipe")
    local_count = w_gate_up.shape[1]
    expert_count = local_count * group_count
    token_count, model_width = x_fwd.shape
    pick_count = route_fwd.shape[1]
    capacity = token_count * pick_count * 4 // (3 * expert_count)
    weight_gu = w_gate_up[0]
    weight_dn = w_down[0]

    upper_half = (lax.axis_index("pipe") >= section_count // 2).astype(jnp.int32)
    which = jnp.stack([upper_half, 1 - upper_half])
    core = lax.axis_index("expert") % 2
    chips = 2 * jnp.arange(group_count // 2, dtype=jnp.int32)
    order = jnp.concatenate([chips + core, chips + 1 - core])
    sides = jnp.stack([core, 1 - core])

    send_gates = jnp.stack(
        [
            expert_gates(gate_fwd, route_fwd, expert_count),
            expert_gates(gate_bwd, route_bwd, expert_count),
        ]
    ).reshape(2, group_count, local_count, token_count)
    recv_gates = lax.all_to_all(
        send_gates.transpose(1, 0, 2, 3), "expert", split_axis=0, concat_axis=0, tiled=True
    )
    gates_f = recv_gates[:, 0]
    gates_b = recv_gates[:, 1][order][:, which]
    gathered_bwd = lax.all_gather(
        normed(x_bwd, norm_gain, cotangent)[None], "expert", axis=0, tiled=True
    )
    gathered_fwd = lax.all_gather(normed(x_fwd, norm_gain), "expert", axis=0, tiled=True)

    mirror = [(i, section_count - 1 - i) for i in range(section_count)]
    keep_c, keep_h, *give = place_rows(gathered_bwd, gates_b, sides, capacity)
    far = [lax.ppermute(part, "pipe", mirror) for part in give]

    own_dh, other_dh, keep_hidden, keep_d = backward_rows(
        keep_c, keep_h, give, weight_gu, weight_dn, gates_b, which, capacity
    )
    other_dh, far[0] = lax.optimization_barrier((other_dh, far[0]))
    other_dh = swap_cores(other_dh)
    middle = token_count // 2
    chip_dh = [
        (own_dh[:, part].astype(jnp.float32) + other_dh[:, part].astype(jnp.float32)).astype(
            jnp.bfloat16
        )
        for part in (slice(0, middle), slice(middle, token_count))
    ]
    chip_dh, gathered_fwd = lax.optimization_barrier((chip_dh, gathered_fwd))
    parts_dh = [exchange_sums(chip) for chip in chip_dh]

    partial_y = forward_rows(gathered_fwd, gates_f, weight_gu, weight_dn, capacity)
    partial_y, parts_dh[0], far[1] = lax.optimization_barrier((partial_y, parts_dh[0], far[1]))
    y_fwd = lax.psum_scatter(
        partial_y.reshape(group_count * token_count, model_width),
        "expert",
        scatter_dimension=0,
        tiled=True,
    )

    out_gu, out_dn = weight_gradients(
        which, keep_c, keep_h, keep_hidden, keep_d, far, weight_gu, weight_dn
    )

    dh_sum = jnp.concatenate([jnp.sum(part.astype(jnp.float32), axis=0) for part in parts_dh])
    bwd_hat, bwd_scale = normalize(x_bwd)
    scaled_dh = norm_gain * dh_sum
    dx_bwd = (
        bwd_scale * (scaled_dh - bwd_hat * jnp.mean(bwd_hat * scaled_dh, axis=-1, keepdims=True))
    ).astype(jnp.bfloat16)
    return (y_fwd, dx_bwd, out_gu[None, None], out_dn[None, None])


def solution(mesh):
    rows = P(("pipe", "expert"), None)
    experts = P("pipe", "expert", None, None)
    return jax.shard_map(
        per_device,
        mesh=mesh,
        in_specs=(rows,) * 7 + (P(), experts, experts),
        out_specs=(rows, rows, experts, experts),
        check_vma=False,
    )
```

time: 214 us -> 204 us (0.953)
  other arithmetic: 12.1 us -> 6.65 us
  waiting for transfers between devices: 95.5 us -> 90.3 us
    reduce_scatter x1, waiting for transfers between devices: 9.96 us -> 4.73 us  [per_device(): lax.psum_scatter(partial_y.reshape(group_count * token_count, model_width...]
    pallas_call x3 -> x5, Pallas kernels: 57.1 us -> 59.7 us  [the longest x1 22.4 us: backward_rows(): pl.pallas_call(functools.partial(backward_kernel, capacity), in_specs=[sc...]
    reduce_sum x2 -> x1, other arithmetic: 2.35 us -> 0.16 us  [normalize(): jnp.mean(values * values, axis=-1, keepdims=True) + norm_eps]
  transfers between devices with their start and end apart: 10 -> 10, of which waited for: 7 -> 7; matrix products, arithmetic and copies ran while one was open for 4% -> 4% of each run, Pallas kernels for 30% -> 32%
where the time goes in v3:
time: 204 us; the launch traced here: 203 us
  waiting for transfers between devices  90.3 us (44%)
  Pallas kernels  66.6 us (33%)
  starting transfers between devices  21.9 us (11%)
  between operations  13.9 us (7%)
  other arithmetic  6.65 us (3%)
  local copies, waits for them, and re-layouts  3.64 us (2%)
    all_gather x1, waiting for transfers between devices, per_device(): lax.all_gather(normed(x_bwd, norm_gain, cotangent)[None], 'expert', axis=...  50.4 us
    ppermute x3, waiting for transfers between devices, per_device(): far = [lax.ppermute(part, 'pipe', mirror) for part in give]  27.3 us
    pallas_call x1, Pallas kernels, backward_rows(): pl.pallas_call(functools.partial(backward_kernel, capacity), in_specs=[sc...  22.4 us
    pallas_call x1, Pallas kernels, weight_gradients(): pl.pallas_call(gradient_kernel, in_specs=[scalar] + [anywhere] * 9, out_s...  18.5 us
    pallas_call x1, Pallas kernels, forward_rows(): pl.pallas_call(functools.partial(forward_kernel, capacity), in_specs=[vec...  14.7 us
    all_to_all x2, starting transfers between devices, exchange_sums(): lax.all_to_all(chip, 'expert', split_axis=0, concat_axis=0, tiled=True, a...  9.22 us
    pallas_call x1, Pallas kernels, place_rows(): pl.pallas_call(functools.partial(place_kernel, capacity), grid_spec=pltpu...  6.96 us
    ppermute x3, starting transfers between devices, per_device(): far = [lax.ppermute(part, 'pipe', mirror) for part in give]  6.4 us
  transfers between devices with their start and end apart: 10, of which 7 were waited for; matrix products, arithmetic and copies ran while one was open for 4% of the time, Pallas kernels for 32%

profile of v3, /device:TPU:9, one launch (start us, length us, event | category | flops | bytes accessed | tf_op | source)
XLA Modules:
  0.0 203.1 jit_solution(9425665455161640196)
XLA Ops:
  7.2 0.0 copy-start.5
  7.2 0.0 copy-start.6
  7.2 0.0 copy-start.7
  7.2 0.0 copy-start.8
  7.2 0.0 all-gather.6.cloned.1.call-start
  7.3 2.2 %normed.2 = bf16[2,128,1536]{2,1,0:T(8,128)(2,1)} custom-call(bf16[128,1536]{1,0:T(8,128)(2,1)} %x_ref.2, f32[1536]{0:T(1024)} %gain_ref.3, bf16[128,1536]{1,0:T(8,128)(2,1)} %refs_0_.1), custom_call_target="tpu_custom_call" | custom-call | flops 1000 | bytes 1000 | tf_op jit(solution)/shard_map/normed/pallas_call | solution.py:45
  9.5 0.0 all-gather.6.cloned.1.call-update
  9.5 0.0 all-gather.4.cloned.1.call-start
  9.5 1.9 normed.3
  11.5 0.0 all-gather.4.cloned.1.call-update
  11.5 0.0 copy-done.5
  11.5 0.0 copy-done.6
  11.5 0.0 copy-done.7
  11.5 0.0 copy-done.8
  11.6 0.6 maximum_bitcast_fusion
  12.2 5.6 %all-to-all-start = ((f32[8,2,2,128]{3,2,1,0:T(2,128)}), f32[8,2,2,128]{3,2,1,0:T(2,128)S(1)}, u32[]{:S(2)}, u32[]{:S(2)}) async-start(f32[8,2,2,128]{3,2,1,0:T(2,128)} %maximum_bitcast_fusion), calls=%async_computation | async-start | bytes 32768 | tf_op jit(solution)/shard_map/all_to_all | solution.py:494
  17.8 0.1 fusion.7
  17.9 0.1 fusion.8
  18.0 0.6 pad_add_fusion.1.sides_ref
  18.6 3.1 %all-to-all-done = f32[8,2,2,128]{3,2,1,0:T(2,128)S(1)} async-done(((f32[8,2,2,128]{3,2,1,0:T(2,128)}), f32[8,2,2,128]{3,2,1,0:T(2,128)S(1)}, u32[]{:S(2)}, u32[]{:S(2)}) %all-to-all-start) | async-done | bytes 16416 | tf_op jit(solution)/shard_map/all_to_all | solution.py:494
  21.7 0.6 slice_bitcast_fusion
  22.3 0.6 gather_fusion
  22.9 0.5 gather_fusion.1
  23.5 0.6 copy.43
  24.1 50.4 %all-gather.6.cloned.1.call-done = bf16[16,128,1536]{2,1,0:T(8,128)(2,1)} async-done(((bf16[2,128,1536]{2,1,0:T(8,128)(2,1)}), bf16[16,128,1536]{2,1,0:T(8,128)(2,1)}) %all-gather.6.cloned.1.call-update) | async-done | bytes 6291472 | tf_op jit(solution)/shard_map/all_gather | solution.py:499
  74.4 7.0 %place_rows.1 = (bf16[512,1536]{1,0:T(8,128)(2,1)}, bf16[512,1536]{1,0:T(8,128)(2,1)}, bf16[320,1536]{1,0:T(8,128)(2,1)}, bf16[240,1536]{1,0:T(8,128)(2,1)}, bf16[464,1536]{1,0:T(8,128)(2,1)}) custom-call(s32[2]{0:T(128)} %pad_add_fusion.1.sides_ref, bf16[4,2,2,128,1536]{4,3,2,1,0:T(8,128)(2,1)} %bitcast.42, bf16[4,2,2,128,1536]{4,3,2,1,0:T(8,128)(2,1)} %bitcast.43, ...), custom_call_target="tpu_custom_call" | custom-call | flops 1000 | bytes 1000 | tf_op jit(solution)/shard_map/place_rows/pallas_call | solution.py:136
  81.4 2.2 %collective-permute-start = (bf16[320,1536]{1,0:T(8,128)(2,1)}, bf16[320,1536]{1,0:T(8,128)(2,1)S(1)}, u32[]{:S(2)}, u32[]{:S(2)}) collective-permute-start(bf16[320,1536]{1,0:T(8,128)(2,1)} %get-tuple-element.25.give_1_ref), channel_id=1, source_target_pairs={{0,24},{8,16},{16,8},{24,0},{1,25},{9,17},{17,9},{25,1},{2,26},{10... | collective-permute-start | bytes 2949128 | tf_op jit(solution)/shard_map/ppermute | solution.py:506
  83.6 0.6 pad_add_fusion.which_ref
  84.2 22.4 %backward_rows.1 = (bf16[4,128,1536]{2,1,0:T(8,128)(2,1)}, bf16[4,128,1536]{2,1,0:T(8,128)(2,1)}, bf16[512,768]{1,0:T(8,128)(2,1)}, bf16[512,1536]{1,0:T(8,128)(2,1)}) custom-call(s32[2]{0:T(128)} %pad_add_fusion.which_ref, f32[16,128]{1,0:T(8,128)} %bitcast.46, bf16[512,1536]{1,0:T(8,128)(2,1)} %get-tuple-element.23.keep_c_ref, ...), custom_call_target="tpu_custom_call" | custom-call | flops 1000 | bytes 1000 | tf_op jit(solution)/shard_map/backward_rows/pallas_call | solution.py:282
  106.6 0.0 collective-permute-done.far_1_ref
  106.6 0.0 copy-start.1
  106.6 0.6 collective-permute-start.1
  107.2 3.2 %collective-permute-done.1 = bf16[4,128,1536]{2,1,0:T(8,128)(2,1)S(1)} collective-permute-done((bf16[4,128,1536]{2,1,0:T(8,128)(2,1)}, bf16[4,128,1536]{2,1,0:T(8,128)(2,1)S(1)}, u32[]{:S(2)}, u32[]{:S(2)}) %collective-permute-start.1) | collective-permute-done | bytes 1572896 | tf_op jit(solution)/shard_map/ppermute | solution.py:457
  110.4 2.9 %add_convert_fusion = (bf16[4,64,1536]{2,1,0:T(8,128)(2,1)}, bf16[4,64,1536]{2,1,0:T(8,128)(2,1)}) fusion(bf16[4,128,1536]{2,1,0:T(8,128)(2,1)S(1)} %collective-permute-done.1, bf16[4,128,1536]{2,1,0:T(8,128)(2,1)} %get-tuple-element.28), kind=kLoop, calls=%fused_computation.4 | loop fusion | flops 3145728 | bytes 4718592 | tf_op jit(solution)/shard_map/convert_element_type | solution.py:515
  113.4 0.0 copy-done.1
  113.4 0.0 copy-start.3
  113.4 1.5 all-gather.4.cloned.1.call-done.tokens_ref
  114.8 4.7 %all-to-all-start.1 = ((bf16[4,64,1536]{2,1,0:T(8,128)(2,1)}), bf16[4,64,1536]{2,1,0:T(8,128)(2,1)S(1)}, u32[]{:S(2)}, u32[]{:S(2)}) async-start(bf16[4,64,1536]{2,1,0:T(8,128)(2,1)} %get-tuple-element.32), calls=%async_computation.1 | async-start | bytes 1572864 | tf_op jit(solution)/shard_map/all_to_all | solution.py:463
  119.5 0.0 reduce-scatter.2.cloned.1.call-start
  119.5 0.0 copy-done.3
  119.5 2.1 %collective-permute-start.2 = (bf16[240,1536]{1,0:T(8,128)(2,1)S(1)}, bf16[240,1536]{1,0:T(8,128)(2,1)S(1)}, u32[]{:S(2)}, u32[]{:S(2)}) collective-permute-start(bf16[240,1536]{1,0:T(8,128)(2,1)S(1)} %copy-done.3), channel_id=1, source_target_pairs={{0,24},{8,16},{16,8},{24,0},{1,25},{9,17},{17,9},{25,1},{2,26},{10... | collective-permute-start | bytes 2211848 | tf_op jit(solution)/shard_map/ppermute | solution.py:506
  121.6 14.7 %forward_rows.1 = bf16[8,128,1536]{2,1,0:T(8,128)(2,1)} custom-call(f32[16,128]{1,0:T(8,128)} %bitcast.47, bf16[8,128,1536]{2,1,0:T(8,128)(2,1)} %all-gather.4.cloned.1.call-done.tokens_ref, bf16[2,1536,1536]{2,1,0:T(8,128)(2,1)} %bitcast.37, bf16[2,768,1536]{2,1,0:T(8,128)(2,1)} %bitcast.40), custom_call_target="tpu_custom_call" | custom-call | flops 1000 | bytes 1000 | tf_op jit(solution)/shard_map/forward_rows/pallas_call | solution.py:365
  136.3 1.6 collective-permute-done.2.far_2_ref
  137.9 0.0 copy-start.2
  137.9 0.0 all-to-all-done.1
  137.9 0.0 reduce-scatter.2.cloned.1.call-update
  137.9 0.8 copy-done.2
  138.8 0.0 copy-start
  138.8 2.1 %collective-permute-start.3 = (bf16[464,1536]{1,0:T(8,128)(2,1)}, bf16[464,1536]{1,0:T(8,128)(2,1)}, u32[]{:S(2)}, u32[]{:S(2)}) collective-permute-start(bf16[464,1536]{1,0:T(8,128)(2,1)} %get-tuple-element.27.give_3_ref), channel_id=1, source_target_pairs={{0,24},{8,16},{16,8},{24,0},{1,25},{9,17},{17,9},{25,1},{2,26},{10... | collective-permute-start | bytes 4276232 | tf_op jit(solution)/shard_map/ppermute | solution.py:506
  140.9 4.5 %all-to-all-start.2 = ((bf16[4,64,1536]{2,1,0:T(8,128)(2,1)}), bf16[4,64,1536]{2,1,0:T(8,128)(2,1)S(1)}, u32[]{:S(2)}, u32[]{:S(2)}) async-start(bf16[4,64,1536]{2,1,0:T(8,128)(2,1)} %get-tuple-element.35), calls=%async_computation.3 | async-start | bytes 1572864 | tf_op jit(solution)/shard_map/all_to_all | solution.py:463
  145.4 0.0 copy-done
  145.4 0.2 fusion.6
  145.6 25.7 %collective-permute-done.3.far_3_ref = bf16[464,1536]{1,0:T(8,128)(2,1)} collective-permute-done((bf16[464,1536]{1,0:T(8,128)(2,1)}, bf16[464,1536]{1,0:T(8,128)(2,1)}, u32[]{:S(2)}, u32[]{:S(2)}) %collective-permute-start.3) | collective-permute-done | bytes 1425440 | tf_op jit(solution)/shard_map/ppermute | solution.py:506
  171.3 18.5 %weight_gradients.1 = (bf16[1536,1536]{1,0:T(8,128)(2,1)}, bf16[768,1536]{1,0:T(8,128)(2,1)}) custom-call(s32[2]{0:T(128)} %pad_add_fusion.which_ref, bf16[512,1536]{1,0:T(8,128)(2,1)} %get-tuple-element.23.keep_c_ref, bf16[512,1536]{1,0:T(8,128)(2,1)} %get-tuple-element.24.keep_h_ref, bf16[512,768]{1,0:T(8,128)(2,1)} %get-tuple-element.36.hidden_ref, ...), custom_call_target="tpu_custom_call" | custom-call | flops 1000 | bytes 1000 | tf_op jit(solution)/shard_map/weight_gradients/pallas_call | solution.py:434
  189.8 0.0 copy-start.4
  189.8 0.1 convert_reduce_fusion.1
  189.9 0.0 all-to-all-done.2
  189.9 0.1 convert_reduce_fusion
  190.1 0.4 copy-done.4
  190.5 0.3 fusion.2
  190.8 1.0 fusion.5
  191.8 4.7 %reduce-scatter.2.cloned.1.call-done = bf16[128,1536]{1,0:T(8,128)(2,1)} async-done(((bf16[1024,1536]{1,0:T(8,128)(2,1)}), bf16[128,1536]{1,0:T(8,128)(2,1)}) %reduce-scatter.2.cloned.1.call-update) | async-done | bytes 393232 | tf_op jit(solution)/shard_map/reduce_scatter | solution.py:525
  (8 shorter events, 0.1 us)
Async XLA Ops:
  7.2 4.3 %copy-start.5 = (f32[128,6]{0,1:T(8,128)S(1)}, f32[128,6]{0,1:T(8,128)}, u32[]{:S(2)}) copy-start(f32[128,6]{0,1:T(8,128)} %param.14) | copy-start | bytes 9220
  7.2 4.3 %copy-start.6 = (s32[128,6]{0,1:T(8,128)S(1)}, s32[128,6]{0,1:T(8,128)}, u32[]{:S(2)}) copy-start(s32[128,6]{0,1:T(8,128)} %param.15) | copy-start | bytes 9220
  7.2 4.4 %copy-start.7 = (f32[128,6]{0,1:T(8,128)S(1)}, f32[128,6]{0,1:T(8,128)}, u32[]{:S(2)}) copy-start(f32[128,6]{0,1:T(8,128)} %param.11) | copy-start | bytes 9220
  7.2 4.4 %copy-start.8 = (s32[128,6]{0,1:T(8,128)S(1)}, s32[128,6]{0,1:T(8,128)}, u32[]{:S(2)}) copy-start(s32[128,6]{0,1:T(8,128)} %param.12) | copy-start | bytes 9220
  7.2 67.2 %all-gather.6.cloned.1.call-start = ((), (), s32[]{:S(2)}) async-start(), calls=%async_computation.6 | async-start | bytes 7077888 | tf_op jit(solution)/shard_map/all_gather | solution.py:499
  9.5 105.3 %all-gather.4.cloned.1.call-start = ((), (), s32[]{:S(2)}) async-start(), calls=%async_computation.4 | async-start | bytes 3538944 | tf_op jit(solution)/shard_map/all_gather | solution.py:502
  12.2 9.5 %all-to-all-start = ((f32[8,2,2,128]{3,2,1,0:T(2,128)}), f32[8,2,2,128]{3,2,1,0:T(2,128)S(1)}, u32[]{:S(2)}, u32[]{:S(2)}) async-start(f32[8,2,2,128]{3,2,1,0:T(2,128)} %maximum_bitcast_fusion), calls=%async_computation | async-start | bytes 32768 | tf_op jit(solution)/shard_map/all_to_all | solution.py:494
  81.4 25.2 %collective-permute-start = (bf16[320,1536]{1,0:T(8,128)(2,1)}, bf16[320,1536]{1,0:T(8,128)(2,1)S(1)}, u32[]{:S(2)}, u32[]{:S(2)}) collective-permute-start(bf16[320,1536]{1,0:T(8,128)(2,1)} %get-tuple-element.25.give_1_ref), channel_id=1, source_target_pairs={{0,24},{8,16},{16,8},{24,0},{1,25},{9,17},{17,9},{25,1},{2,26},{10... | collective-permute-start | bytes 2949128 | tf_op jit(solution)/shard_map/ppermute | solution.py:506
  106.6 6.8 %copy-start.1 = (bf16[320,1536]{1,0:T(8,128)(2,1)}, bf16[320,1536]{1,0:T(8,128)(2,1)S(1)}, u32[]{:S(2)}) copy-start(bf16[320,1536]{1,0:T(8,128)(2,1)S(1)} %collective-permute-done.far_1_ref) | copy-start | bytes 2949124
  106.6 3.8 %collective-permute-start.1 = (bf16[4,128,1536]{2,1,0:T(8,128)(2,1)}, bf16[4,128,1536]{2,1,0:T(8,128)(2,1)S(1)}, u32[]{:S(2)}, u32[]{:S(2)}) collective-permute-start(bf16[4,128,1536]{2,1,0:T(8,128)(2,1)} %get-tuple-element.30), channel_id=1, source_target_pairs={{0,1},{1,0},{2,3},{3,2},{4,5},{5,4},{6,7},{7,6},{8,9},{9,8},{10,11... | collective-permute-start | bytes 4718600 | tf_op jit(solution)/shard_map/ppermute | solution.py:457
  113.4 6.2 %copy-start.3 = (bf16[240,1536]{1,0:T(8,128)(2,1)S(1)}, bf16[240,1536]{1,0:T(8,128)(2,1)}, u32[]{:S(2)}) copy-start(bf16[240,1536]{1,0:T(8,128)(2,1)} %get-tuple-element.26.give_2_ref) | copy-start | bytes 2211844
  114.8 23.1 %all-to-all-start.1 = ((bf16[4,64,1536]{2,1,0:T(8,128)(2,1)}), bf16[4,64,1536]{2,1,0:T(8,128)(2,1)S(1)}, u32[]{:S(2)}, u32[]{:S(2)}) async-start(bf16[4,64,1536]{2,1,0:T(8,128)(2,1)} %get-tuple-element.32), calls=%async_computation.1 | async-start | bytes 1572864 | tf_op jit(solution)/shard_map/all_to_all | solution.py:463
  119.5 77.0 %reduce-scatter.2.cloned.1.call-start = ((), (), s32[]{:S(2)}) async-start(), calls=%async_computation.5 | async-start | bytes 3538944 | tf_op jit(solution)/shard_map/reduce_scatter | solution.py:525
  119.5 18.4 %collective-permute-start.2 = (bf16[240,1536]{1,0:T(8,128)(2,1)S(1)}, bf16[240,1536]{1,0:T(8,128)(2,1)S(1)}, u32[]{:S(2)}, u32[]{:S(2)}) collective-permute-start(bf16[240,1536]{1,0:T(8,128)(2,1)S(1)} %copy-done.3), channel_id=1, source_target_pairs={{0,24},{8,16},{16,8},{24,0},{1,25},{9,17},{17,9},{25,1},{2,26},{10... | collective-permute-start | bytes 2211848 | tf_op jit(solution)/shard_map/ppermute | solution.py:506
  137.9 0.9 copy-start.2
  138.8 6.6 %copy-start = (bf16[128,1536]{1,0:T(8,128)(2,1)S(1)}, bf16[128,1536]{1,0:T(8,128)(2,1)}, u32[]{:S(2)}) copy-start(bf16[128,1536]{1,0:T(8,128)(2,1)} %x_ref.2) | copy-start | bytes 1179652
  138.8 32.5 %collective-permute-start.3 = (bf16[464,1536]{1,0:T(8,128)(2,1)}, bf16[464,1536]{1,0:T(8,128)(2,1)}, u32[]{:S(2)}, u32[]{:S(2)}) collective-permute-start(bf16[464,1536]{1,0:T(8,128)(2,1)} %get-tuple-element.27.give_3_ref), channel_id=1, source_target_pairs={{0,24},{8,16},{16,8},{24,0},{1,25},{9,17},{17,9},{25,1},{2,26},{10... | collective-permute-start | bytes 4276232 | tf_op jit(solution)/shard_map/ppermute | solution.py:506
  140.9 49.0 %all-to-all-start.2 = ((bf16[4,64,1536]{2,1,0:T(8,128)(2,1)}), bf16[4,64,1536]{2,1,0:T(8,128)(2,1)S(1)}, u32[]{:S(2)}, u32[]{:S(2)}) async-start(bf16[4,64,1536]{2,1,0:T(8,128)(2,1)} %get-tuple-element.35), calls=%async_computation.3 | async-start | bytes 1572864 | tf_op jit(solution)/shard_map/all_to_all | solution.py:463
  189.8 0.7 copy-start.4
Sparse Core Ops, SparseCore 0:
  10.3 64.1 all-gather.5
  76.6 38.1 all-gather.3
  138.1 58.4 reduce-scatter.1

commit v4 on v3

--- a/solution.py
+++ b/solution.py
@@ -10,11 +10,12 @@
 norm_eps = 1e-06
 tile = 256
 vmem_bytes = 56 * 1024 * 1024
+shared_vmem_bytes = 28 * 1024 * 1024
 
 
 def params():
     return pltpu.CompilerParams(
-        dimension_semantics=("arbitrary",), vmem_limit_bytes=vmem_bytes
+        dimension_semantics=("arbitrary",), vmem_limit_bytes=shared_vmem_bytes
     )
 
 
@@ -87,7 +88,7 @@
 
 
 def cuts(row_count):
-    ends = [0, row_count * 5 // 8, row_count * 35 // 32, row_count * 2]
+    ends = [0, row_count * 9 // 32, row_count // 2, row_count]
     return [(start, end) for start, end in zip(ends[:-1], ends[1:])]
 
 
@@ -117,12 +118,16 @@
             keep_c_ref[here] = rows_c[:capacity]
             keep_h_ref[here] = rows_h[:capacity]
             first = (side * half + group) * capacity
-            for base, rows in ((first, rows_c), (row_count + first, rows_h)):
-                for send, there, part in overlaps(row_count, base, base + capacity):
-                    give_refs[send][there] = rows[capacity:][part]
+            for send, there, part in overlaps(row_count, first, first + capacity):
+                give_refs[send][0, there] = rows_c[capacity:][part]
+                give_refs[send][1, there] = rows_h[capacity:][part]
 
     for side in range(2):
         pl.when(pl.program_id(0) == side)(functools.partial(place, side))
+
+
+def in_main(value):
+    return pltpu.with_memory_space_constraint(value, pltpu.HBM)
 
 
 def place_rows(tokens, gates, sides, capacity):
@@ -130,7 +135,7 @@
     half = group_count // 2
     row_count = group_count * capacity
     rows_spec = pl.BlockSpec((row_count // 2, width), lambda i, sides: (i, 0))
-    give_shapes = [(end - start, width) for start, end in cuts(row_count)]
+    give_shapes = [(2, end - start, width) for start, end in cuts(row_count)]
     block = (half, 1, 1, token_count, width)
     tokens = tokens.reshape(half, 2, 2, token_count, width)
     return pl.pallas_call(
@@ -144,14 +149,14 @@
                 pl.BlockSpec((1, half * 2, token_count), lambda i, sides: (i, 0, 0)),
             ],
             out_specs=[rows_spec, rows_spec]
-            + [pl.BlockSpec(shape, lambda i, sides: (0, 0)) for shape in give_shapes],
+            + [pl.BlockSpec(shape, lambda i, sides: (0, 0, 0)) for shape in give_shapes],
         ),
-        out_shape=[jax.ShapeDtypeStruct((row_count, width), jnp.bfloat16)] * 2
-        + [jax.ShapeDtypeStruct(shape, jnp.bfloat16) for shape in give_shapes],
+        out_shape=[pltpu.HBM((row_count, width), jnp.bfloat16)] * 2
+        + [pltpu.HBM(shape, jnp.bfloat16) for shape in give_shapes],
         compiler_params=params(),
         cost_estimate=light(),
         name="place_rows",
-    )(sides, tokens, tokens, gates.reshape(2, half * 2, token_count))
+    )(sides, in_main(tokens), in_main(tokens), gates.reshape(2, half * 2, token_count))
 
 
 class Copies:
@@ -185,16 +190,22 @@
         copies.start(("dn", expert, start), dn_ref.at[source, rows], dn.at[expert, rows])
 
 
-def hidden_gradients(copies, expert, h, c, gu, dn, hidden_ref, d_ref):
-    hidden_units = dn.shape[1]
+def down_copies(copies, expert, source, dn_ref, dn):
+    for start in range(0, dn.shape[1], tile):
+        part = slice(start, start + tile)
+        copies.start(("dn", expert, start), dn_ref.at[source, part], dn.at[expert, part])
+
+
+def hidden_gradients(copies, key, h, c, gu, dn, hidden_ref, d_ref):
+    hidden_units = dn.shape[0]
     for start in range(0, hidden_units, tile):
         cols = slice(start, start + tile)
         up_cols = slice(hidden_units + start, hidden_units + start + tile)
-        copies.wait(("gu", expert, start))
-        gate_pre = dot(h(), gu[expert, :, cols])
-        up_pre = dot(h(), gu[expert, :, up_cols])
-        copies.wait(("dn", expert, start))
-        back = dot(c(), dn[expert, cols, :], ((1,), (1,)))
+        copies.wait(("gu", key, start))
+        gate_pre = dot(h(), gu[:, cols])
+        up_pre = dot(h(), gu[:, up_cols])
+        copies.wait(("dn", key, start))
+        back = dot(c(), dn[cols, :], ((1,), (1,)))
         squash = 1.0 / (1.0 + jnp.exp(-gate_pre))
         activated = gate_pre * squash
         if hidden_ref is not None:
@@ -210,8 +221,12 @@
 scalar = pl.BlockSpec(memory_space=pltpu.SMEM)
 
 
-def kernel_params():
-    return pltpu.CompilerParams(vmem_limit_bytes=vmem_bytes)
+def in_vector(value):
+    return pltpu.with_memory_space_constraint(value, pltpu.VMEM)
+
+
+def kernel_params(limit=vmem_bytes):
+    return pltpu.CompilerParams(vmem_limit_bytes=limit)
 
 
 def combine(gates, rows_ref, capacity, store):
@@ -223,8 +238,8 @@
 
 def backward_kernel(
     capacity, which_ref, gates_ref, keep_c_ref, keep_h_ref, give_1_ref, give_2_ref, give_3_ref,
-    gu_ref, dn_ref, own_ref, other_ref, hidden_out, d_out,
-    c, h, gu, dn, hidden, d, dh, sums, sems,
+    gu, dn_ref, own_ref, other_ref, hidden_out, d_out,
+    c, h, dn, hidden, d, dh, sums, sems,
 ):
     row_count, width = keep_c_ref.shape
     group_count = row_count // capacity
@@ -232,14 +247,14 @@
     copies = Copies(sems)
     copies.start("h0", keep_h_ref, h.at[0])
     copies.start("c0", keep_c_ref, c.at[0])
-    weight_copies(copies, 0, which_ref[0], gu_ref, dn_ref, gu, dn)
-    for name, target, base in (("c1", c, 0), ("h1", h, row_count)):
-        for send, there, part in overlaps(row_count, base, base + row_count):
-            copies.start(
-                name, (give_1_ref, give_2_ref, give_3_ref)[send].at[there], target.at[1, part]
-            )
-    weight_copies(copies, 1, which_ref[1], gu_ref, dn_ref, gu, dn)
+    down_copies(copies, 0, which_ref[0], dn_ref, dn)
+    for send, there, part in overlaps(row_count, 0, row_count):
+        give_ref = (give_1_ref, give_2_ref, give_3_ref)[send]
+        copies.start("c1", give_ref.at[0, there], c.at[1, part])
+        copies.start("h1", give_ref.at[1, there], h.at[1, part])
+    down_copies(copies, 1, which_ref[1], dn_ref, dn)
     for expert in range(2):
+        source = which_ref[expert]
         copies.wait("h%d" % expert)
         copies.wait("c%d" % expert)
         hidden_gradients(
@@ -247,8 +262,8 @@
             expert,
             lambda: h[expert],
             lambda: c[expert],
-            gu,
-            dn,
+            gu.at[source],
+            dn.at[expert],
             hidden if expert == 0 else None,
             d.at[expert],
         )
@@ -257,7 +272,7 @@
             copies.start("out", d.at[0], d_out)
         for start in range(0, width, tile):
             cols = slice(start, start + tile)
-            part = dot(d[expert], gu[expert, cols, :], ((1,), (1,))).astype(jnp.bfloat16)
+            part = dot(d[expert], gu[source, cols, :], ((1,), (1,))).astype(jnp.bfloat16)
             dh[:, expert * capacity : (expert + 1) * capacity, cols] = part.reshape(
                 group_count, capacity, tile
             )
@@ -277,33 +292,31 @@
     group_count = row_count // capacity
     token_count = gates.shape[-1]
     half = (group_count // 2, token_count, width)
-    tiles = hidden_units // tile
     bf16 = jnp.bfloat16
     return pl.pallas_call(
         functools.partial(backward_kernel, capacity),
-        in_specs=[scalar, vector] + [anywhere] * 7,
+        in_specs=[scalar, vector] + [anywhere] * 5 + [vector, anywhere],
         out_specs=[anywhere] * 4,
         out_shape=[
-            jax.ShapeDtypeStruct(half, bf16),
-            jax.ShapeDtypeStruct(half, bf16),
-            jax.ShapeDtypeStruct((row_count, hidden_units), bf16),
-            jax.ShapeDtypeStruct((row_count, 2 * hidden_units), bf16),
+            pltpu.HBM(half, bf16),
+            pltpu.HBM(half, bf16),
+            pltpu.HBM((row_count, hidden_units), bf16),
+            pltpu.HBM((row_count, 2 * hidden_units), bf16),
         ],
         scratch_shapes=[
             pltpu.VMEM((2, row_count, width), bf16),
             pltpu.VMEM((2, row_count, width), bf16),
-            pltpu.VMEM(weight_gu.shape, bf16),
             pltpu.VMEM(weight_dn.shape, bf16),
             pltpu.VMEM((row_count, hidden_units), bf16),
             pltpu.VMEM((2, row_count, 2 * hidden_units), bf16),
             pltpu.VMEM((group_count, 2 * capacity, width), bf16),
             pltpu.VMEM((group_count, token_count, width), bf16),
-            pltpu.SemaphoreType.DMA((8 + 6 * tiles + group_count,)),
+            pltpu.SemaphoreType.DMA((10 + 2 * (hidden_units // tile) + group_count,)),
         ],
-        compiler_params=kernel_params(),
+        compiler_params=kernel_params(shared_vmem_bytes),
         cost_estimate=light(),
         name="backward_rows",
-    )(which, gates.reshape(-1, token_count), keep_c, keep_h, *give, weight_gu, weight_dn)
+    )(which, gates.reshape(-1, token_count), *map(in_main, (keep_c, keep_h, *give)), in_vector(weight_gu), in_main(weight_dn))
 
 
 def forward_kernel(
@@ -384,63 +397,69 @@
     )(gates.reshape(-1, token_count), tokens, weight_gu, weight_dn)
 
 
-def gradient_kernel(
-    which_ref, keep_c_ref, keep_h_ref, hidden_ref, d_ref, far_1_ref, far_2_ref, far_3_ref,
-    gu_ref, dn_ref, gu_out, dn_out, c, h, hidden, d, gu, dn, gu_sums, dn_sums, sems,
-):
-    row_count, width = keep_c_ref.shape
+def gradient_kernel(near_rows, send_count, which_ref, *refs):
+    before, refs = refs[: 4 if near_rows else 2], refs[4 if near_rows else 2 :]
+    sends, refs = refs[:send_count], refs[send_count:]
+    gu_ref, dn_ref, gu_out, dn_out, c, h, hidden, d, gu, dn, gu_sums, dn_sums, sems = refs
+    row_count, width = c.shape
     hidden_units = dn.shape[1]
-    far = slice(row_count, 2 * row_count)
-    near = slice(0, row_count)
+    near = slice(0, near_rows)
+    far = slice(near_rows, row_count)
     copies = Copies(sems)
-    for name, target, base in (("far", h, row_count), ("far", c, 0)):
-        for send, there, part in overlaps(row_count, base, base + row_count):
-            place = slice(row_count + part.start, row_count + part.stop)
-            copies.start(
-                name, (far_1_ref, far_2_ref, far_3_ref)[send].at[there], target.at[place]
-            )
+    start = near_rows
+    for send in sends:
+        place = slice(start, start + send.shape[1])
+        start = place.stop
+        copies.start("far", send.at[1], h.at[place])
+        copies.start("far", send.at[0], c.at[place])
     weight_copies(copies, 0, which_ref[0], gu_ref, dn_ref, gu, dn)
-    copies.start("hidden", hidden_ref, hidden.at[near])
-    copies.start("c", keep_c_ref, c.at[near])
-    copies.start("d", d_ref, d.at[near])
-    copies.start("h", keep_h_ref, h.at[near])
+    if near_rows:
+        copies.start("dn sums", before[2], hidden.at[near])
+        copies.start("dn sums", before[0], c.at[near])
+        copies.start("gu sums", before[3], d.at[near])
+        copies.start("gu sums", before[1], h.at[near])
+    else:
+        copies.start("dn sums", before[1], dn_sums)
+        copies.start("gu sums", before[0], gu_sums)
     copies.wait("far")
     hidden_gradients(
-        copies, 0, lambda: h[far], lambda: c[far], gu, dn, hidden.at[far], d.at[far]
-    )
-    first = ((0,), (0,))
-    copies.wait("hidden")
-    copies.wait("c")
-    for start in range(0, hidden_units, tile):
-        cols = slice(start, start + tile)
-        dn_sums[cols] = dot(hidden[:, cols], c[...], first).astype(jnp.bfloat16)
-        copies.start("out", dn_sums.at[cols], dn_out.at[cols])
-    copies.wait("d")
-    copies.wait("h")
-    for start in range(0, width, tile):
-        cols = slice(start, start + tile)
-        gu_sums[cols] = dot(h[:, cols], d[...], first).astype(jnp.bfloat16)
-        copies.start("out", gu_sums.at[cols], gu_out.at[cols])
+        copies, 0, lambda: h[far], lambda: c[far], gu.at[0], dn.at[0], hidden.at[far], d.at[far]
+    )
+
+    def accumulate(name, left, right, sums, out):
+        copies.wait(name)
+        for start in range(0, left.shape[1], tile):
+            cols = slice(start, start + tile)
+            total = dot(left[:, cols], right[...], ((0,), (0,)))
+            if not near_rows:
+                total = total + sums[cols].astype(jnp.float32)
+            sums[cols] = total.astype(jnp.bfloat16)
+            copies.start("out", sums.at[cols], out.at[cols])
+
+    accumulate("dn sums", hidden, c, dn_sums, dn_out)
+    accumulate("gu sums", h, d, gu_sums, gu_out)
     copies.wait_all()
 
 
-def weight_gradients(which, keep_c, keep_h, hidden, d, far, weight_gu, weight_dn):
-    row_count, width = keep_c.shape
+def weight_gradients(which, before, sends, weight_gu, weight_dn):
+    width = weight_gu.shape[1]
     hidden_units = weight_dn.shape[1]
+    near_rows = before[0].shape[0] if len(before) == 4 else 0
+    row_count = near_rows + sum(send.shape[1] for send in sends)
     bf16 = jnp.bfloat16
     gu_shape = (width, 2 * hidden_units)
     dn_shape = (hidden_units, width)
-    count = 4 + 4 + 4 * (hidden_units // tile) + width // tile
+    count = 2 * len(sends) + len(before) + 4 * (hidden_units // tile) + width // tile
     return pl.pallas_call(
-        gradient_kernel,
-        in_specs=[scalar] + [anywhere] * 9,
+        functools.partial(gradient_kernel, near_rows, len(sends)),
+        in_specs=[scalar] + [anywhere] * (len(before) + len(sends) + 2),
         out_specs=[anywhere] * 2,
         out_shape=[jax.ShapeDtypeStruct(gu_shape, bf16), jax.ShapeDtypeStruct(dn_shape, bf16)],
         scratch_shapes=[
-            pltpu.VMEM((2 * row_count, width), bf16),
-            pltpu.VMEM((2 * row_count, width), bf16),
-            pltpu.VMEM((2 * row_count, hidden_units), bf16),
-            pltpu.VMEM((2 * row_count, 2 * hidden_units), bf16),
+            pltpu.VMEM((row_count, width), bf16),
+            pltpu.VMEM((row_count, width), bf16),
+            pltpu.VMEM((row_count, hidden_units), bf16),
+            pltpu.VMEM((row_count, 2 * hidden_units), bf16),
             pltpu.VMEM((1,) + gu_shape, bf16),
             pltpu.VMEM((1,) + dn_shape, bf16),
             pltpu.VMEM(gu_shape, bf16),
@@ -450,7 +469,7 @@
         compiler_params=kernel_params(),
         cost_estimate=light(),
         name="weight_gradients",
-    )(which, keep_c, keep_h, hidden, d, *far, weight_gu, weight_dn)
+    )(which, *before, *sends, weight_gu, weight_dn)
 
 
 def swap_cores(value):
@@ -517,7 +536,6 @@
         )
         for part in (slice(0, middle), slice(middle, token_count))
     ]
-    chip_dh, gathered_fwd = lax.optimization_barrier((chip_dh, gathered_fwd))
     parts_dh = [exchange_sums(chip) for chip in chip_dh]
 
     partial_y = forward_rows(gathered_fwd, gates_f, weight_gu, weight_dn, capacity)
@@ -529,16 +547,18 @@
         tiled=True,
     )
 
-    out_gu, out_dn = weight_gradients(
-        which, keep_c, keep_h, keep_hidden, keep_d, far, weight_gu, weight_dn
-    )
-
     dh_sum = jnp.concatenate([jnp.sum(part.astype(jnp.float32), axis=0) for part in parts_dh])
     bwd_hat, bwd_scale = normalize(x_bwd)
     scaled_dh = norm_gain * dh_sum
     dx_bwd = (
         bwd_scale * (scaled_dh - bwd_hat * jnp.mean(bwd_hat * scaled_dh, axis=-1, keepdims=True))
     ).astype(jnp.bfloat16)
+
+    dx_bwd, far[2] = lax.optimization_barrier((dx_bwd, far[2]))
+    gradients = weight_gradients(
+        which, (keep_c, keep_h, keep_hidden, keep_d), far[:2], weight_gu, weight_dn
+    )
+    out_gu, out_dn = weight_gradients(which, gradients, far[2:], weight_gu, weight_dn)
     return (y_fwd, dx_bwd, out_gu[None, None], out_dn[None, None])
 
 

time: 204 us -> 199 us (0.975)
  waiting for transfers between devices: 90.3 us -> 83.2 us
  Pallas kernels: 66.6 us -> 69.8 us
    ppermute x3, waiting for transfers between devices: 27.3 us -> 9.99 us  [per_device(): far = [lax.ppermute(part, 'pipe', mirror) for part in give]]
    all_to_all x2, waiting for transfers between devices: 0.01 us -> 9.48 us  [exchange_sums(): lax.all_to_all(chip, 'expert', split_axis=0, concat_axis=0, tiled=True, a...]
    pallas_call x1 -> x2, Pallas kernels: 18.5 us -> 23.2 us  [weight_gradients(): pl.pallas_call(functools.partial(gradient_kernel, near_rows, len(sends)),...]
  transfers between devices with their start and end apart: 10 -> 10, of which waited for: 7 -> 7; matrix products, arithmetic and copies ran while one was open for 4% -> 4% of each run, Pallas kernels for 32% -> 34%
where the time goes in v4:
time: 199 us
  waiting for transfers between devices  83.2 us (42%)
  Pallas kernels  69.8 us (35%)
  starting transfers between devices  23.5 us (12%)
  between operations  13.9 us (7%)
  other arithmetic  5.66 us (3%)
  local copies, waits for them, and re-layouts  2.6 us (1%)
    all_gather x1, waiting for transfers between devices, per_device(): lax.all_gather(normed(x_bwd, norm_gain, cotangent)[None], 'expert', axis=...  50.9 us
    pallas_call x2, Pallas kernels, weight_gradients(): pl.pallas_call(functools.partial(gradient_kernel, near_rows, len(sends)),...  23.2 us
    pallas_call x1, Pallas kernels, backward_rows(): pl.pallas_call(functools.partial(backward_kernel, capacity), in_specs=[sc...  20.8 us
    pallas_call x1, Pallas kernels, forward_rows(): pl.pallas_call(functools.partial(forward_kernel, capacity), in_specs=[vec...  14.5 us
    all_to_all x2, starting transfers between devices, exchange_sums(): lax.all_to_all(chip, 'expert', split_axis=0, concat_axis=0, tiled=True, a...  11.1 us
    ppermute x3, waiting for transfers between devices, per_device(): far = [lax.ppermute(part, 'pipe', mirror) for part in give]  9.99 us
    all_to_all x2, waiting for transfers between devices, exchange_sums(): lax.all_to_all(chip, 'expert', split_axis=0, concat_axis=0, tiled=True, a...  9.48 us
    pallas_call x1, Pallas kernels, place_rows(): pl.pallas_call(functools.partial(place_kernel, capacity), grid_spec=pltpu...  7.19 us
  transfers between devices with their start and end apart: 10, of which 7 were waited for; matrix products, arithmetic and copies ran while one was open for 4% of the time, Pallas kernels for 34%

profile of v4, /device:TPU:9, one launch (start us, length us, event | category | flops | bytes accessed | tf_op | source)
XLA Modules:
  0.0 198.7 jit_solution(10693229819083453766)
XLA Ops:
  7.2 0.0 copy-start.7
  7.2 0.0 copy-start.8
  7.2 0.0 copy-start.9
  7.2 0.0 copy-start.10
  7.2 0.0 all-gather.6.cloned.1.call-start
  7.3 2.2 %normed.3 = bf16[2,128,1536]{2,1,0:T(8,128)(2,1)} custom-call(bf16[128,1536]{1,0:T(8,128)(2,1)} %x_ref.3, f32[1536]{0:T(1024)} %gain_ref.3, bf16[128,1536]{1,0:T(8,128)(2,1)} %refs_0_.1), custom_call_target="tpu_custom_call" | custom-call | flops 1000 | bytes 1000 | tf_op jit(solution)/shard_map/normed/pallas_call | solution.py:46
  9.5 0.0 all-gather.6.cloned.1.call-update
  9.5 0.0 all-gather.4.cloned.1.call-start
  9.5 1.9 normed.2
  11.5 0.0 all-gather.4.cloned.1.call-update
  11.5 0.0 copy-done.7
  11.5 0.0 copy-done.8
  11.5 0.0 copy-done.9
  11.5 0.0 copy-done.10
  11.6 0.6 maximum_bitcast_fusion
  12.2 5.6 %all-to-all-start = ((f32[8,2,2,128]{3,2,1,0:T(2,128)}), f32[8,2,2,128]{3,2,1,0:T(2,128)S(1)}, u32[]{:S(2)}, u32[]{:S(2)}) async-start(f32[8,2,2,128]{3,2,1,0:T(2,128)} %maximum_bitcast_fusion), calls=%async_computation | async-start | bytes 32768 | tf_op jit(solution)/shard_map/all_to_all | solution.py:513
  17.8 0.1 fusion.7
  17.9 0.1 fusion.8
  18.0 0.1 pad_add_fusion.1.sides_ref
  18.1 3.6 %all-to-all-done = f32[8,2,2,128]{3,2,1,0:T(2,128)S(1)} async-done(((f32[8,2,2,128]{3,2,1,0:T(2,128)}), f32[8,2,2,128]{3,2,1,0:T(2,128)S(1)}, u32[]{:S(2)}, u32[]{:S(2)}) %all-to-all-start) | async-done | bytes 16416 | tf_op jit(solution)/shard_map/all_to_all | solution.py:513
  21.7 0.6 slice_bitcast_fusion
  22.3 0.6 gather_fusion
  22.9 0.5 gather_fusion.1
  23.5 50.9 %all-gather.6.cloned.1.call-done = bf16[16,128,1536]{2,1,0:T(8,128)(2,1)} async-done(((bf16[2,128,1536]{2,1,0:T(8,128)(2,1)}), bf16[16,128,1536]{2,1,0:T(8,128)(2,1)}) %all-gather.6.cloned.1.call-update) | async-done | bytes 6291472 | tf_op jit(solution)/shard_map/all_gather | solution.py:518
  74.4 0.0 copy-start
  74.4 7.2 %place_rows.1 = (bf16[512,1536]{1,0:T(8,128)(2,1)}, bf16[512,1536]{1,0:T(8,128)(2,1)}, bf16[2,144,1536]{2,1,0:T(8,128)(2,1)}, bf16[2,112,1536]{2,1,0:T(8,128)(2,1)}, bf16[2,256,1536]{2,1,0:T(8,128)(2,1)}) custom-call(s32[2]{0:T(128)S(1)} %pad_add_fusion.1.sides_ref, bf16[4,2,2,128,1536]{4,3,2,1,0:T(8,128)(2,1)} %bitcast.46, ...), custom_call_target="tpu_custom_call" | custom-call | flops 1000 | bytes 1000 | tf_op jit(solution)/shard_map/place_rows/pallas_call | solution.py:141
  81.6 2.2 %collective-permute-start = (bf16[2,144,1536]{2,1,0:T(8,128)(2,1)}, bf16[2,144,1536]{2,1,0:T(8,128)(2,1)S(1)}, u32[]{:S(2)}, u32[]{:S(2)}) collective-permute-start(bf16[2,144,1536]{2,1,0:T(8,128)(2,1)} %get-tuple-element.26.give_1_ref), channel_id=1, source_target_pairs={{0,24},{8,16},{16,8},{24,0},{1,25},{9,17},{17,9},{25,1},{2,26},{10... | collective-permute-start | bytes 2654216 | tf_op jit(solution)/shard_map/ppermute | solution.py:525
  83.8 0.1 pad_add_fusion.which_ref
  83.9 0.0 copy-start.1
  83.9 0.0 copy-done
  83.9 20.8 %backward_rows.1 = (bf16[4,128,1536]{2,1,0:T(8,128)(2,1)}, bf16[4,128,1536]{2,1,0:T(8,128)(2,1)}, bf16[512,768]{1,0:T(8,128)(2,1)}, bf16[512,1536]{1,0:T(8,128)(2,1)}) custom-call(s32[2]{0:T(128)S(1)} %pad_add_fusion.which_ref, f32[16,128]{1,0:T(8,128)S(1)} %bitcast.41, bf16[512,1536]{1,0:T(8,128)(2,1)} %get-tuple-element.24.keep_c_ref.refs_0_, ...), custom_call_target="tpu_custom_call" | custom-call | flops 1000 | bytes 1000 | tf_op jit(solution)/shard_map/backward_rows/pallas_call | solution.py:296
  104.7 0.0 copy-done.1
  104.7 0.0 collective-permute-done.refs_4_
  104.7 0.0 copy-start.3
  104.7 0.7 collective-permute-start.1
  105.4 3.3 %collective-permute-done.1 = bf16[4,128,1536]{2,1,0:T(8,128)(2,1)S(1)} collective-permute-done((bf16[4,128,1536]{2,1,0:T(8,128)(2,1)}, bf16[4,128,1536]{2,1,0:T(8,128)(2,1)S(1)}, u32[]{:S(2)}, u32[]{:S(2)}) %collective-permute-start.1) | collective-permute-done | bytes 1572896 | tf_op jit(solution)/shard_map/ppermute | solution.py:476
  108.7 3.0 %add_convert_fusion = (bf16[4,64,1536]{2,1,0:T(8,128)(2,1)}, bf16[4,64,1536]{2,1,0:T(8,128)(2,1)}) fusion(bf16[4,128,1536]{2,1,0:T(8,128)(2,1)S(1)} %collective-permute-done.1, bf16[4,128,1536]{2,1,0:T(8,128)(2,1)} %get-tuple-element.29), kind=kLoop, calls=%fused_computation.3 | loop fusion | flops 3145728 | bytes 4718592 | tf_op jit(solution)/shard_map/convert_element_type | solution.py:534
  111.7 0.0 copy-done.3
  111.7 0.0 copy-start.4
  111.7 5.7 %all-to-all-start.1 = ((bf16[4,64,1536]{2,1,0:T(8,128)(2,1)}), bf16[4,64,1536]{2,1,0:T(8,128)(2,1)S(1)}, u32[]{:S(2)}, u32[]{:S(2)}) async-start(bf16[4,64,1536]{2,1,0:T(8,128)(2,1)} %get-tuple-element.45), calls=%async_computation.1 | async-start | bytes 1572864 | tf_op jit(solution)/shard_map/all_to_all | solution.py:482
  117.4 0.0 reduce-scatter.2.cloned.1.call-start
  117.4 0.0 copy-done.4
  117.4 1.9 collective-permute-start.2
  119.2 0.0 all-gather.4.cloned.1.call-done.tokens_ref
  119.2 14.5 %forward_rows.1 = bf16[8,128,1536]{2,1,0:T(8,128)(2,1)} custom-call(f32[16,128]{1,0:T(8,128)} %bitcast.49, bf16[8,128,1536]{2,1,0:T(8,128)(2,1)} %all-gather.4.cloned.1.call-done.tokens_ref, bf16[2,1536,1536]{2,1,0:T(8,128)(2,1)} %bitcast.36, bf16[2,768,1536]{2,1,0:T(8,128)(2,1)} %bitcast.43), custom_call_target="tpu_custom_call" | custom-call | flops 1000 | bytes 1000 | tf_op jit(solution)/shard_map/forward_rows/pallas_call | solution.py:378
  133.8 0.8 collective-permute-done.2.refs_5_
  134.6 0.0 all-to-all-done.1
  134.6 0.0 reduce-scatter.2.cloned.1.call-update
  134.6 0.8 copy-done.5
  135.4 5.4 %all-to-all-start.2 = ((bf16[4,64,1536]{2,1,0:T(8,128)(2,1)}), bf16[4,64,1536]{2,1,0:T(8,128)(2,1)S(1)}, u32[]{:S(2)}, u32[]{:S(2)}) async-start(bf16[4,64,1536]{2,1,0:T(8,128)(2,1)} %get-tuple-element.44), calls=%async_computation.3 | async-start | bytes 1572864 | tf_op jit(solution)/shard_map/all_to_all | solution.py:482
  140.9 1.9 collective-permute-start.3
  142.7 0.0 copy-done.2
  142.7 0.2 fusion.6
  142.9 13.3 %weight_gradients.2 = (bf16[1536,1536]{1,0:T(8,128)(2,1)}, bf16[768,1536]{1,0:T(8,128)(2,1)}) custom-call(s32[2]{0:T(128)} %copy-done.1, bf16[512,1536]{1,0:T(8,128)(2,1)} %get-tuple-element.24.keep_c_ref.refs_0_, bf16[512,1536]{1,0:T(8,128)(2,1)} %get-tuple-element.25.keep_h_ref.refs_1_, bf16[512,768]{1,0:T(8,128)(2,1)} %get-tuple-element.35.refs_2_, ...), custom_call_target="tpu_custom_call" | custom-call | flops 1000 | bytes 1000 | tf_op jit(solution)/shard_map/weight_gradients/pallas_call | solution.py:453
  156.2 0.0 copy-start.6
  156.2 0.1 convert_reduce_fusion.1
  156.4 9.5 %all-to-all-done.2 = bf16[4,64,1536]{2,1,0:T(8,128)(2,1)S(1)} async-done(((bf16[4,64,1536]{2,1,0:T(8,128)(2,1)}), bf16[4,64,1536]{2,1,0:T(8,128)(2,1)S(1)}, u32[]{:S(2)}, u32[]{:S(2)}) %all-to-all-start.2) | async-done | bytes 786464 | tf_op jit(solution)/shard_map/all_to_all | solution.py:482
  165.9 0.1 convert_reduce_fusion
  166.0 0.0 copy-done.6
  166.0 0.3 fusion.2
  166.2 1.0 fusion.5
  167.3 9.2 %collective-permute-done.3.refs_2_ = bf16[2,256,1536]{2,1,0:T(8,128)(2,1)} collective-permute-done((bf16[2,256,1536]{2,1,0:T(8,128)(2,1)}, bf16[2,256,1536]{2,1,0:T(8,128)(2,1)}, u32[]{:S(2)}, u32[]{:S(2)}) %collective-permute-start.3) | collective-permute-done | bytes 1572896 | tf_op jit(solution)/shard_map/ppermute | solution.py:525
  176.5 9.9 %weight_gradients.3 = (bf16[1536,1536]{1,0:T(8,128)(2,1)}, bf16[768,1536]{1,0:T(8,128)(2,1)}) custom-call(s32[2]{0:T(128)} %copy-done.1, bf16[1536,1536]{1,0:T(8,128)(2,1)} %get-tuple-element.39.refs_0_, bf16[768,1536]{1,0:T(8,128)(2,1)} %get-tuple-element.40.refs_1_, bf16[2,256,1536]{2,1,0:T(8,128)(2,1)} %collective-permute-done.3.refs_2_, ...), custom_call_target="tpu_custom_call" | custom-call | flops 1000 | bytes 1000 | tf_op jit(solution)/shard_map/weight_gradients/pallas_call | solution.py:453
  186.3 5.9 %reduce-scatter.2.cloned.1.call-done = bf16[128,1536]{1,0:T(8,128)(2,1)} async-done(((bf16[1024,1536]{1,0:T(8,128)(2,1)}), bf16[128,1536]{1,0:T(8,128)(2,1)}) %reduce-scatter.2.cloned.1.call-update) | async-done | bytes 393232 | tf_op jit(solution)/shard_map/reduce_scatter | solution.py:543
  (11 shorter events, 0.1 us)
Async XLA Ops:
  7.2 4.3 %copy-start.7 = (f32[128,6]{0,1:T(8,128)S(1)}, f32[128,6]{0,1:T(8,128)}, u32[]{:S(2)}) copy-start(f32[128,6]{0,1:T(8,128)} %param.14) | copy-start | bytes 9220
  7.2 4.3 %copy-start.8 = (s32[128,6]{0,1:T(8,128)S(1)}, s32[128,6]{0,1:T(8,128)}, u32[]{:S(2)}) copy-start(s32[128,6]{0,1:T(8,128)} %param.15) | copy-start | bytes 9220
  7.2 4.4 %copy-start.9 = (f32[128,6]{0,1:T(8,128)S(1)}, f32[128,6]{0,1:T(8,128)}, u32[]{:S(2)}) copy-start(f32[128,6]{0,1:T(8,128)} %param.11) | copy-start | bytes 9220
  7.2 4.4 %copy-start.10 = (s32[128,6]{0,1:T(8,128)S(1)}, s32[128,6]{0,1:T(8,128)}, u32[]{:S(2)}) copy-start(s32[128,6]{0,1:T(8,128)} %param.12) | copy-start | bytes 9220
  7.2 67.2 %all-gather.6.cloned.1.call-start = ((), (), s32[]{:S(2)}) async-start(), calls=%async_computation.6 | async-start | bytes 7077888 | tf_op jit(solution)/shard_map/all_gather | solution.py:518
  9.5 109.7 %all-gather.4.cloned.1.call-start = ((), (), s32[]{:S(2)}) async-start(), calls=%async_computation.4 | async-start | bytes 3538944 | tf_op jit(solution)/shard_map/all_gather | solution.py:521
  12.2 9.5 %all-to-all-start = ((f32[8,2,2,128]{3,2,1,0:T(2,128)}), f32[8,2,2,128]{3,2,1,0:T(2,128)S(1)}, u32[]{:S(2)}, u32[]{:S(2)}) async-start(f32[8,2,2,128]{3,2,1,0:T(2,128)} %maximum_bitcast_fusion), calls=%async_computation | async-start | bytes 32768 | tf_op jit(solution)/shard_map/all_to_all | solution.py:513
  74.4 9.5 %copy-start = (bf16[1,2,1536,1536]{3,2,1,0:T(8,128)(2,1)S(1)}, bf16[1,2,1536,1536]{3,2,1,0:T(8,128)(2,1)}, u32[]{:S(2)}) copy-start(bf16[1,2,1536,1536]{3,2,1,0:T(8,128)(2,1)} %param.18) | copy-start | bytes 28311556
  81.6 23.1 %collective-permute-start = (bf16[2,144,1536]{2,1,0:T(8,128)(2,1)}, bf16[2,144,1536]{2,1,0:T(8,128)(2,1)S(1)}, u32[]{:S(2)}, u32[]{:S(2)}) collective-permute-start(bf16[2,144,1536]{2,1,0:T(8,128)(2,1)} %get-tuple-element.26.give_1_ref), channel_id=1, source_target_pairs={{0,24},{8,16},{16,8},{24,0},{1,25},{9,17},{17,9},{25,1},{2,26},{10... | collective-permute-start | bytes 2654216 | tf_op jit(solution)/shard_map/ppermute | solution.py:525
  83.9 20.8 %copy-start.1 = (s32[2]{0:T(128)}, s32[2]{0:T(128)S(1)}, u32[]{:S(2)}) copy-start(s32[2]{0:T(128)S(1)} %pad_add_fusion.which_ref) | copy-start | bytes 28
  104.7 7.0 %copy-start.3 = (bf16[2,144,1536]{2,1,0:T(8,128)(2,1)}, bf16[2,144,1536]{2,1,0:T(8,128)(2,1)S(1)}, u32[]{:S(2)}) copy-start(bf16[2,144,1536]{2,1,0:T(8,128)(2,1)S(1)} %collective-permute-done.refs_4_) | copy-start | bytes 2654212
  104.7 4.0 %collective-permute-start.1 = (bf16[4,128,1536]{2,1,0:T(8,128)(2,1)}, bf16[4,128,1536]{2,1,0:T(8,128)(2,1)S(1)}, u32[]{:S(2)}, u32[]{:S(2)}) collective-permute-start(bf16[4,128,1536]{2,1,0:T(8,128)(2,1)} %get-tuple-element.31), channel_id=1, source_target_pairs={{0,1},{1,0},{2,3},{3,2},{4,5},{5,4},{6,7},{7,6},{8,9},{9,8},{10,11... | collective-permute-start | bytes 4718600 | tf_op jit(solution)/shard_map/ppermute | solution.py:476
  111.7 5.7 %copy-start.4 = (bf16[2,112,1536]{2,1,0:T(8,128)(2,1)S(1)}, bf16[2,112,1536]{2,1,0:T(8,128)(2,1)}, u32[]{:S(2)}) copy-start(bf16[2,112,1536]{2,1,0:T(8,128)(2,1)} %get-tuple-element.27.give_2_ref) | copy-start | bytes 2064388
  111.7 22.9 %all-to-all-start.1 = ((bf16[4,64,1536]{2,1,0:T(8,128)(2,1)}), bf16[4,64,1536]{2,1,0:T(8,128)(2,1)S(1)}, u32[]{:S(2)}, u32[]{:S(2)}) async-start(bf16[4,64,1536]{2,1,0:T(8,128)(2,1)} %get-tuple-element.45), calls=%async_computation.1 | async-start | bytes 1572864 | tf_op jit(solution)/shard_map/all_to_all | solution.py:482
  117.4 74.8 %reduce-scatter.2.cloned.1.call-start = ((), (), s32[]{:S(2)}) async-start(), calls=%async_computation.5 | async-start | bytes 3538944 | tf_op jit(solution)/shard_map/reduce_scatter | solution.py:543
  117.4 17.2 %collective-permute-start.2 = (bf16[2,112,1536]{2,1,0:T(8,128)(2,1)S(1)}, bf16[2,112,1536]{2,1,0:T(8,128)(2,1)S(1)}, u32[]{:S(2)}, u32[]{:S(2)}) collective-permute-start(bf16[2,112,1536]{2,1,0:T(8,128)(2,1)S(1)} %copy-done.4), channel_id=1, source_target_pairs={{0,24},{8,16},{16,8},{24,0},{1,25},{9,17},{17,9},{25,1},{2,26},{10... | collective-permute-start | bytes 2064392 | tf_op jit(solution)/shard_map/ppermute | solution.py:525
  134.6 0.8 copy-start.5
  135.4 7.3 %copy-start.2 = (bf16[128,1536]{1,0:T(8,128)(2,1)S(1)}, bf16[128,1536]{1,0:T(8,128)(2,1)}, u32[]{:S(2)}) copy-start(bf16[128,1536]{1,0:T(8,128)(2,1)} %x_ref.3) | copy-start | bytes 1179652
  135.4 30.4 %all-to-all-start.2 = ((bf16[4,64,1536]{2,1,0:T(8,128)(2,1)}), bf16[4,64,1536]{2,1,0:T(8,128)(2,1)S(1)}, u32[]{:S(2)}, u32[]{:S(2)}) async-start(bf16[4,64,1536]{2,1,0:T(8,128)(2,1)} %get-tuple-element.44), calls=%async_computation.3 | async-start | bytes 1572864 | tf_op jit(solution)/shard_map/all_to_all | solution.py:482
  140.9 35.6 %collective-permute-start.3 = (bf16[2,256,1536]{2,1,0:T(8,128)(2,1)}, bf16[2,256,1536]{2,1,0:T(8,128)(2,1)}, u32[]{:S(2)}, u32[]{:S(2)}) collective-permute-start(bf16[2,256,1536]{2,1,0:T(8,128)(2,1)} %get-tuple-element.28.give_3_ref), channel_id=1, source_target_pairs={{0,24},{8,16},{16,8},{24,0},{1,25},{9,17},{17,9},{25,1},{2,26},{10... | collective-permute-start | bytes 4718600 | tf_op jit(solution)/shard_map/ppermute | solution.py:525
  156.2 9.7 %copy-start.6 = (f32[1536]{0:T(1024)S(1)}, f32[1536]{0:T(1024)}, u32[]{:S(2)}) copy-start(f32[1536]{0:T(1024)} %gain_ref.3) | copy-start | bytes 18436
Sparse Core Ops, SparseCore 0:
  10.3 64.1 all-gather.5
  76.6 38.1 all-gather.3
  134.7 57.4 reduce-scatter.1

commit v5 on v4

--- a/solution.py
+++ b/solution.py
@@ -204,6 +204,7 @@
         copies.wait(("gu", key, start))
         gate_pre = dot(h(), gu[:, cols])
         up_pre = dot(h(), gu[:, up_cols])
+        copies.wait("c%d" % key)
         copies.wait(("dn", key, start))
         back = dot(c(), dn[cols, :], ((1,), (1,)))
         squash = 1.0 / (1.0 + jnp.exp(-gate_pre))
@@ -248,6 +249,7 @@
     copies.start("h0", keep_h_ref, h.at[0])
     copies.start("c0", keep_c_ref, c.at[0])
     down_copies(copies, 0, which_ref[0], dn_ref, dn)
+    copies.wait("h0")
     for send, there, part in overlaps(row_count, 0, row_count):
         give_ref = (give_1_ref, give_2_ref, give_3_ref)[send]
         copies.start("c1", give_ref.at[0, there], c.at[1, part])
@@ -256,7 +258,6 @@
     for expert in range(2):
         source = which_ref[expert]
         copies.wait("h%d" % expert)
-        copies.wait("c%d" % expert)
         hidden_gradients(
             copies,
             expert,

time: 199 us -> 199 us (level)
  no operation moved by 1% of the time
where the time goes in v5:
time: 199 us; the launch traced here: 198 us
  waiting for transfers between devices  82.6 us (42%)
  Pallas kernels  69.3 us (35%)
  starting transfers between devices  24.3 us (12%)
  between operations  13.9 us (7%)
  other arithmetic  5.63 us (3%)
  local copies, waits for them, and re-layouts  2.6 us (1%)
    all_gather x1, waiting for transfers between devices, per_device(): lax.all_gather(normed(x_bwd, norm_gain, cotangent)[None], 'expert', axis=...  50.9 us
    pallas_call x2, Pallas kernels, weight_gradients(): pl.pallas_call(functools.partial(gradient_kernel, near_rows, len(sends)),...  23.2 us
    pallas_call x1, Pallas kernels, backward_rows(): pl.pallas_call(functools.partial(backward_kernel, capacity), in_specs=[sc...  20.2 us
    pallas_call x1, Pallas kernels, forward_rows(): pl.pallas_call(functools.partial(forward_kernel, capacity), in_specs=[vec...  14.5 us
    all_to_all x2, starting transfers between devices, exchange_sums(): lax.all_to_all(chip, 'expert', split_axis=0, concat_axis=0, tiled=True, a...  11.5 us
    ppermute x3, waiting for transfers between devices, per_device(): far = [lax.ppermute(part, 'pipe', mirror) for part in give]  10.5 us
    all_to_all x2, waiting for transfers between devices, exchange_sums(): lax.all_to_all(chip, 'expert', split_axis=0, concat_axis=0, tiled=True, a...  8.51 us
    pallas_call x1, Pallas kernels, place_rows(): pl.pallas_call(functools.partial(place_kernel, capacity), grid_spec=pltpu...  7.19 us
  transfers between devices with their start and end apart: 10, of which 7 were waited for; matrix products, arithmetic and copies ran while one was open for 4% of the time, Pallas kernels for 34%

profile of v5, /device:TPU:9, one launch (start us, length us, event | category | flops | bytes accessed | tf_op | source)
XLA Modules:
  0.0 198.4 jit_solution(11978494708579630264)
XLA Ops:
  7.2 0.0 copy-start.7
  7.2 0.0 copy-start.8
  7.2 0.0 copy-start.9
  7.2 0.0 copy-start.10
  7.2 0.0 all-gather.6.cloned.1.call-start
  7.3 2.2 %normed.3 = bf16[2,128,1536]{2,1,0:T(8,128)(2,1)} custom-call(bf16[128,1536]{1,0:T(8,128)(2,1)} %x_ref.3, f32[1536]{0:T(1024)} %gain_ref.3, bf16[128,1536]{1,0:T(8,128)(2,1)} %refs_0_.1), custom_call_target="tpu_custom_call" | custom-call | flops 1000 | bytes 1000 | tf_op jit(solution)/shard_map/normed/pallas_call | solution.py:46
  9.5 0.0 all-gather.6.cloned.1.call-update
  9.5 0.0 all-gather.4.cloned.1.call-start
  9.5 1.9 normed.2
  11.5 0.0 all-gather.4.cloned.1.call-update
  11.5 0.0 copy-done.7
  11.5 0.0 copy-done.8
  11.5 0.0 copy-done.9
  11.5 0.0 copy-done.10
  11.6 0.6 maximum_bitcast_fusion
  12.2 5.6 %all-to-all-start = ((f32[8,2,2,128]{3,2,1,0:T(2,128)}), f32[8,2,2,128]{3,2,1,0:T(2,128)S(1)}, u32[]{:S(2)}, u32[]{:S(2)}) async-start(f32[8,2,2,128]{3,2,1,0:T(2,128)} %maximum_bitcast_fusion), calls=%async_computation | async-start | bytes 32768 | tf_op jit(solution)/shard_map/all_to_all | solution.py:514
  17.8 0.1 fusion.7
  17.9 0.1 fusion.8
  18.0 0.1 pad_add_fusion.1.sides_ref
  18.1 3.6 %all-to-all-done = f32[8,2,2,128]{3,2,1,0:T(2,128)S(1)} async-done(((f32[8,2,2,128]{3,2,1,0:T(2,128)}), f32[8,2,2,128]{3,2,1,0:T(2,128)S(1)}, u32[]{:S(2)}, u32[]{:S(2)}) %all-to-all-start) | async-done | bytes 16416 | tf_op jit(solution)/shard_map/all_to_all | solution.py:514
  21.7 0.6 slice_bitcast_fusion
  22.3 0.6 gather_fusion
  22.9 0.5 gather_fusion.1
  23.5 50.9 %all-gather.6.cloned.1.call-done = bf16[16,128,1536]{2,1,0:T(8,128)(2,1)} async-done(((bf16[2,128,1536]{2,1,0:T(8,128)(2,1)}), bf16[16,128,1536]{2,1,0:T(8,128)(2,1)}) %all-gather.6.cloned.1.call-update) | async-done | bytes 6291472 | tf_op jit(solution)/shard_map/all_gather | solution.py:519
  74.4 0.0 copy-start
  74.4 7.2 %place_rows.1 = (bf16[512,1536]{1,0:T(8,128)(2,1)}, bf16[512,1536]{1,0:T(8,128)(2,1)}, bf16[2,144,1536]{2,1,0:T(8,128)(2,1)}, bf16[2,112,1536]{2,1,0:T(8,128)(2,1)}, bf16[2,256,1536]{2,1,0:T(8,128)(2,1)}) custom-call(s32[2]{0:T(128)S(1)} %pad_add_fusion.1.sides_ref, bf16[4,2,2,128,1536]{4,3,2,1,0:T(8,128)(2,1)} %bitcast.46, ...), custom_call_target="tpu_custom_call" | custom-call | flops 1000 | bytes 1000 | tf_op jit(solution)/shard_map/place_rows/pallas_call | solution.py:141
  81.6 2.2 %collective-permute-start = (bf16[2,144,1536]{2,1,0:T(8,128)(2,1)}, bf16[2,144,1536]{2,1,0:T(8,128)(2,1)S(1)}, u32[]{:S(2)}, u32[]{:S(2)}) collective-permute-start(bf16[2,144,1536]{2,1,0:T(8,128)(2,1)} %get-tuple-element.26.give_1_ref), channel_id=1, source_target_pairs={{0,24},{8,16},{16,8},{24,0},{1,25},{9,17},{17,9},{25,1},{2,26},{10... | collective-permute-start | bytes 2654216 | tf_op jit(solution)/shard_map/ppermute | solution.py:526
  83.8 0.1 pad_add_fusion.which_ref
  83.9 0.0 copy-start.1
  83.9 0.0 copy-done
  83.9 20.2 %backward_rows.1 = (bf16[4,128,1536]{2,1,0:T(8,128)(2,1)}, bf16[4,128,1536]{2,1,0:T(8,128)(2,1)}, bf16[512,768]{1,0:T(8,128)(2,1)}, bf16[512,1536]{1,0:T(8,128)(2,1)}) custom-call(s32[2]{0:T(128)S(1)} %pad_add_fusion.which_ref, f32[16,128]{1,0:T(8,128)S(1)} %bitcast.41, bf16[512,1536]{1,0:T(8,128)(2,1)} %get-tuple-element.24.keep_c_ref.refs_0_, ...), custom_call_target="tpu_custom_call" | custom-call | flops 1000 | bytes 1000 | tf_op jit(solution)/shard_map/backward_rows/pallas_call | solution.py:297
  104.1 0.0 copy-done.1
  104.1 0.0 collective-permute-done.refs_4_
  104.1 0.0 copy-start.3
  104.1 0.7 collective-permute-start.1
  104.8 3.2 %collective-permute-done.1 = bf16[4,128,1536]{2,1,0:T(8,128)(2,1)S(1)} collective-permute-done((bf16[4,128,1536]{2,1,0:T(8,128)(2,1)}, bf16[4,128,1536]{2,1,0:T(8,128)(2,1)S(1)}, u32[]{:S(2)}, u32[]{:S(2)}) %collective-permute-start.1) | collective-permute-done | bytes 1572896 | tf_op jit(solution)/shard_map/ppermute | solution.py:477
  108.1 3.0 %add_convert_fusion = (bf16[4,64,1536]{2,1,0:T(8,128)(2,1)}, bf16[4,64,1536]{2,1,0:T(8,128)(2,1)}) fusion(bf16[4,128,1536]{2,1,0:T(8,128)(2,1)S(1)} %collective-permute-done.1, bf16[4,128,1536]{2,1,0:T(8,128)(2,1)} %get-tuple-element.29), kind=kLoop, calls=%fused_computation.3 | loop fusion | flops 3145728 | bytes 4718592 | tf_op jit(solution)/shard_map/convert_element_type | solution.py:535
  111.1 0.0 copy-done.3
  111.1 0.0 copy-start.4
  111.1 6.1 %all-to-all-start.1 = ((bf16[4,64,1536]{2,1,0:T(8,128)(2,1)}), bf16[4,64,1536]{2,1,0:T(8,128)(2,1)S(1)}, u32[]{:S(2)}, u32[]{:S(2)}) async-start(bf16[4,64,1536]{2,1,0:T(8,128)(2,1)} %get-tuple-element.45), calls=%async_computation.1 | async-start | bytes 1572864 | tf_op jit(solution)/shard_map/all_to_all | solution.py:483
  117.1 0.0 reduce-scatter.2.cloned.1.call-start
  117.1 0.0 copy-done.4
  117.1 2.1 %collective-permute-start.2 = (bf16[2,112,1536]{2,1,0:T(8,128)(2,1)S(1)}, bf16[2,112,1536]{2,1,0:T(8,128)(2,1)S(1)}, u32[]{:S(2)}, u32[]{:S(2)}) collective-permute-start(bf16[2,112,1536]{2,1,0:T(8,128)(2,1)S(1)} %copy-done.4), channel_id=1, source_target_pairs={{0,24},{8,16},{16,8},{24,0},{1,25},{9,17},{17,9},{25,1},{2,26},{10... | collective-permute-start | bytes 2064392 | tf_op jit(solution)/shard_map/ppermute | solution.py:526
  119.2 0.0 all-gather.4.cloned.1.call-done.tokens_ref
  119.2 14.5 %forward_rows.1 = bf16[8,128,1536]{2,1,0:T(8,128)(2,1)} custom-call(f32[16,128]{1,0:T(8,128)} %bitcast.49, bf16[8,128,1536]{2,1,0:T(8,128)(2,1)} %all-gather.4.cloned.1.call-done.tokens_ref, bf16[2,1536,1536]{2,1,0:T(8,128)(2,1)} %bitcast.36, bf16[2,768,1536]{2,1,0:T(8,128)(2,1)} %bitcast.43), custom_call_target="tpu_custom_call" | custom-call | flops 1000 | bytes 1000 | tf_op jit(solution)/shard_map/forward_rows/pallas_call | solution.py:379
  133.8 0.6 collective-permute-done.2.refs_5_
  134.3 0.0 all-to-all-done.1
  134.3 0.0 reduce-scatter.2.cloned.1.call-update
  134.4 0.8 copy-done.5
  135.2 5.4 %all-to-all-start.2 = ((bf16[4,64,1536]{2,1,0:T(8,128)(2,1)}), bf16[4,64,1536]{2,1,0:T(8,128)(2,1)S(1)}, u32[]{:S(2)}, u32[]{:S(2)}) async-start(bf16[4,64,1536]{2,1,0:T(8,128)(2,1)} %get-tuple-element.44), calls=%async_computation.3 | async-start | bytes 1572864 | tf_op jit(solution)/shard_map/all_to_all | solution.py:483
  140.6 2.1 %collective-permute-start.3 = (bf16[2,256,1536]{2,1,0:T(8,128)(2,1)}, bf16[2,256,1536]{2,1,0:T(8,128)(2,1)}, u32[]{:S(2)}, u32[]{:S(2)}) collective-permute-start(bf16[2,256,1536]{2,1,0:T(8,128)(2,1)} %get-tuple-element.28.give_3_ref), channel_id=1, source_target_pairs={{0,24},{8,16},{16,8},{24,0},{1,25},{9,17},{17,9},{25,1},{2,26},{10... | collective-permute-start | bytes 4718600 | tf_op jit(solution)/shard_map/ppermute | solution.py:526
  142.7 0.0 copy-done.2
  142.7 0.2 fusion.6
  142.9 13.3 %weight_gradients.2 = (bf16[1536,1536]{1,0:T(8,128)(2,1)}, bf16[768,1536]{1,0:T(8,128)(2,1)}) custom-call(s32[2]{0:T(128)} %copy-done.1, bf16[512,1536]{1,0:T(8,128)(2,1)} %get-tuple-element.24.keep_c_ref.refs_0_, bf16[512,1536]{1,0:T(8,128)(2,1)} %get-tuple-element.25.keep_h_ref.refs_1_, bf16[512,768]{1,0:T(8,128)(2,1)} %get-tuple-element.35.refs_2_, ...), custom_call_target="tpu_custom_call" | custom-call | flops 1000 | bytes 1000 | tf_op jit(solution)/shard_map/weight_gradients/pallas_call | solution.py:454
  156.2 0.0 copy-start.6
  156.2 0.1 convert_reduce_fusion.1
  156.4 8.5 %all-to-all-done.2 = bf16[4,64,1536]{2,1,0:T(8,128)(2,1)S(1)} async-done(((bf16[4,64,1536]{2,1,0:T(8,128)(2,1)}), bf16[4,64,1536]{2,1,0:T(8,128)(2,1)S(1)}, u32[]{:S(2)}, u32[]{:S(2)}) %all-to-all-start.2) | async-done | bytes 786464 | tf_op jit(solution)/shard_map/all_to_all | solution.py:483
  164.9 0.1 convert_reduce_fusion
  165.0 0.0 copy-done.6
  165.0 0.3 fusion.2
  165.3 1.0 fusion.5
  166.3 9.9 %collective-permute-done.3.refs_2_ = bf16[2,256,1536]{2,1,0:T(8,128)(2,1)} collective-permute-done((bf16[2,256,1536]{2,1,0:T(8,128)(2,1)}, bf16[2,256,1536]{2,1,0:T(8,128)(2,1)}, u32[]{:S(2)}, u32[]{:S(2)}) %collective-permute-start.3) | collective-permute-done | bytes 1572896 | tf_op jit(solution)/shard_map/ppermute | solution.py:526
  176.2 9.9 %weight_gradients.3 = (bf16[1536,1536]{1,0:T(8,128)(2,1)}, bf16[768,1536]{1,0:T(8,128)(2,1)}) custom-call(s32[2]{0:T(128)} %copy-done.1, bf16[1536,1536]{1,0:T(8,128)(2,1)} %get-tuple-element.39.refs_0_, bf16[768,1536]{1,0:T(8,128)(2,1)} %get-tuple-element.40.refs_1_, bf16[2,256,1536]{2,1,0:T(8,128)(2,1)} %collective-permute-done.3.refs_2_, ...), custom_call_target="tpu_custom_call" | custom-call | flops 1000 | bytes 1000 | tf_op jit(solution)/shard_map/weight_gradients/pallas_call | solution.py:454
  186.1 5.7 %reduce-scatter.2.cloned.1.call-done = bf16[128,1536]{1,0:T(8,128)(2,1)} async-done(((bf16[1024,1536]{1,0:T(8,128)(2,1)}), bf16[128,1536]{1,0:T(8,128)(2,1)}) %reduce-scatter.2.cloned.1.call-update) | async-done | bytes 393232 | tf_op jit(solution)/shard_map/reduce_scatter | solution.py:544
  (11 shorter events, 0.1 us)
Async XLA Ops:
  7.2 4.3 %copy-start.7 = (f32[128,6]{0,1:T(8,128)S(1)}, f32[128,6]{0,1:T(8,128)}, u32[]{:S(2)}) copy-start(f32[128,6]{0,1:T(8,128)} %param.14) | copy-start | bytes 9220
  7.2 4.3 %copy-start.8 = (s32[128,6]{0,1:T(8,128)S(1)}, s32[128,6]{0,1:T(8,128)}, u32[]{:S(2)}) copy-start(s32[128,6]{0,1:T(8,128)} %param.15) | copy-start | bytes 9220
  7.2 4.4 %copy-start.9 = (f32[128,6]{0,1:T(8,128)S(1)}, f32[128,6]{0,1:T(8,128)}, u32[]{:S(2)}) copy-start(f32[128,6]{0,1:T(8,128)} %param.11) | copy-start | bytes 9220
  7.2 4.4 %copy-start.10 = (s32[128,6]{0,1:T(8,128)S(1)}, s32[128,6]{0,1:T(8,128)}, u32[]{:S(2)}) copy-start(s32[128,6]{0,1:T(8,128)} %param.12) | copy-start | bytes 9220
  7.2 67.2 %all-gather.6.cloned.1.call-start = ((), (), s32[]{:S(2)}) async-start(), calls=%async_computation.6 | async-start | bytes 7077888 | tf_op jit(solution)/shard_map/all_gather | solution.py:519
  9.5 109.7 %all-gather.4.cloned.1.call-start = ((), (), s32[]{:S(2)}) async-start(), calls=%async_computation.4 | async-start | bytes 3538944 | tf_op jit(solution)/shard_map/all_gather | solution.py:522
  12.2 9.5 %all-to-all-start = ((f32[8,2,2,128]{3,2,1,0:T(2,128)}), f32[8,2,2,128]{3,2,1,0:T(2,128)S(1)}, u32[]{:S(2)}, u32[]{:S(2)}) async-start(f32[8,2,2,128]{3,2,1,0:T(2,128)} %maximum_bitcast_fusion), calls=%async_computation | async-start | bytes 32768 | tf_op jit(solution)/shard_map/all_to_all | solution.py:514
  74.4 9.5 %copy-start = (bf16[1,2,1536,1536]{3,2,1,0:T(8,128)(2,1)S(1)}, bf16[1,2,1536,1536]{3,2,1,0:T(8,128)(2,1)}, u32[]{:S(2)}) copy-start(bf16[1,2,1536,1536]{3,2,1,0:T(8,128)(2,1)} %param.18) | copy-start | bytes 28311556
  81.6 22.5 %collective-permute-start = (bf16[2,144,1536]{2,1,0:T(8,128)(2,1)}, bf16[2,144,1536]{2,1,0:T(8,128)(2,1)S(1)}, u32[]{:S(2)}, u32[]{:S(2)}) collective-permute-start(bf16[2,144,1536]{2,1,0:T(8,128)(2,1)} %get-tuple-element.26.give_1_ref), channel_id=1, source_target_pairs={{0,24},{8,16},{16,8},{24,0},{1,25},{9,17},{17,9},{25,1},{2,26},{10... | collective-permute-start | bytes 2654216 | tf_op jit(solution)/shard_map/ppermute | solution.py:526
  83.9 20.2 %copy-start.1 = (s32[2]{0:T(128)}, s32[2]{0:T(128)S(1)}, u32[]{:S(2)}) copy-start(s32[2]{0:T(128)S(1)} %pad_add_fusion.which_ref) | copy-start | bytes 28
  104.1 6.9 %copy-start.3 = (bf16[2,144,1536]{2,1,0:T(8,128)(2,1)}, bf16[2,144,1536]{2,1,0:T(8,128)(2,1)S(1)}, u32[]{:S(2)}) copy-start(bf16[2,144,1536]{2,1,0:T(8,128)(2,1)S(1)} %collective-permute-done.refs_4_) | copy-start | bytes 2654212
  104.1 4.0 %collective-permute-start.1 = (bf16[4,128,1536]{2,1,0:T(8,128)(2,1)}, bf16[4,128,1536]{2,1,0:T(8,128)(2,1)S(1)}, u32[]{:S(2)}, u32[]{:S(2)}) collective-permute-start(bf16[4,128,1536]{2,1,0:T(8,128)(2,1)} %get-tuple-element.31), channel_id=1, source_target_pairs={{0,1},{1,0},{2,3},{3,2},{4,5},{5,4},{6,7},{7,6},{8,9},{9,8},{10,11... | collective-permute-start | bytes 4718600 | tf_op jit(solution)/shard_map/ppermute | solution.py:477
  111.1 6.1 %copy-start.4 = (bf16[2,112,1536]{2,1,0:T(8,128)(2,1)S(1)}, bf16[2,112,1536]{2,1,0:T(8,128)(2,1)}, u32[]{:S(2)}) copy-start(bf16[2,112,1536]{2,1,0:T(8,128)(2,1)} %get-tuple-element.27.give_2_ref) | copy-start | bytes 2064388
  111.1 23.3 %all-to-all-start.1 = ((bf16[4,64,1536]{2,1,0:T(8,128)(2,1)}), bf16[4,64,1536]{2,1,0:T(8,128)(2,1)S(1)}, u32[]{:S(2)}, u32[]{:S(2)}) async-start(bf16[4,64,1536]{2,1,0:T(8,128)(2,1)} %get-tuple-element.45), calls=%async_computation.1 | async-start | bytes 1572864 | tf_op jit(solution)/shard_map/all_to_all | solution.py:483
  117.1 74.7 %reduce-scatter.2.cloned.1.call-start = ((), (), s32[]{:S(2)}) async-start(), calls=%async_computation.5 | async-start | bytes 3538944 | tf_op jit(solution)/shard_map/reduce_scatter | solution.py:544
  117.1 17.2 %collective-permute-start.2 = (bf16[2,112,1536]{2,1,0:T(8,128)(2,1)S(1)}, bf16[2,112,1536]{2,1,0:T(8,128)(2,1)S(1)}, u32[]{:S(2)}, u32[]{:S(2)}) collective-permute-start(bf16[2,112,1536]{2,1,0:T(8,128)(2,1)S(1)} %copy-done.4), channel_id=1, source_target_pairs={{0,24},{8,16},{16,8},{24,0},{1,25},{9,17},{17,9},{25,1},{2,26},{10... | collective-permute-start | bytes 2064392 | tf_op jit(solution)/shard_map/ppermute | solution.py:526
  134.3 0.8 copy-start.5
  135.2 7.5 %copy-start.2 = (bf16[128,1536]{1,0:T(8,128)(2,1)S(1)}, bf16[128,1536]{1,0:T(8,128)(2,1)}, u32[]{:S(2)}) copy-start(bf16[128,1536]{1,0:T(8,128)(2,1)} %x_ref.3) | copy-start | bytes 1179652
  135.2 29.7 %all-to-all-start.2 = ((bf16[4,64,1536]{2,1,0:T(8,128)(2,1)}), bf16[4,64,1536]{2,1,0:T(8,128)(2,1)S(1)}, u32[]{:S(2)}, u32[]{:S(2)}) async-start(bf16[4,64,1536]{2,1,0:T(8,128)(2,1)} %get-tuple-element.44), calls=%async_computation.3 | async-start | bytes 1572864 | tf_op jit(solution)/shard_map/all_to_all | solution.py:483
  140.6 35.6 %collective-permute-start.3 = (bf16[2,256,1536]{2,1,0:T(8,128)(2,1)}, bf16[2,256,1536]{2,1,0:T(8,128)(2,1)}, u32[]{:S(2)}, u32[]{:S(2)}) collective-permute-start(bf16[2,256,1536]{2,1,0:T(8,128)(2,1)} %get-tuple-element.28.give_3_ref), channel_id=1, source_target_pairs={{0,24},{8,16},{16,8},{24,0},{1,25},{9,17},{17,9},{25,1},{2,26},{10... | collective-permute-start | bytes 4718600 | tf_op jit(solution)/shard_map/ppermute | solution.py:526
  156.2 8.8 %copy-start.6 = (f32[1536]{0:T(1024)S(1)}, f32[1536]{0:T(1024)}, u32[]{:S(2)}) copy-start(f32[1536]{0:T(1024)} %gain_ref.3) | copy-start | bytes 18436
Sparse Core Ops, SparseCore 0:
  10.3 64.1 all-gather.5
  76.6 38.1 all-gather.3
  134.5 57.2 reduce-scatter.1

commit v6 on v5

--- a/solution.py
+++ b/solution.py
@@ -237,9 +237,13 @@
         store(group, dot(onehot, rows_ref[group]).astype(jnp.bfloat16))
 
 
+def token_halves(token_count):
+    return (slice(0, token_count // 2), slice(token_count // 2, token_count))
+
+
 def backward_kernel(
     capacity, which_ref, gates_ref, keep_c_ref, keep_h_ref, give_1_ref, give_2_ref, give_3_ref,
-    gu, dn_ref, own_ref, other_ref, hidden_out, d_out,
+    gu, dn_ref, own_ref, other_1_ref, other_2_ref, hidden_out, d_out,
     c, h, dn, hidden, d, dh, sums, sems,
 ):
     row_count, width = keep_c_ref.shape
@@ -280,8 +284,11 @@
 
     def store(group, value):
         sums[group] = value
-        target = own_ref if group < half else other_ref
-        copies.start("out", sums.at[group], target.at[group % half])
+        if group < half:
+            copies.start("out", sums.at[group], own_ref.at[group])
+        else:
+            for part, target in zip(token_halves(sums.shape[1]), (other_1_ref, other_2_ref)):
+                copies.start("out", sums.at[group, part], target.at[group - half])
 
     combine(gates_ref[...], dh, capacity, store)
     copies.wait_all()
@@ -293,14 +300,16 @@
     group_count = row_count // capacity
     token_count = gates.shape[-1]
     half = (group_count // 2, token_count, width)
+    quarter = (group_count // 2, token_count // 2, width)
     bf16 = jnp.bfloat16
     return pl.pallas_call(
         functools.partial(backward_kernel, capacity),
         in_specs=[scalar, vector] + [anywhere] * 5 + [vector, anywhere],
-        out_specs=[anywhere] * 4,
+        out_specs=[anywhere] * 5,
         out_shape=[
             pltpu.HBM(half, bf16),
-            pltpu.HBM(half, bf16),
+            pltpu.HBM(quarter, bf16),
+            pltpu.HBM(quarter, bf16),
             pltpu.HBM((row_count, hidden_units), bf16),
             pltpu.HBM((row_count, 2 * hidden_units), bf16),
         ],
@@ -312,7 +321,7 @@
             pltpu.VMEM((2, row_count, 2 * hidden_units), bf16),
             pltpu.VMEM((group_count, 2 * capacity, width), bf16),
             pltpu.VMEM((group_count, token_count, width), bf16),
-            pltpu.SemaphoreType.DMA((10 + 2 * (hidden_units // tile) + group_count,)),
+            pltpu.SemaphoreType.DMA((10 + 2 * (hidden_units // tile) + 3 * group_count // 2,)),
         ],
         compiler_params=kernel_params(shared_vmem_bytes),
         cost_estimate=light(),
@@ -525,19 +534,14 @@
     keep_c, keep_h, *give = place_rows(gathered_bwd, gates_b, sides, capacity)
     far = [lax.ppermute(part, "pipe", mirror) for part in give]
 
-    own_dh, other_dh, keep_hidden, keep_d = backward_rows(
+    own_dh, *other_dh, keep_hidden, keep_d = backward_rows(
         keep_c, keep_h, give, weight_gu, weight_dn, gates_b, which, capacity
     )
-    other_dh, far[0] = lax.optimization_barrier((other_dh, far[0]))
-    other_dh = swap_cores(other_dh)
-    middle = token_count // 2
-    chip_dh = [
-        (own_dh[:, part].astype(jnp.float32) + other_dh[:, part].astype(jnp.float32)).astype(
-            jnp.bfloat16
-        )
-        for part in (slice(0, middle), slice(middle, token_count))
-    ]
-    parts_dh = [exchange_sums(chip) for chip in chip_dh]
+    other_dh[0], far[0] = lax.optimization_barrier((other_dh[0], far[0]))
+    parts_dh = []
+    for part, other in zip(token_halves(token_count), other_dh):
+        chip_dh = own_dh[:, part].astype(jnp.float32) + swap_cores(other).astype(jnp.float32)
+        parts_dh.append(exchange_sums(chip_dh.astype(jnp.bfloat16)))
 
     partial_y = forward_rows(gathered_fwd, gates_f, weight_gu, weight_dn, capacity)
     partial_y, parts_dh[0], far[1] = lax.optimization_barrier((partial_y, parts_dh[0], far[1]))

time: 199 us -> 199 us (level)
  starting transfers between devices: 24.3 us -> 22.2 us
    all_to_all x2, waiting for transfers between devices: 8.51 us -> 12.9 us  [exchange_sums(): lax.all_to_all(chip, 'expert', split_axis=0, concat_axis=0, tiled=True, a...]
    ppermute x3, waiting for transfers between devices: 10.5 us -> 8.18 us  [per_device(): far = [lax.ppermute(part, 'pipe', mirror) for part in give]]
    ppermute x3, starting transfers between devices: 6.4 us -> 4.31 us  [per_device(): far = [lax.ppermute(part, 'pipe', mirror) for part in give]]
  transfers between devices with their start and end apart: 10 -> 11, of which waited for: 7 -> 8; matrix products, arithmetic and copies ran while one was open for 4% -> 4% of each run, Pallas kernels for 34% -> 34%
where the time goes in v6:
time: 199 us; the launch traced here: 198 us
  waiting for transfers between devices  84.4 us (42%)
  Pallas kernels  69.3 us (35%)
  starting transfers between devices  22.2 us (11%)
  between operations  13.9 us (7%)
  other arithmetic  5.59 us (3%)
  local copies, waits for them, and re-layouts  2.67 us (1%)
    all_gather x1, waiting for transfers between devices, per_device(): lax.all_gather(normed(x_bwd, norm_gain, cotangent)[None], 'expert', axis=...  50.9 us
    pallas_call x2, Pallas kernels, weight_gradients(): pl.pallas_call(functools.partial(gradient_kernel, near_rows, len(sends)),...  23.2 us
    pallas_call x1, Pallas kernels, backward_rows(): pl.pallas_call(functools.partial(backward_kernel, capacity), in_specs=[sc...  20.2 us
    pallas_call x1, Pallas kernels, forward_rows(): pl.pallas_call(functools.partial(forward_kernel, capacity), in_specs=[vec...  14.6 us
    all_to_all x2, waiting for transfers between devices, exchange_sums(): lax.all_to_all(chip, 'expert', split_axis=0, concat_axis=0, tiled=True, a...  12.9 us
    all_to_all x2, starting transfers between devices, exchange_sums(): lax.all_to_all(chip, 'expert', split_axis=0, concat_axis=0, tiled=True, a...  11.5 us
    ppermute x3, waiting for transfers between devices, per_device(): far = [lax.ppermute(part, 'pipe', mirror) for part in give]  8.18 us
    pallas_call x1, Pallas kernels, place_rows(): pl.pallas_call(functools.partial(place_kernel, capacity), grid_spec=pltpu...  7.19 us
  transfers between devices with their start and end apart: 11, of which 8 were waited for; matrix products, arithmetic and copies ran while one was open for 4% of the time, Pallas kernels for 34%

profile of v6, /device:TPU:9, one launch (start us, length us, event | category | flops | bytes accessed | tf_op | source)
XLA Modules:
  0.0 198.1 jit_solution(3268659656144483353)
XLA Ops:
  7.2 0.0 copy-start.7
  7.2 0.0 copy-start.8
  7.2 0.0 copy-start.9
  7.2 0.0 copy-start.10
  7.2 0.0 all-gather.6.cloned.1.call-start
  7.3 2.2 %normed.3 = bf16[2,128,1536]{2,1,0:T(8,128)(2,1)} custom-call(bf16[128,1536]{1,0:T(8,128)(2,1)} %x_ref.3, f32[1536]{0:T(1024)} %gain_ref.3, bf16[128,1536]{1,0:T(8,128)(2,1)} %refs_0_.1), custom_call_target="tpu_custom_call" | custom-call | flops 1000 | bytes 1000 | tf_op jit(solution)/shard_map/normed/pallas_call | solution.py:46
  9.5 0.0 all-gather.6.cloned.1.call-update
  9.5 0.0 all-gather.4.cloned.1.call-start
  9.5 1.9 normed.2
  11.5 0.0 all-gather.4.cloned.1.call-update
  11.5 0.0 copy-done.7
  11.5 0.0 copy-done.8
  11.5 0.0 copy-done.9
  11.5 0.0 copy-done.10
  11.6 0.6 maximum_bitcast_fusion
  12.2 5.6 %all-to-all-start = ((f32[8,2,2,128]{3,2,1,0:T(2,128)}), f32[8,2,2,128]{3,2,1,0:T(2,128)S(1)}, u32[]{:S(2)}, u32[]{:S(2)}) async-start(f32[8,2,2,128]{3,2,1,0:T(2,128)} %maximum_bitcast_fusion), calls=%async_computation | async-start | bytes 32768 | tf_op jit(solution)/shard_map/all_to_all | solution.py:523
  17.8 0.1 fusion.7
  17.9 0.1 fusion.8
  18.0 0.1 pad_add_fusion.1.sides_ref
  18.1 3.6 %all-to-all-done = f32[8,2,2,128]{3,2,1,0:T(2,128)S(1)} async-done(((f32[8,2,2,128]{3,2,1,0:T(2,128)}), f32[8,2,2,128]{3,2,1,0:T(2,128)S(1)}, u32[]{:S(2)}, u32[]{:S(2)}) %all-to-all-start) | async-done | bytes 16416 | tf_op jit(solution)/shard_map/all_to_all | solution.py:523
  21.7 0.6 slice_bitcast_fusion
  22.3 0.6 gather_fusion
  22.9 0.5 gather_fusion.1
  23.5 50.9 %all-gather.6.cloned.1.call-done = bf16[16,128,1536]{2,1,0:T(8,128)(2,1)} async-done(((bf16[2,128,1536]{2,1,0:T(8,128)(2,1)}), bf16[16,128,1536]{2,1,0:T(8,128)(2,1)}) %all-gather.6.cloned.1.call-update) | async-done | bytes 6291472 | tf_op jit(solution)/shard_map/all_gather | solution.py:528
  74.4 0.0 copy-start
  74.4 7.2 %place_rows.1 = (bf16[512,1536]{1,0:T(8,128)(2,1)}, bf16[512,1536]{1,0:T(8,128)(2,1)}, bf16[2,144,1536]{2,1,0:T(8,128)(2,1)}, bf16[2,112,1536]{2,1,0:T(8,128)(2,1)}, bf16[2,256,1536]{2,1,0:T(8,128)(2,1)}) custom-call(s32[2]{0:T(128)S(1)} %pad_add_fusion.1.sides_ref, bf16[4,2,2,128,1536]{4,3,2,1,0:T(8,128)(2,1)} %bitcast.46, ...), custom_call_target="tpu_custom_call" | custom-call | flops 1000 | bytes 1000 | tf_op jit(solution)/shard_map/place_rows/pallas_call | solution.py:141
  81.6 2.2 %collective-permute-start = (bf16[2,144,1536]{2,1,0:T(8,128)(2,1)}, bf16[2,144,1536]{2,1,0:T(8,128)(2,1)S(1)}, u32[]{:S(2)}, u32[]{:S(2)}) collective-permute-start(bf16[2,144,1536]{2,1,0:T(8,128)(2,1)} %get-tuple-element.27.give_1_ref), channel_id=1, source_target_pairs={{0,24},{8,16},{16,8},{24,0},{1,25},{9,17},{17,9},{25,1},{2,26},{10... | collective-permute-start | bytes 2654216 | tf_op jit(solution)/shard_map/ppermute | solution.py:535
  83.8 0.1 pad_add_fusion.which_ref
  83.9 0.0 copy-start.1
  83.9 0.0 copy-done
  83.9 20.2 %backward_rows.1 = (bf16[4,128,1536]{2,1,0:T(8,128)(2,1)}, bf16[4,64,1536]{2,1,0:T(8,128)(2,1)}, bf16[4,64,1536]{2,1,0:T(8,128)(2,1)}, bf16[512,768]{1,0:T(8,128)(2,1)}, bf16[512,1536]{1,0:T(8,128)(2,1)}) custom-call(s32[2]{0:T(128)S(1)} %pad_add_fusion.which_ref, f32[16,128]{1,0:T(8,128)S(1)} %bitcast.41, ...), custom_call_target="tpu_custom_call" | custom-call | flops 1000 | bytes 1000 | tf_op jit(solution)/shard_map/backward_rows/pallas_call | solution.py:305
  104.1 0.0 copy-done.1
  104.1 0.6 collective-permute-start.3
  104.7 0.0 collective-permute-done.refs_4_
  104.7 0.0 copy-start.3
  104.7 0.1 collective-permute-start.1
  104.9 2.0 %collective-permute-done.3 = bf16[4,64,1536]{2,1,0:T(8,128)(2,1)S(1)} collective-permute-done((bf16[4,64,1536]{2,1,0:T(8,128)(2,1)}, bf16[4,64,1536]{2,1,0:T(8,128)(2,1)S(1)}, u32[]{:S(2)}, u32[]{:S(2)}) %collective-permute-start.3) | collective-permute-done | bytes 786464 | tf_op jit(solution)/shard_map/ppermute | solution.py:486
  106.8 1.1 collective-permute-done.1
  108.0 2.9 %add_convert_fusion = (bf16[4,64,1536]{2,1,0:T(8,128)(2,1)}, bf16[4,64,1536]{2,1,0:T(8,128)(2,1)}) fusion(bf16[4,64,1536]{2,1,0:T(8,128)(2,1)S(1)} %collective-permute-done.3, bf16[4,128,1536]{2,1,0:T(8,128)(2,1)} %get-tuple-element.30, bf16[4,64,1536]{2,1,0:T(8,128)(2,1)S(1)} %collective-permute-done.1), kind=kLoop, calls=%fused_computation.3 | loop fusion | flops 3145728 | bytes 4718592 | tf_op jit(solution)/shard_map/convert_element_type | solution.py:544
  110.9 0.0 copy-done.3
  110.9 6.1 %all-to-all-start.1 = ((bf16[4,64,1536]{2,1,0:T(8,128)(2,1)}), bf16[4,64,1536]{2,1,0:T(8,128)(2,1)S(1)}, u32[]{:S(2)}, u32[]{:S(2)}) async-start(bf16[4,64,1536]{2,1,0:T(8,128)(2,1)} %get-tuple-element.47), calls=%async_computation.1 | async-start | bytes 1572864 | tf_op jit(solution)/shard_map/all_to_all | solution.py:492
  117.0 0.0 reduce-scatter.2.cloned.1.call-start
  117.0 0.0 copy-done.4
  117.0 1.1 collective-permute-start.2
  118.1 14.6 %forward_rows.1 = bf16[8,128,1536]{2,1,0:T(8,128)(2,1)} custom-call(f32[16,128]{1,0:T(8,128)} %bitcast.49, bf16[8,128,1536]{2,1,0:T(8,128)(2,1)} %all-gather.4.cloned.1.call-done.tokens_ref, bf16[2,1536,1536]{2,1,0:T(8,128)(2,1)} %bitcast.36, bf16[2,768,1536]{2,1,0:T(8,128)(2,1)} %bitcast.43), custom_call_target="tpu_custom_call" | custom-call | flops 1000 | bytes 1000 | tf_op jit(solution)/shard_map/forward_rows/pallas_call | solution.py:388
  132.7 1.6 collective-permute-done.2.refs_5_
  134.3 0.0 all-to-all-done.1
  134.3 0.0 reduce-scatter.2.cloned.1.call-update
  134.3 0.9 copy-done.5
  135.2 5.4 %all-to-all-start.2 = ((bf16[4,64,1536]{2,1,0:T(8,128)(2,1)}), bf16[4,64,1536]{2,1,0:T(8,128)(2,1)S(1)}, u32[]{:S(2)}, u32[]{:S(2)}) async-start(bf16[4,64,1536]{2,1,0:T(8,128)(2,1)} %get-tuple-element.46), calls=%async_computation.3 | async-start | bytes 1572864 | tf_op jit(solution)/shard_map/all_to_all | solution.py:492
  140.5 1.0 collective-permute-start.4
  141.6 0.0 copy-done.2
  141.6 0.2 fusion.6
  141.8 13.3 %weight_gradients.2 = (bf16[1536,1536]{1,0:T(8,128)(2,1)}, bf16[768,1536]{1,0:T(8,128)(2,1)}) custom-call(s32[2]{0:T(128)} %copy-done.1, bf16[512,1536]{1,0:T(8,128)(2,1)} %get-tuple-element.25.keep_c_ref.refs_0_, bf16[512,1536]{1,0:T(8,128)(2,1)} %get-tuple-element.26.keep_h_ref.refs_1_, bf16[512,768]{1,0:T(8,128)(2,1)} %get-tuple-element.37.refs_2_, ...), custom_call_target="tpu_custom_call" | custom-call | flops 1000 | bytes 1000 | tf_op jit(solution)/shard_map/weight_gradients/pallas_call | solution.py:463
  155.1 0.0 copy-start.6
  155.1 0.1 convert_reduce_fusion.1
  155.2 12.9 %all-to-all-done.2 = bf16[4,64,1536]{2,1,0:T(8,128)(2,1)S(1)} async-done(((bf16[4,64,1536]{2,1,0:T(8,128)(2,1)}), bf16[4,64,1536]{2,1,0:T(8,128)(2,1)S(1)}, u32[]{:S(2)}, u32[]{:S(2)}) %all-to-all-start.2) | async-done | bytes 786464 | tf_op jit(solution)/shard_map/all_to_all | solution.py:492
  168.1 0.1 convert_reduce_fusion
  168.3 0.0 copy-done.6
  168.3 0.3 fusion.2
  168.5 1.0 fusion.5
  169.6 6.6 %collective-permute-done.4.refs_2_ = bf16[2,256,1536]{2,1,0:T(8,128)(2,1)} collective-permute-done((bf16[2,256,1536]{2,1,0:T(8,128)(2,1)}, bf16[2,256,1536]{2,1,0:T(8,128)(2,1)}, u32[]{:S(2)}, u32[]{:S(2)}) %collective-permute-start.4) | collective-permute-done | bytes 1572896 | tf_op jit(solution)/shard_map/ppermute | solution.py:535
  176.2 9.8 %weight_gradients.3 = (bf16[1536,1536]{1,0:T(8,128)(2,1)}, bf16[768,1536]{1,0:T(8,128)(2,1)}) custom-call(s32[2]{0:T(128)} %copy-done.1, bf16[1536,1536]{1,0:T(8,128)(2,1)} %get-tuple-element.41.refs_0_, bf16[768,1536]{1,0:T(8,128)(2,1)} %get-tuple-element.42.refs_1_, bf16[2,256,1536]{2,1,0:T(8,128)(2,1)} %collective-permute-done.4.refs_2_, ...), custom_call_target="tpu_custom_call" | custom-call | flops 1000 | bytes 1000 | tf_op jit(solution)/shard_map/weight_gradients/pallas_call | solution.py:463
  186.0 5.5 %reduce-scatter.2.cloned.1.call-done = bf16[128,1536]{1,0:T(8,128)(2,1)} async-done(((bf16[1024,1536]{1,0:T(8,128)(2,1)}), bf16[128,1536]{1,0:T(8,128)(2,1)}) %reduce-scatter.2.cloned.1.call-update) | async-done | bytes 393232 | tf_op jit(solution)/shard_map/reduce_scatter | solution.py:548
  (13 shorter events, 0.1 us)
Async XLA Ops:
  7.2 4.3 %copy-start.7 = (f32[128,6]{0,1:T(8,128)S(1)}, f32[128,6]{0,1:T(8,128)}, u32[]{:S(2)}) copy-start(f32[128,6]{0,1:T(8,128)} %param.14) | copy-start | bytes 9220
  7.2 4.3 %copy-start.8 = (s32[128,6]{0,1:T(8,128)S(1)}, s32[128,6]{0,1:T(8,128)}, u32[]{:S(2)}) copy-start(s32[128,6]{0,1:T(8,128)} %param.15) | copy-start | bytes 9220
  7.2 4.4 %copy-start.9 = (f32[128,6]{0,1:T(8,128)S(1)}, f32[128,6]{0,1:T(8,128)}, u32[]{:S(2)}) copy-start(f32[128,6]{0,1:T(8,128)} %param.11) | copy-start | bytes 9220
  7.2 4.4 %copy-start.10 = (s32[128,6]{0,1:T(8,128)S(1)}, s32[128,6]{0,1:T(8,128)}, u32[]{:S(2)}) copy-start(s32[128,6]{0,1:T(8,128)} %param.12) | copy-start | bytes 9220
  7.2 67.2 %all-gather.6.cloned.1.call-start = ((), (), s32[]{:S(2)}) async-start(), calls=%async_computation.6 | async-start | bytes 7077888 | tf_op jit(solution)/shard_map/all_gather | solution.py:528
  9.5 108.6 %all-gather.4.cloned.1.call-start = ((), (), s32[]{:S(2)}) async-start(), calls=%async_computation.4 | async-start | bytes 3538944 | tf_op jit(solution)/shard_map/all_gather | solution.py:531
  12.2 9.5 %all-to-all-start = ((f32[8,2,2,128]{3,2,1,0:T(2,128)}), f32[8,2,2,128]{3,2,1,0:T(2,128)S(1)}, u32[]{:S(2)}, u32[]{:S(2)}) async-start(f32[8,2,2,128]{3,2,1,0:T(2,128)} %maximum_bitcast_fusion), calls=%async_computation | async-start | bytes 32768 | tf_op jit(solution)/shard_map/all_to_all | solution.py:523
  74.4 9.5 %copy-start = (bf16[1,2,1536,1536]{3,2,1,0:T(8,128)(2,1)S(1)}, bf16[1,2,1536,1536]{3,2,1,0:T(8,128)(2,1)}, u32[]{:S(2)}) copy-start(bf16[1,2,1536,1536]{3,2,1,0:T(8,128)(2,1)} %param.18) | copy-start | bytes 28311556
  81.6 23.1 %collective-permute-start = (bf16[2,144,1536]{2,1,0:T(8,128)(2,1)}, bf16[2,144,1536]{2,1,0:T(8,128)(2,1)S(1)}, u32[]{:S(2)}, u32[]{:S(2)}) collective-permute-start(bf16[2,144,1536]{2,1,0:T(8,128)(2,1)} %get-tuple-element.27.give_1_ref), channel_id=1, source_target_pairs={{0,24},{8,16},{16,8},{24,0},{1,25},{9,17},{17,9},{25,1},{2,26},{10... | collective-permute-start | bytes 2654216 | tf_op jit(solution)/shard_map/ppermute | solution.py:535
  83.9 20.2 %copy-start.1 = (s32[2]{0:T(128)}, s32[2]{0:T(128)S(1)}, u32[]{:S(2)}) copy-start(s32[2]{0:T(128)S(1)} %pad_add_fusion.which_ref) | copy-start | bytes 28
  104.1 2.7 %collective-permute-start.3 = (bf16[4,64,1536]{2,1,0:T(8,128)(2,1)}, bf16[4,64,1536]{2,1,0:T(8,128)(2,1)S(1)}, u32[]{:S(2)}, u32[]{:S(2)}) collective-permute-start(bf16[4,64,1536]{2,1,0:T(8,128)(2,1)} %get-tuple-element.35), channel_id=1, source_target_pairs={{0,1},{1,0},{2,3},{3,2},{4,5},{5,4},{6,7},{7,6},{8,9},{9,8},{10,11... | collective-permute-start | bytes 2359304 | tf_op jit(solution)/shard_map/ppermute | solution.py:486
  104.7 6.2 %copy-start.3 = (bf16[2,144,1536]{2,1,0:T(8,128)(2,1)}, bf16[2,144,1536]{2,1,0:T(8,128)(2,1)S(1)}, u32[]{:S(2)}) copy-start(bf16[2,144,1536]{2,1,0:T(8,128)(2,1)S(1)} %collective-permute-done.refs_4_) | copy-start | bytes 2654212
  104.7 3.3 %collective-permute-start.1 = (bf16[4,64,1536]{2,1,0:T(8,128)(2,1)}, bf16[4,64,1536]{2,1,0:T(8,128)(2,1)S(1)}, u32[]{:S(2)}, u32[]{:S(2)}) collective-permute-start(bf16[4,64,1536]{2,1,0:T(8,128)(2,1)} %get-tuple-element.32), channel_id=1, source_target_pairs={{0,1},{1,0},{2,3},{3,2},{4,5},{5,4},{6,7},{7,6},{8,9},{9,8},{10,11... | collective-permute-start | bytes 2359304 | tf_op jit(solution)/shard_map/ppermute | solution.py:486
  110.9 6.1 %copy-start.4 = (bf16[2,112,1536]{2,1,0:T(8,128)(2,1)S(1)}, bf16[2,112,1536]{2,1,0:T(8,128)(2,1)}, u32[]{:S(2)}) copy-start(bf16[2,112,1536]{2,1,0:T(8,128)(2,1)} %get-tuple-element.28.give_2_ref) | copy-start | bytes 2064388
  110.9 23.4 %all-to-all-start.1 = ((bf16[4,64,1536]{2,1,0:T(8,128)(2,1)}), bf16[4,64,1536]{2,1,0:T(8,128)(2,1)S(1)}, u32[]{:S(2)}, u32[]{:S(2)}) async-start(bf16[4,64,1536]{2,1,0:T(8,128)(2,1)} %get-tuple-element.47), calls=%async_computation.1 | async-start | bytes 1572864 | tf_op jit(solution)/shard_map/all_to_all | solution.py:492
  117.0 74.5 %reduce-scatter.2.cloned.1.call-start = ((), (), s32[]{:S(2)}) async-start(), calls=%async_computation.5 | async-start | bytes 3538944 | tf_op jit(solution)/shard_map/reduce_scatter | solution.py:548
  117.0 17.2 %collective-permute-start.2 = (bf16[2,112,1536]{2,1,0:T(8,128)(2,1)S(1)}, bf16[2,112,1536]{2,1,0:T(8,128)(2,1)S(1)}, u32[]{:S(2)}, u32[]{:S(2)}) collective-permute-start(bf16[2,112,1536]{2,1,0:T(8,128)(2,1)S(1)} %copy-done.4), channel_id=1, source_target_pairs={{0,24},{8,16},{16,8},{24,0},{1,25},{9,17},{17,9},{25,1},{2,26},{10... | collective-permute-start | bytes 2064392 | tf_op jit(solution)/shard_map/ppermute | solution.py:535
  134.3 0.9 copy-start.5
  135.2 6.4 %copy-start.2 = (bf16[128,1536]{1,0:T(8,128)(2,1)S(1)}, bf16[128,1536]{1,0:T(8,128)(2,1)}, u32[]{:S(2)}) copy-start(bf16[128,1536]{1,0:T(8,128)(2,1)} %x_ref.3) | copy-start | bytes 1179652
  135.2 33.0 %all-to-all-start.2 = ((bf16[4,64,1536]{2,1,0:T(8,128)(2,1)}), bf16[4,64,1536]{2,1,0:T(8,128)(2,1)S(1)}, u32[]{:S(2)}, u32[]{:S(2)}) async-start(bf16[4,64,1536]{2,1,0:T(8,128)(2,1)} %get-tuple-element.46), calls=%async_computation.3 | async-start | bytes 1572864 | tf_op jit(solution)/shard_map/all_to_all | solution.py:492
  140.5 35.6 %collective-permute-start.4 = (bf16[2,256,1536]{2,1,0:T(8,128)(2,1)}, bf16[2,256,1536]{2,1,0:T(8,128)(2,1)}, u32[]{:S(2)}, u32[]{:S(2)}) collective-permute-start(bf16[2,256,1536]{2,1,0:T(8,128)(2,1)} %get-tuple-element.29.give_3_ref), channel_id=1, source_target_pairs={{0,24},{8,16},{16,8},{24,0},{1,25},{9,17},{17,9},{25,1},{2,26},{10... | collective-permute-start | bytes 4718600 | tf_op jit(solution)/shard_map/ppermute | solution.py:535
  155.1 13.2 %copy-start.6 = (f32[1536]{0:T(1024)S(1)}, f32[1536]{0:T(1024)}, u32[]{:S(2)}) copy-start(f32[1536]{0:T(1024)} %gain_ref.3) | copy-start | bytes 18436
Sparse Core Ops, SparseCore 0:
  10.3 64.1 all-gather.5
  76.6 38.1 all-gather.3
  134.4 57.0 reduce-scatter.1
